TPU v7x, 32 devices: a whole 2x2x4 slice. The times are simulated.
32 devices in a mesh: row: 16 (over z, y, core), hid: 2 (over x).
Axes of the slice: x: 2, y: 2, z: 4, core: 2. Of those that a mesh axis runs over, the one named last changes fastest.
Arguments:
- features: bfloat16 [64, 256, 512], P('row'), may hold values from -6 to 6
- dw_weight: float32 [2, 7, 7, 512], replicated, may hold values from -0.875 to 0.875
- dw_bias: float32 [2, 512], replicated, may hold values from -3 to 3
- ln_gain: float32 [2, 512], replicated, may hold values from 0.1 to 1.9
- ln_bias: float32 [2, 512], replicated, may hold values from -3 to 3
- w_up: bfloat16 [2, 512, 2048], P(None, None, 'hid'), may hold values from -0.25 to 0.25
- b_up: float32 [2, 2048], P(None, 'hid'), may hold values from -3 to 3
- w_down: bfloat16 [2, 2048, 512], P(None, 'hid'), may hold values from -0.125 to 0.125
- b_down: float32 [2, 512], replicated, may hold values from -3 to 3
- layer_scale: float32 [2, 512], replicated, may hold values from 0.2 to 1
Outputs:
- result_map: bfloat16 [64, 256, 512], P('row')
All inputs are finite; a program needn't handle non-finite values.
Results may differ from a plain program's by a relative error of at most 0.018.
Values may be sent and summed in bfloat16 or wider, within the bound.
No kernel may reach another device: no remote copies, remote signals or barrier semaphores. Data moves between devices by JAX's collectives and lax.ppermute only.
A program may use at most 64 MiB of HBM per device.

v0:
```python
import jax
import jax.numpy as jnp
from jax import lax
from jax.sharding import PartitionSpec as P


def extended(block, sides, width):
    for axis, dim in sides:
        count = lax.axis_size(axis)
        forward = [(i, i + 1) for i in range(count - 1)]
        backward = [(target, source) for source, target in forward]
        low = lax.ppermute(
            lax.slice_in_dim(block, block.shape[dim] - width, None, axis=dim), axis, forward
        )
        high = lax.ppermute(lax.slice_in_dim(block, 0, width, axis=dim), axis, backward)
        block = jnp.concatenate([low, block, high], axis=dim)
    return block


def depthwise(padded, kernel, bias):
    pad = kernel.shape[0] // 2
    rows = padded.shape[0] - 2 * pad
    width = padded.shape[1]
    wide = jnp.pad(padded, ((0, 0), (pad, pad), (0, 0)))
    total = jnp.zeros((rows, width, padded.shape[2]), jnp.float32)
    for i in range(kernel.shape[0]):
        for j in range(kernel.shape[1]):
            total = total + wide[i : i + rows, j : j + width, :].astype(jnp.float32) * kernel[i, j]
    return (total + bias).astype(jnp.bfloat16)


def expand(conv, gain, shift, w_first, b_first):
    values = conv.reshape(-1, conv.shape[2]).astype(jnp.float32)
    mean = jnp.mean(values, axis=1, keepdims=True)
    var = jnp.mean((values - mean) ** 2, axis=1, keepdims=True)
    normed = ((values - mean) / jnp.sqrt(var + 1e-06) * gain + shift).astype(jnp.bfloat16)
    return jax.nn.gelu(
        jnp.dot(normed, w_first, preferred_element_type=jnp.float32) + b_first, approximate=False
    ).astype(jnp.bfloat16)


def pointwise(conv, gain, shift, w_first, b_first, w_second):
    hidden = expand(conv, gain, shift, w_first, b_first)
    partial_sum = jnp.dot(hidden, w_second, preferred_element_type=jnp.float32)
    return partial_sum.reshape(conv.shape[0], conv.shape[1], -1)


def shards(features, dw_weight, dw_bias, ln_gain, ln_bias, w_up, b_up, w_down, b_down, layer_scale):
    reach = dw_weight.shape[1] // 2
    state = features
    for b in range(dw_weight.shape[0]):
        padded = extended(state, (("row", 0),), reach)
        conv = depthwise(padded, dw_weight[b], dw_bias[b])
        partial_sum = pointwise(conv, ln_gain[b], ln_bias[b], w_up[b], b_up[b], w_down[b])
        summed = lax.psum(partial_sum.astype(jnp.bfloat16), "hid").astype(jnp.float32)
        state = (state.astype(jnp.float32) + layer_scale[b] * (summed + b_down[b])).astype(
            jnp.bfloat16
        )
    return state


def solution(mesh):
    return jax.shard_map(
        shards,
        mesh=mesh,
        in_specs=(
            P("row", None, None),
            P(),
            P(),
            P(),
            P(),
            P(None, None, "hid"),
            P(None, "hid"),
            P(None, "hid", None),
            P(),
            P(),
        ),
        out_specs=P("row", None, None),
        check_vma=False,
    )
```

profile of v0, /device:TPU:12, one launch (start us, length us, event | category | flops | bytes accessed | tf_op | source)
XLA Modules:
  0.0 205.1 jit_solution(16031831734847137141)
XLA Ops:
  6.6 1.6 fusion.99
  8.3 2.1 %collective-permute-start = (bf16[3,256,512]{2,1,0:T(8,128)(2,1)S(1)}, bf16[3,256,512]{2,1,0:T(8,128)(2,1)S(1)}, u32[]{:S(2)}, u32[]{:S(2)}) collective-permute-start(bf16[3,256,512]{2,1,0:T(8,128)(2,1)S(1)} %get-tuple-element.13), channel_id=1, source_target_pairs={{0,2},{2,4},{4,6},{6,8},{8,10},{10,12},{12,14},{14,16},{16,18},{18... | collective-permute-start | bytes 2359304 | tf_op jit(solution)/shard_map/ppermute | solution.py:12
  10.3 3.6 %collective-permute-start.1 = (bf16[3,256,512]{2,1,0:T(8,128)(2,1)S(1)}, bf16[3,256,512]{2,1,0:T(8,128)(2,1)S(1)}, u32[]{:S(2)}, u32[]{:S(2)}) collective-permute-start(bf16[3,256,512]{2,1,0:T(8,128)(2,1)S(1)} %get-tuple-element.14), channel_id=1, source_target_pairs={{2,0},{4,2},{6,4},{8,6},{10,8},{12,10},{14,12},{16,14},{18,16},{20... | collective-permute-start | bytes 2359304 | tf_op jit(solution)/shard_map/ppermute | solution.py:15
  14.4 15.7 %collective-permute-done = bf16[3,256,512]{2,1,0:T(8,128)(2,1)S(1)} collective-permute-done((bf16[3,256,512]{2,1,0:T(8,128)(2,1)S(1)}, bf16[3,256,512]{2,1,0:T(8,128)(2,1)S(1)}, u32[]{:S(2)}, u32[]{:S(2)}) %collective-permute-start) | collective-permute-done | bytes 786464 | tf_op jit(solution)/shard_map/ppermute | solution.py:12
  30.4 0.9 select_maximum_fusion.2
  31.3 16.1 %convert_reduce_fusion.1 = (f32[4,256]{1,0:T(4,128)S(1)}, bf16[4,256,512]{2,1,0:T(8,128)(2,1)S(1)}) fusion(f32[512]{0:T(512)S(1)} %bitcast.239, f32[512]{0:T(512)S(1)} %bitcast.169, bf16[10,262,512]{2,1,0:T(8,128)(2,1)S(1)} %select_maximum_fusion.2, f32[512]{0:T(512)S(1)} %bitcast.170, f32[512]{0:T(512)S(1)} %bitcast.171, f32[512]{0:T(512)S(1)} %bitcast.172, ...), kind=kLoop, calls=%fused_computation.51 | loop fusion | flops 78642176 | bytes 52535296 | tf_op jit(solution)/shard_map/reduce_sum | solution.py:34
  47.4 0.5 fusion.30
  48.4 0.6 copy-done.8
  49.0 9.9 %fusion.3 = bf16[1024,1024]{1,0:T(8,128)(2,1)S(1)} fusion(bf16[1024,512]{1,0:T(8,128)(2,1)S(1)} %bitcast.137, f32[1024]{0:T(1024)S(1)} %bitcast.247, bf16[2,512,1024]{2,1,0:T(8,128)(2,1)S(1)} %copy-done.8), kind=kOutput, calls=%fused_computation.7 | convolution fusion | flops 1142947840 | bytes 4198400 | tf_op jit(solution)/shard_map/dot_general | solution.py:38
  59.0 2.2 %convolution_convert_fusion.1 = bf16[4,256,512]{2,1,0:T(8,128)(2,1)} fusion(bf16[4,256,1024]{2,1,0:T(8,128)(2,1)S(1)} %bitcast.248, bf16[2,1024,512]{2,1,0:T(8,128)(2,1)S(1)} %copy-done.10), kind=kOutput, calls=%fused_computation.129 | convolution fusion | flops 1074266112 | bytes 4194304 | tf_op jit(solution)/shard_map/dot_general | solution.py:44
  61.3 40.3 %all-reduce.5.cloned.1.call-done = bf16[4,256,512]{2,1,0:T(8,128)(2,1)} async-done(((bf16[4,256,512]{2,1,0:T(8,128)(2,1)}), bf16[4,256,512]{2,1,0:T(8,128)(2,1)}) %all-reduce.5.cloned.1.call-update) | async-done | bytes 1048592 | tf_op jit(solution)/shard_map/psum | solution.py:55
  101.7 1.6 fusion.59
  103.4 1.9 collective-permute-start.2
  105.3 3.8 %collective-permute-start.3 = (bf16[3,256,512]{2,1,0:T(8,128)(2,1)S(1)}, bf16[3,256,512]{2,1,0:T(8,128)(2,1)S(1)}, u32[]{:S(2)}, u32[]{:S(2)}) collective-permute-start(bf16[3,256,512]{2,1,0:T(8,128)(2,1)S(1)} %get-tuple-element.10), channel_id=1, source_target_pairs={{2,0},{4,2},{6,4},{8,6},{10,8},{12,10},{14,12},{16,14},{18,16},{20... | collective-permute-start | bytes 2359304 | tf_op jit(solution)/shard_map/ppermute | solution.py:15
  109.3 15.9 %collective-permute-done.2 = bf16[3,256,512]{2,1,0:T(8,128)(2,1)S(1)} collective-permute-done((bf16[3,256,512]{2,1,0:T(8,128)(2,1)S(1)}, bf16[3,256,512]{2,1,0:T(8,128)(2,1)S(1)}, u32[]{:S(2)}, u32[]{:S(2)}) %collective-permute-start.2) | collective-permute-done | bytes 786464 | tf_op jit(solution)/shard_map/ppermute | solution.py:12
  125.1 0.8 select_maximum_fusion
  126.0 16.3 %convert_reduce_fusion = (f32[4,256]{1,0:T(4,128)S(1)}, bf16[4,256,512]{2,1,0:T(8,128)(2,1)S(1)}) fusion(f32[512]{0:T(512)S(1)} %bitcast.236, f32[512]{0:T(512)S(1)} %bitcast.199, bf16[10,262,512]{2,1,0:T(8,128)(2,1)S(1)} %select_maximum_fusion, f32[512]{0:T(512)S(1)} %bitcast.200, f32[512]{0:T(512)S(1)} %bitcast.201, f32[512]{0:T(512)S(1)} %bitcast.202, ...), kind=kLoop, calls=%fused_computation.47 | loop fusion | flops 81787904 | bytes 47816704 | tf_op jit(solution)/shard_map/reduce_sum | solution.py:34
  142.3 0.5 fusion.26
  142.8 0.5 fusion.29
  143.3 0.6 copy-done.9
  143.9 9.9 %fusion.6 = bf16[1024,1024]{1,0:T(8,128)(2,1)S(1)} fusion(bf16[1024,512]{1,0:T(8,128)(2,1)S(1)} %bitcast.136, f32[1024]{0:T(1024)S(1)} %bitcast.246, bf16[2,512,1024]{2,1,0:T(8,128)(2,1)S(1)} %copy-done.9), kind=kOutput, calls=%fused_computation.10 | convolution fusion | flops 1142947840 | bytes 4198400 | tf_op jit(solution)/shard_map/dot_general | solution.py:38
  153.8 2.2 %convolution_convert_fusion = bf16[4,256,512]{2,1,0:T(8,128)(2,1)} fusion(bf16[4,256,1024]{2,1,0:T(8,128)(2,1)S(1)} %bitcast.249, bf16[2,1024,512]{2,1,0:T(8,128)(2,1)S(1)} %copy-done.11), kind=kOutput, calls=%fused_computation.128 | convolution fusion | flops 1074266112 | bytes 4194304 | tf_op jit(solution)/shard_map/dot_general | solution.py:44
  156.1 39.7 %all-reduce.7.cloned.1.call-done = bf16[4,256,512]{2,1,0:T(8,128)(2,1)} async-done(((bf16[4,256,512]{2,1,0:T(8,128)(2,1)}), bf16[4,256,512]{2,1,0:T(8,128)(2,1)}) %all-reduce.7.cloned.1.call-update) | async-done | bytes 1048592 | tf_op jit(solution)/shard_map/psum | solution.py:55
  195.7 2.6 %fusion.85 = bf16[4,256,512]{2,1,0:T(8,128)(2,1)} fusion(bf16[4,256,512]{2,1,0:T(8,128)(2,1)S(1)} %fusion.59, bf16[4,256,512]{2,1,0:T(8,128)(2,1)} %all-reduce.7.cloned.1.call-done, f32[512]{0:T(512)S(1)} %bitcast.238, f32[512]{0:T(512)S(1)} %bitcast.237), kind=kLoop, calls=%fused_computation.121 | loop fusion | flops 3145728 | bytes 3149824 | tf_op jit(solution)/shard_map/convert_element_type | solution.py:56
  (51 shorter events, 1.5 us)
Async XLA Ops:
  6.5 7.4 %copy-start.1 = (f32[2,7,7,512]{3,0,2,1:T(2,128)S(1)}, f32[2,7,7,512]{3,0,2,1:T(2,128)}, u32[]{:S(2)}) copy-start(f32[2,7,7,512]{3,0,2,1:T(2,128)} %param.11) | copy-start | bytes 602116
  6.5 7.7 %copy-start.3 = (f32[2,512]{1,0:T(2,128)S(1)}, f32[2,512]{1,0:T(2,128)}, u32[]{:S(2)}) copy-start(f32[2,512]{1,0:T(2,128)} %param.12) | copy-start | bytes 12292
  6.5 7.7 %copy-start.2 = (f32[2,1024]{1,0:T(2,128)S(1)}, f32[2,1024]{1,0:T(2,128)}, u32[]{:S(2)}) copy-start(f32[2,1024]{1,0:T(2,128)} %param.16) | copy-start | bytes 24580
  6.5 7.7 %copy-start.4 = (f32[2,512]{1,0:T(2,128)S(1)}, f32[2,512]{1,0:T(2,128)}, u32[]{:S(2)}) copy-start(f32[2,512]{1,0:T(2,128)} %param.13) | copy-start | bytes 12292
  6.5 7.7 %copy-start.5 = (f32[2,512]{1,0:T(2,128)S(1)}, f32[2,512]{1,0:T(2,128)}, u32[]{:S(2)}) copy-start(f32[2,512]{1,0:T(2,128)} %param.14) | copy-start | bytes 12292
  6.5 95.1 %all-reduce.5.cloned.1.call-start = ((), (), s32[]{:S(2)}) async-start(), calls=%async_computation | async-start | bytes 2097152 | tf_op jit(solution)/shard_map/psum | solution.py:55
  8.2 21.9 %copy-start = (bf16[4,256,512]{2,1,0:T(8,128)(2,1)S(1)}, bf16[4,256,512]{2,1,0:T(8,128)(2,1)}, u32[]{:S(2)}) copy-start(bf16[4,256,512]{2,1,0:T(8,128)(2,1)} %param.10) | copy-start | bytes 3145732
  8.3 21.9 %collective-permute-start = (bf16[3,256,512]{2,1,0:T(8,128)(2,1)S(1)}, bf16[3,256,512]{2,1,0:T(8,128)(2,1)S(1)}, u32[]{:S(2)}, u32[]{:S(2)}) collective-permute-start(bf16[3,256,512]{2,1,0:T(8,128)(2,1)S(1)} %get-tuple-element.13), channel_id=1, source_target_pairs={{0,2},{2,4},{4,6},{6,8},{8,10},{10,12},{12,14},{14,16},{16,18},{18... | collective-permute-start | bytes 2359304 | tf_op jit(solution)/shard_map/ppermute | solution.py:12
  10.3 20.1 %collective-permute-start.1 = (bf16[3,256,512]{2,1,0:T(8,128)(2,1)S(1)}, bf16[3,256,512]{2,1,0:T(8,128)(2,1)S(1)}, u32[]{:S(2)}, u32[]{:S(2)}) collective-permute-start(bf16[3,256,512]{2,1,0:T(8,128)(2,1)S(1)} %get-tuple-element.14), channel_id=1, source_target_pairs={{2,0},{4,2},{6,4},{8,6},{10,8},{12,10},{14,12},{16,14},{18,16},{20... | collective-permute-start | bytes 2359304 | tf_op jit(solution)/shard_map/ppermute | solution.py:15
  47.4 1.6 copy-start.8
  49.0 9.9 %copy-start.10 = (bf16[2,1024,512]{2,1,0:T(8,128)(2,1)S(1)}, bf16[2,1024,512]{2,1,0:T(8,128)(2,1)}, u32[]{:S(2)}) copy-start(bf16[2,1024,512]{2,1,0:T(8,128)(2,1)} %param.17) | copy-start | bytes 6291460
  59.0 2.3 %copy-start.6 = (f32[2,512]{1,0:T(2,128)S(1)}, f32[2,512]{1,0:T(2,128)}, u32[]{:S(2)}) copy-start(f32[2,512]{1,0:T(2,128)} %param.19) | copy-start | bytes 12292
  59.0 2.3 %copy-start.7 = (f32[2,512]{1,0:T(2,128)S(1)}, f32[2,512]{1,0:T(2,128)}, u32[]{:S(2)}) copy-start(f32[2,512]{1,0:T(2,128)} %param.18) | copy-start | bytes 12292
  61.2 134.5 %all-reduce.7.cloned.1.call-start = ((), (), s32[]{:S(2)}) async-start(), calls=%async_computation.1 | async-start | bytes 2097152 | tf_op jit(solution)/shard_map/psum | solution.py:55
  103.4 21.7 %collective-permute-start.2 = (bf16[3,256,512]{2,1,0:T(8,128)(2,1)S(1)}, bf16[3,256,512]{2,1,0:T(8,128)(2,1)S(1)}, u32[]{:S(2)}, u32[]{:S(2)}) collective-permute-start(bf16[3,256,512]{2,1,0:T(8,128)(2,1)S(1)} %get-tuple-element.9), channel_id=1, source_target_pairs={{0,2},{2,4},{4,6},{6,8},{8,10},{10,12},{12,14},{14,16},{16,18},{18... | collective-permute-start | bytes 2359304 | tf_op jit(solution)/shard_map/ppermute | solution.py:12
  105.3 19.8 %collective-permute-start.3 = (bf16[3,256,512]{2,1,0:T(8,128)(2,1)S(1)}, bf16[3,256,512]{2,1,0:T(8,128)(2,1)S(1)}, u32[]{:S(2)}, u32[]{:S(2)}) collective-permute-start(bf16[3,256,512]{2,1,0:T(8,128)(2,1)S(1)} %get-tuple-element.10), channel_id=1, source_target_pairs={{2,0},{4,2},{6,4},{8,6},{10,8},{12,10},{14,12},{16,14},{18,16},{20... | collective-permute-start | bytes 2359304 | tf_op jit(solution)/shard_map/ppermute | solution.py:15
  142.3 1.6 copy-start.9
  143.9 9.9 %copy-start.11 = (bf16[2,1024,512]{2,1,0:T(8,128)(2,1)S(1)}, bf16[2,1024,512]{2,1,0:T(8,128)(2,1)}, u32[]{:S(2)}) copy-start(bf16[2,1024,512]{2,1,0:T(8,128)(2,1)} %param.17) | copy-start | bytes 6291460
Sparse Core Ops, SparseCore 0:
  61.3 40.2 all-reduce.4
  156.2 39.4 all-reduce.6
where the time goes:
time: 207 us; the launch traced here: 205 us
  waiting for transfers between devices  112 us (54%)
  other arithmetic  40.2 us (19%)
  matrix products  24.3 us (12%)
  between operations  13.8 us (7%)
  starting transfers between devices  11.5 us (6%)
  local copies, waits for them, and re-layouts  3.63 us (2%)
    psum x2, waiting for transfers between devices, shards(): lax.psum(partial_sum.astype(jnp.bfloat16), 'hid').astype(jnp.float32)  80 us
    reduce_sum x2, other arithmetic, expand(): mean = jnp.mean(values, axis=1, keepdims=True)  32.3 us
    ppermute x2, waiting for transfers between devices, extended(): lax.ppermute(lax.slice_in_dim(block, block.shape[dim] - width, None, axis...  31.6 us
    dot_general x2, matrix products, expand(): jnp.dot(normed, w_first, preferred_element_type=jnp.float32) + b_first  19.9 us
    ppermute x2, starting transfers between devices, extended(): lax.ppermute(lax.slice_in_dim(block, 0, width, axis=dim), axis, backward)  7.46 us
    dot_general x2, matrix products, pointwise(): partial_sum = jnp.dot(hidden, w_second, preferred_element_type=jnp.float32)  4.44 us
    convert_element_type x2, other arithmetic, shards(): (state.astype(jnp.float32) + layer_scale[b] * (summed + b_down[b])).astyp...  4.17 us
  transfers between devices with their start and end apart: 6, of which 4 were waited for; matrix products, arithmetic and copies ran while one was open for 0% of the time, Pallas kernels for 0%

commit v1 on v0

v1 whole, which is shorter than its diff:
```python
import functools

import jax
import jax.numpy as jnp
from jax import lax
from jax.experimental import pallas as pl
from jax.experimental.pallas import tpu as pltpu
from jax.sharding import PartitionSpec as P

LANES = 128
MARGIN = 16
ERF = (
    0.7978842161099958,
    0.03633428353366734,
    -3.3130008237205104e-05,
    -5.524015421773868e-05,
    3.969108888631555e-06,
    -1.33446374821295e-07,
    1.8056156531812635e-09,
)
VMEM = pl.BlockSpec(memory_space=pltpu.VMEM)
SMEM = pl.BlockSpec(memory_space=pltpu.SMEM)
PARAMS = pltpu.CompilerParams(vmem_limit_bytes=48 * 1024 * 1024)


def gelu(u):
    v = u * u
    p = jnp.full_like(u, ERF[-1])
    for c in ERF[-2::-1]:
        p = p * v + c
    half = 0.5 * u
    return half * jnp.tanh(u * p) + half


def tile_of(width):
    return next(s for s in (48, 32, 16) if width % s == 0)


def own_kernel(b, place, own, taps, bias, out, wide):
    groups, rows, width, _ = out.shape
    size = taps.shape[1]
    reach = size // 2
    for k in range(width // MARGIN + 2):
        at = place[0] + (k - 1) * MARGIN
        inside = (at >= 0) & (at <= own.shape[1] - MARGIN)
        at = pl.multiple_of(jnp.clip(at, 0, own.shape[1] - MARGIN), MARGIN)
        for r in range(rows):
            for c in range(groups):
                x = own[r, pl.ds(at, MARGIN), c * LANES : (c + 1) * LANES].astype(jnp.float32)
                wide[c, r, k * MARGIN : (k + 1) * MARGIN] = jnp.where(inside, x, 0.0)
    step = tile_of(width)

    def group(c, _):
        lanes = pl.ds(pl.multiple_of(c * LANES, LANES), LANES)
        for start in range(0, width, step):
            sums = [jnp.broadcast_to(bias[b : b + 1, lanes], (step, LANES)) for _ in range(rows)]
            for i in range(rows):
                for j in range(size):
                    first = start + MARGIN + j - reach
                    x = wide[c, i, first : first + step]
                    for r in range(rows):
                        t = i - r + reach
                        if 0 <= t < size:
                            sums[r] = sums[r] + x * taps[b, t, j : j + 1, lanes]
            for r in range(rows):
                out[c, r, start : start + step] = sums[r]
        return 0

    lax.fori_loop(0, groups, group, 0)


def add_halo(b, place, near, far, before, taps, conv, wide):
    groups, rows, width, _ = conv.shape
    size = taps.shape[1]
    reach = size // 2
    wide[...] = jnp.zeros(wide.shape, jnp.float32)
    at = pl.ds(pl.multiple_of(place[1], MARGIN), near.shape[1])
    odd = place[2]
    for c in range(groups):
        for k in range(reach):
            lanes = slice(c * LANES, (c + 1) * LANES)
            wide[c, (1 - odd) * reach + k, at] = near[k, :, lanes].astype(jnp.float32)
            wide[c, odd * reach + k, at] = far[k, :, lanes].astype(jnp.float32)
    step = tile_of(width)

    def group(c, _):
        lanes = pl.ds(pl.multiple_of(c * LANES, LANES), LANES)
        for start in range(0, width, step):
            sums = [before[c, r, start : start + step] for r in range(rows)]
            for i in range(2 * reach):
                row = i - reach if i < reach else i - reach + rows
                for j in range(size):
                    first = start + MARGIN + j - reach
                    x = wide[c, i, first : first + step]
                    for r in range(rows):
                        t = row - r + reach
                        if 0 <= t < size:
                            sums[r] = sums[r] + x * taps[b, t, j : j + 1, lanes]
            for r in range(rows):
                conv[c, r, start : start + step] = sums[r]
        return 0

    lax.fori_loop(0, groups, group, 0)


def normalise(b, conv, gain, shift, out):
    groups, rows, width, _ = conv.shape
    channels = groups * LANES
    for r in range(rows):
        x = [conv[c, r].astype(jnp.bfloat16).astype(jnp.float32) for c in range(groups)]
        mean = jnp.sum(functools.reduce(jnp.add, x), axis=1, keepdims=True) * (1.0 / channels)
        x = [v - mean for v in x]
        var = jnp.sum(functools.reduce(jnp.add, [v * v for v in x]), axis=1, keepdims=True)
        scale = lax.rsqrt(var * (1.0 / channels) + 1e-06)
        for c in range(groups):
            lanes = slice(c * LANES, (c + 1) * LANES)
            y = x[c] * scale * gain[b : b + 1, lanes] + shift[b : b + 1, lanes]
            out[r * width : (r + 1) * width, lanes] = y.astype(out.dtype)


def project(x, up, b_up, down, total, before=None):
    hidden = down.shape[0]
    part = 256 if hidden % 256 == 0 else 128
    for k in range(0, hidden, part):
        u = jnp.dot(x[...], up[:, k : k + part], preferred_element_type=jnp.float32)
        h = gelu(u + b_up[:, k : k + part]).astype(jnp.bfloat16)
        y = jnp.dot(h, down[k : k + part, :], preferred_element_type=jnp.float32)
        if k:
            total[...] += y
        else:
            total[...] = y if before is None else before[...] + y


def rest_kernel(
    b, place, near, far, before, taps, gain, shift, up, b_up, down, normed, total, conv, wide
):
    add_halo(b, place, near, far, before, taps, conv, wide)
    normalise(b, conv, gain, shift, normed)
    project(normed, up.at[b], b_up.at[b : b + 1], down.at[b], total)


def more_kernel(b, kind, last, place, x, before, *refs):
    channels = x.shape[1]
    if kind == "plain":
        up, b_up, down, *refs = refs
        b_up = b_up[...]
    else:
        if kind == "halves":
            mine, other, down, *refs = refs
            up = refs.pop()
            half = channels // 2
            up[pl.ds(pl.multiple_of(place[3] * half, half), half), :] = mine[...]
            up[pl.ds(pl.multiple_of((1 - place[3]) * half, half), half), :] = other[...]
        else:
            packed, *refs = refs
            up, down = packed.at[:channels], packed.at[channels:]
        hidden = down.shape[0] - MARGIN
        terms = down[hidden:, :].astype(jnp.float32)
        b_up, down = terms[0:1] + terms[1:2], down.at[:hidden]
    if not last:
        project(x, up, b_up, down, refs[0], before)
        return
    state, b_down, scale, out, total = refs
    project(x, up, b_up, down, total, before)
    rows, width, _ = out.shape
    for r in range(rows):
        s = state[r, pl.ds(pl.multiple_of(place[0], MARGIN), width), :].astype(jnp.float32)
        y = total[r * width : (r + 1) * width, :] + b_down[b : b + 1]
        out[r] = (s + scale[b : b + 1] * y).astype(out.dtype)


def cost(flops, transcendentals=0):
    return pl.CostEstimate(flops=flops, bytes_accessed=flops // 512, transcendentals=transcendentals)


def conv_own(b, place, own, width, taps, bias):
    rows, _, channels = own.shape
    groups = channels // LANES
    return pl.pallas_call(
        functools.partial(own_kernel, b),
        out_shape=jax.ShapeDtypeStruct((groups, rows, width, LANES), jnp.float32),
        in_specs=[SMEM] + [VMEM] * 3,
        out_specs=VMEM,
        scratch_shapes=[pltpu.VMEM((groups, rows, width + 2 * MARGIN, LANES), jnp.float32)],
        compiler_params=PARAMS,
        cost_estimate=cost(56 * rows * rows * width * channels),
        name="conv_own",
    )(place, own, taps, bias)


def conv_rest(b, place, near, far, before, taps, gain, shift, up, b_up, down):
    groups, rows, width, _ = before.shape
    channels, reach = groups * LANES, near.shape[0]
    positions = rows * width
    return pl.pallas_call(
        functools.partial(rest_kernel, b),
        out_shape=(
            jax.ShapeDtypeStruct((positions, channels), jnp.bfloat16),
            jax.ShapeDtypeStruct((positions, channels), jnp.float32),
        ),
        in_specs=[SMEM] + [VMEM] * 9,
        out_specs=(VMEM, VMEM),
        scratch_shapes=[
            pltpu.VMEM((groups, rows, width, LANES), jnp.float32),
            pltpu.VMEM((groups, 2 * reach, width + 2 * MARGIN, LANES), jnp.float32),
        ],
        compiler_params=PARAMS,
        cost_estimate=cost(4 * positions * channels * up.shape[2], positions * up.shape[2]),
        name="conv_rest",
    )(place, near, far, before, taps, gain, shift, up, b_up, down)


def more(b, place, x, before, part, last=None, rows=0):
    positions, channels = x.shape
    args = [place, x, before] + list(part) + list(last or ())
    kind = ("packed", "halves", "plain")[0 if len(part) == 1 else 1 if part[0].dtype == part[1].dtype else 2]
    hidden = part[0].shape[1]
    scratch = []
    if last is None:
        shape = jax.ShapeDtypeStruct((positions, channels), jnp.float32)
    else:
        shape = jax.ShapeDtypeStruct((rows, positions // rows, channels), jnp.bfloat16)
        scratch.append(pltpu.VMEM((positions, channels), jnp.float32))
    if kind == "halves":
        scratch.append(pltpu.VMEM((channels, hidden), jnp.bfloat16))
    return pl.pallas_call(
        functools.partial(more_kernel, b, kind, last is not None),
        out_shape=shape,
        in_specs=[SMEM] + [VMEM] * (len(args) - 1),
        out_specs=VMEM,
        scratch_shapes=scratch,
        compiler_params=PARAMS,
        cost_estimate=cost(4 * positions * channels * hidden, positions * hidden),
        name="more" if last is None else "more_last",
    )(*args)


def halo(block, reach, odd):
    rows, count = block.shape[0], lax.axis_size("row")
    first, final = 0, rows - reach
    within = [(i, i ^ 1) for i in range(count)]
    across = [(i, i + 1) for i in range(1, count - 1, 2)]
    across += [(target, source) for source, target in across]
    pick = lambda start: lax.dynamic_slice_in_dim(block, start, reach, 0)
    far = lax.ppermute(pick(jnp.where(odd == 1, final, first)), "row", across)
    near = lax.ppermute(pick(jnp.where(odd == 1, first, final)), "row", within)
    return near, far


def after(array, *earlier):
    return lax.optimization_barrier((array, *earlier))[0]


def quarter(w_up, b_up, w_down):
    hidden = w_up.shape[1] // 2
    start = lax.rem(lax.axis_index("row"), 2) * hidden
    up = lax.dynamic_slice_in_dim(w_up, start, hidden, 1)
    down = lax.dynamic_slice_in_dim(w_down, start, hidden, 0)
    bias = lax.dynamic_slice_in_dim(b_up, start, hidden, 0)
    high = lax.reduce_precision(bias, 8, 7)
    bias = jnp.pad(jnp.stack([high, bias - high]).astype(jnp.bfloat16), ((0, MARGIN - 2), (0, 0)))
    return up, jnp.concatenate([down, bias])


def swap_hid(array):
    return lax.ppermute(array, "hid", [(0, 1), (1, 0)])


def swap_row(array, bit):
    return lax.ppermute(array, "row", [(i, i ^ bit) for i in range(lax.axis_size("row"))])


def gather(w_up, b_up, w_down):
    number, me = lax.axis_size("hid"), lax.axis_index("hid")
    arrays = [lax.all_gather(a, "hid") for a in (w_up, b_up.reshape(1, -1), w_down)]
    pick = lambda a, k: lax.dynamic_index_in_dim(a, lax.rem(me + k, number), 0, keepdims=False)
    return [tuple(pick(a, k) for a in arrays) for k in range(1, number)]


def shards(features, dw_weight, dw_bias, ln_gain, ln_bias, w_up, b_up, w_down, b_down, layer_scale):
    blocks, reach = dw_weight.shape[0], dw_weight.shape[1] // 2
    rows, columns, channels = features.shape
    number, me = lax.axis_size("hid"), lax.axis_index("hid")
    row, count = lax.axis_index("row"), lax.axis_size("row")
    odd, high = lax.rem(row, 2), lax.rem(row // 4, 2)
    width = columns // number
    pairs = number == 2 and w_up.shape[2] == 2 * channels and count % 8 == 0

    def window(b):
        extra = MARGIN * (blocks - 1 - b)
        size = min(columns, width + (extra if number == 2 else 2 * extra))
        return jnp.clip(me * width - extra, 0, columns - size), size

    state, start = features, 0
    fetched = None
    for b in range(blocks):
        to, size = window(b)
        if b == 0:
            from_halo = to
            near, far = halo(lax.dynamic_slice_in_dim(state, to, size, 1), reach, odd)
        else:
            from_halo = start
            near, far = halo(state, reach, odd)
        place = jnp.stack([to - start, from_halo - to + MARGIN, odd, high]).astype(jnp.int32)
        before = conv_own(b, place, state, size, dw_weight, dw_bias)
        if pairs and b == 0:
            up, down = quarter(w_up[b], b_up[b], w_down[b])
            mine = swap_hid(lax.dynamic_slice_in_dim(up, high * (channels // 2), channels // 2, 0))
            down = swap_hid(down)
            mine = after(mine, before)
            other = swap_row(mine, 4)
            before = after(before, mine)
        normed, total = conv_rest(
            b, place, near, far, before, dw_weight, ln_gain, ln_bias, w_up, b_up, w_down
        )
        if not pairs:
            parts = gather(w_up[b], b_up[b], w_down[b])
        elif b == 0:
            down = after(down, total)
            parts = [(mine, other, down), tuple(swap_row(a, 1) for a in (mine, other, down))]
            if blocks > 1:
                fetched = swap_hid(after(jnp.concatenate(quarter(w_up[1], b_up[1], w_down[1])), down))
        else:
            fetched = after(fetched, total)
            parts = [(fetched,), (swap_row(fetched, 1),)]
            if b + 1 < blocks:
                weights = (w_up[b + 1], b_up[b + 1], w_down[b + 1])
                fetched = swap_hid(after(jnp.concatenate(quarter(*weights)), fetched))
        ending = (state, b_down, layer_scale)
        for k, part in enumerate(parts):
            last = ending if k == len(parts) - 1 else None
            total = more(b, place, normed, total, part, last, rows)
        state, start = total, to
    if number == 2:
        other = swap_hid(state)
        left, right = jnp.where(me == 0, state, other), jnp.where(me == 0, other, state)
        return jnp.concatenate([left, right], axis=1)
    return lax.all_gather(state, "hid", axis=1, tiled=True)


def solution(mesh):
    return jax.shard_map(
        shards,
        mesh=mesh,
        in_specs=(
            P("row", None, None),
            P(),
            P(),
            P(),
            P(),
            P(None, None, "hid"),
            P(None, "hid"),
            P(None, "hid", None),
            P(),
            P(),
        ),
        out_specs=P("row", None, None),
        check_vma=False,
    )
```

time: 207 us -> 76.4 us (0.37)
  waiting for transfers between devices: 112 us -> 26.5 us
  other arithmetic: 40.2 us -> 2.41 us
  Pallas kernels: 0 us -> 27.5 us
  matrix products: 24.3 us -> 0 us
  between operations: 13.8 us -> 0.32 us
  local copies, waits for them, and re-layouts: 3.63 us -> 6.84 us
    psum x2 -> x0, waiting for transfers between devices: 80 us -> none  [shards(): lax.psum(partial_sum.astype(jnp.bfloat16), 'hid').astype(jnp.float32)]
    reduce_sum x4 -> x0, other arithmetic: 33.4 us -> none  [the longest x2 32.3 us: expand(): mean = jnp.mean(values, axis=1, keepdims=True)]
    pallas_call x0 -> x8, Pallas kernels: none -> 27.5 us  [the longest x2 12.8 us: conv_rest(): pl.pallas_call(functools.partial(rest_kernel, b), out_shape=(jax.ShapeDty...]
    dot_general x4 -> x0, matrix products: 24.3 us -> none  [the longest x2 19.9 us: expand(): jnp.dot(normed, w_first, preferred_element_type=jnp.float32) + b_first]
    ppermute x4 -> x13, waiting for transfers between devices: 31.6 us -> 26.5 us  [the longest x2 13.6 us: halo(): far = lax.ppermute(pick(jnp.where(odd == 1, final, first)), 'row', across)]
    convert_element_type x4 -> x0, other arithmetic: 5.12 us -> none  [the longest x2 4.17 us: shards(): (state.astype(jnp.float32) + layer_scale[b] * (summed + b_down[b])).astyp...]
    slice x15 -> x3, local copies, waits for them, and re-layouts: 2.15 us -> 4.46 us  [the longest x1 2.77 us: shards(): w_up[1]]
    dynamic_slice x0 -> x5, local copies, waits for them, and re-layouts: none -> 2.2 us  [the longest x2 1.2 us: halo(): pick = lambda start: lax.dynamic_slice_in_dim(block, start, reach, 0)]
  transfers between devices with their start and end apart: 6 -> 13, of which waited for: 4 -> 4; matrix products, arithmetic and copies ran while one was open for 0% -> 6% of each run, Pallas kernels for 0% -> 34%
where the time goes in v1:
time: 76.4 us; the launch traced here: 74.9 us
  Pallas kernels  27.5 us (36%)
  waiting for transfers between devices  26.5 us (35%)
  starting transfers between devices  11.4 us (15%)
  local copies, waits for them, and re-layouts  6.84 us (9%)
  other arithmetic  2.41 us (3%)
    ppermute x2, waiting for transfers between devices, halo(): far = lax.ppermute(pick(jnp.where(odd == 1, final, first)), 'row', across)  13.6 us
    pallas_call x2, Pallas kernels, conv_rest(): pl.pallas_call(functools.partial(rest_kernel, b), out_shape=(jax.ShapeDty...  12.8 us
    ppermute x4, waiting for transfers between devices, swap_hid(): return lax.ppermute(array, 'hid', [(0, 1), (1, 0)])  12.6 us
    pallas_call x4, Pallas kernels, more(): pl.pallas_call(functools.partial(more_kernel, b, kind, last is not None),...  8.6 us
    pallas_call x2, Pallas kernels, conv_own(): pl.pallas_call(functools.partial(own_kernel, b), out_shape=jax.ShapeDtype...  6.17 us
    ppermute x2, starting transfers between devices, halo(): far = lax.ppermute(pick(jnp.where(odd == 1, final, first)), 'row', across)  5.75 us
    ppermute x4, starting transfers between devices, swap_hid(): return lax.ppermute(array, 'hid', [(0, 1), (1, 0)])  4.18 us
    slice x1, local copies, waits for them, and re-layouts, shards(): w_up[1]  2.77 us
  transfers between devices with their start and end apart: 13, of which 4 were waited for; matrix products, arithmetic and copies ran while one was open for 6% of the time, Pallas kernels for 34%

profile of v1, /device:TPU:12, one launch (start us, length us, event | category | flops | bytes accessed | tf_op | source)
XLA Modules:
  0.0 74.9 jit_solution(4405835362591459528)
XLA Ops:
  0.0 2.8 %fusion.8 = (bf16[1,512,1024]{2,1,0:T(8,128)(2,1)}, bf16[1,512,1024]{2,1,0:T(8,128)(2,1)S(1)}) fusion(bf16[2,512,1024]{2,1,0:T(8,128)(2,1)} %up.3), kind=kLoop, calls=%fused_computation.30 | loop fusion | bytes 4194304 | tf_op jit(solution)/shard_map/slice | solution.py:322
  2.8 0.9 %dynamic-slice_bitcast_fusion.3 = bf16[256,512]{1,0:T(8,128)(2,1)} fusion(bf16[1,512,1024]{2,1,0:T(8,128)(2,1)S(1)} %get-tuple-element.24, s32[]{:T(128)S(6)} %select_n.57, s32[]{:T(128)S(6)} %select_n.59), kind=kLoop, calls=%fused_computation.8 | loop fusion | bytes 524296 | tf_op jit(solution)/shard_map/dynamic_slice | solution.py:308
  3.6 1.5 %collective-permute-start.2 = (bf16[256,512]{1,0:T(8,128)(2,1)}, bf16[256,512]{1,0:T(8,128)(2,1)S(1)}, u32[]{:S(2)}, u32[]{:S(2)}) collective-permute-start(bf16[256,512]{1,0:T(8,128)(2,1)} %dynamic-slice_bitcast_fusion.3), channel_id=1, source_target_pairs={{0,1},{1,0},{2,3},{3,2},{4,5},{5,4},{6,7},{7,6},{8,9},{9,8},{10,11... | collective-permute-start | bytes 786440 | tf_op jit(solution)/shard_map/ppermute | solution.py:266
  5.4 2.5 %collective-permute-start.1 = (bf16[3,144,512]{2,1,0:T(8,128)(2,1)S(1)}, bf16[3,144,512]{2,1,0:T(8,128)(2,1)S(1)}, u32[]{:S(2)}, u32[]{:S(2)}) collective-permute-start(bf16[3,144,512]{2,1,0:T(8,128)(2,1)S(1)} %get-tuple-element.29), channel_id=1, source_target_pairs={{2,4},{6,8},{10,12},{14,16},{18,20},{22,24},{26,28},{4,2},{8,6},{1... | collective-permute-start | bytes 1327112 | tf_op jit(solution)/shard_map/ppermute | solution.py:245
  8.0 1.7 %fusion.9 = (bf16[1,1024,512]{2,1,0:T(8,128)(2,1)S(1)}, bf16[1,1024,512]{2,1,0:T(8,128)(2,1)S(1)}) fusion(bf16[2,1024,512]{2,1,0:T(8,128)(2,1)} %down.3), kind=kLoop, calls=%fused_computation.31 | loop fusion | bytes 4194304 | tf_op jit(solution)/shard_map/slice | solution.py:322
  9.8 0.6 collective-permute-start.4
  10.6 3.2 %conv_own.2.before = f32[4,4,144,128]{3,2,1,0:T(8,128)S(1)} custom-call(s32[4]{0:T(128)S(1)} %add_add_fusion.1.place, bf16[4,256,512]{2,1,0:T(8,128)(2,1)S(1)} %copy-done.1, f32[2,7,7,512]{3,2,1,0:T(8,128)S(1)} %copy.11.taps, f32[2,512]{1,0:T(2,128)S(1)} %copy-done.4), custom_call_target="tpu_custom_call" | custom-call | flops 66060288 | bytes 129024 | tf_op jit(solution)/shard_map/conv_own/pallas_call | solution.py:179
  14.1 0.5 collective-permute-start.3
  14.6 5.2 %collective-permute-done.1.far = bf16[3,144,512]{2,1,0:T(8,128)(2,1)S(1)} collective-permute-done((bf16[3,144,512]{2,1,0:T(8,128)(2,1)S(1)}, bf16[3,144,512]{2,1,0:T(8,128)(2,1)S(1)}, u32[]{:S(2)}, u32[]{:S(2)}) %collective-permute-start.1) | collective-permute-done | bytes 442400 | tf_op jit(solution)/shard_map/ppermute | solution.py:245
  19.8 6.5 %conv_rest.2 = (bf16[576,512]{1,0:T(8,128)(2,1)S(1)}, f32[576,512]{1,0:T(8,128)S(1)}) custom-call(s32[4]{0:T(128)S(1)} %add_add_fusion.1.place, bf16[3,144,512]{2,1,0:T(8,128)(2,1)S(1)} %collective-permute-done.near, bf16[3,144,512]{2,1,0:T(8,128)(2,1)S(1)} %collective-permute-done.1.far, f32[4,4,144,128]{3,2,1,0:T(8,128)S(1)} %conv_own.2.before, ...), custom_call_target="tpu_custom_call" | custom-call | flops 1207959552 | bytes 2359296 | tf_op jit(solution)/shard_map/conv_rest/pallas_call | solution.py:195
  26.4 1.1 %pad_maximum_fusion = bf16[1040,512]{1,0:T(8,128)(2,1)} fusion(bf16[16,512]{1,0:T(8,128)(2,1)S(1)} %fusion.5, bf16[512,512]{1,0:T(8,128)(2,1)S(1)} %get-tuple-element.39, bf16[512,512]{1,0:T(8,128)(2,1)S(1)} %get-tuple-element.40), kind=kLoop, calls=%fused_computation | loop fusion | flops 3194880 | bytes 2129920 | tf_op jit(solution)/shard_map/concatenate | solution.py:322
  27.5 0.5 collective-permute-start.10
  28.5 2.1 %more.2.before = f32[576,512]{1,0:T(8,128)S(1)} custom-call(s32[4]{0:T(128)S(1)} %add_add_fusion.1.place, bf16[576,512]{1,0:T(8,128)(2,1)S(1)} %get-tuple-element.16.x, f32[576,512]{1,0:T(8,128)S(1)} %get-tuple-element.17.before, bf16[256,512]{1,0:T(8,128)(2,1)S(1)} %collective-permute-done.2.refs_0_, bf16[256,512]{1,0:T(8,128)(2,1)S(1)} %collective-permute-done.3.refs_1_, ...), custom_call_target="tpu_custom_call" | custom-call | flops 603979776 | bytes 1179648 | tf_op jit(solution)/shard_map/more/pallas_call | solution.py:226
  30.7 2.1 %more_last.2.own.refs_1_ = bf16[4,144,512]{2,1,0:T(8,128)(2,1)S(1)} custom-call(s32[4]{0:T(128)S(1)} %add_add_fusion.1.place, bf16[576,512]{1,0:T(8,128)(2,1)S(1)} %get-tuple-element.16.x, f32[576,512]{1,0:T(8,128)S(1)} %more.2.before, bf16[256,512]{1,0:T(8,128)(2,1)S(1)} %collective-permute-done.5.refs_0_, ...), custom_call_target="tpu_custom_call" | custom-call | flops 603979776 | bytes 1179648 | tf_op jit(solution)/shard_map/more_last/pallas_call | solution.py:226
  32.8 1.0 %constant_dynamic-slice_fusion.1 = (bf16[3,144,512]{2,1,0:T(8,128)(2,1)}, bf16[3,144,512]{2,1,0:T(8,128)(2,1)}) fusion(bf16[4,144,512]{2,1,0:T(8,128)(2,1)S(1)} %more_last.2.own.refs_1_, s32[]{:T(128)S(6)} %select_n.54, s32[]{:T(128)S(6)} %select_n.52), kind=kLoop, calls=%fused_computation.17 | loop fusion | bytes 1769480 | tf_op jit(solution)/shard_map/dynamic_slice | solution.py:244
  34.0 3.3 %collective-permute-start.9 = (bf16[3,144,512]{2,1,0:T(8,128)(2,1)}, bf16[3,144,512]{2,1,0:T(8,128)(2,1)}, u32[]{:S(2)}, u32[]{:S(2)}) collective-permute-start(bf16[3,144,512]{2,1,0:T(8,128)(2,1)} %get-tuple-element.31), channel_id=1, source_target_pairs={{2,4},{6,8},{10,12},{14,16},{18,20},{22,24},{26,28},{4,2},{8,6},{1... | collective-permute-start | bytes 1327112 | tf_op jit(solution)/shard_map/ppermute | solution.py:245
  37.3 2.9 %conv_own.3.before = f32[4,4,128,128]{3,2,1,0:T(8,128)S(1)} custom-call(s32[4]{0:T(128)S(1)} %add_add_fusion.place, bf16[4,144,512]{2,1,0:T(8,128)(2,1)S(1)} %more_last.2.own.refs_1_, f32[2,7,7,512]{3,2,1,0:T(8,128)S(1)} %copy.11.taps, f32[2,512]{1,0:T(2,128)S(1)} %copy-done.4), custom_call_target="tpu_custom_call" | custom-call | flops 58720256 | bytes 114688 | tf_op jit(solution)/shard_map/conv_own/pallas_call | solution.py:179
  40.3 8.4 %collective-permute-done.9.far = bf16[3,144,512]{2,1,0:T(8,128)(2,1)} collective-permute-done((bf16[3,144,512]{2,1,0:T(8,128)(2,1)}, bf16[3,144,512]{2,1,0:T(8,128)(2,1)}, u32[]{:S(2)}, u32[]{:S(2)}) %collective-permute-start.9) | collective-permute-done | bytes 442400 | tf_op jit(solution)/shard_map/ppermute | solution.py:245
  48.6 6.2 %conv_rest.3 = (bf16[512,512]{1,0:T(8,128)(2,1)S(1)}, f32[512,512]{1,0:T(8,128)S(1)}) custom-call(s32[4]{0:T(128)S(1)} %add_add_fusion.place, bf16[3,144,512]{2,1,0:T(8,128)(2,1)S(1)} %collective-permute-done.8.near, bf16[3,144,512]{2,1,0:T(8,128)(2,1)} %collective-permute-done.9.far, f32[4,4,128,128]{3,2,1,0:T(8,128)S(1)} %conv_own.3.before, ...), custom_call_target="tpu_custom_call" | custom-call | flops 1073741824 | bytes 2097152 | tf_op jit(solution)/shard_map/conv_rest/pallas_call | solution.py:195
  54.9 2.6 %more.3.before = f32[512,512]{1,0:T(8,128)S(1)} custom-call(s32[4]{0:T(128)S(1)} %add_add_fusion.place, bf16[512,512]{1,0:T(8,128)(2,1)S(1)} %get-tuple-element.19.x, f32[512,512]{1,0:T(8,128)S(1)} %get-tuple-element.20.before, bf16[1040,512]{1,0:T(8,128)(2,1)} %collective-permute-done.10.refs_0_), custom_call_target="tpu_custom_call" | custom-call | flops 536870912 | bytes 1048576 | tf_op jit(solution)/shard_map/more/pallas_call | solution.py:226
  57.8 1.9 %more_last.3 = bf16[4,128,512]{2,1,0:T(8,128)(2,1)S(1)} custom-call(s32[4]{0:T(128)S(1)} %add_add_fusion.place, bf16[512,512]{1,0:T(8,128)(2,1)S(1)} %get-tuple-element.19.x, f32[512,512]{1,0:T(8,128)S(1)} %more.3.before, bf16[1040,512]{1,0:T(8,128)(2,1)S(1)} %collective-permute-done.11.refs_0_, bf16[4,144,512]{2,1,0:T(8,128)(2,1)S(1)} %more_last.2.own.refs_1_, ...), custom_call_target="tpu_custom_call" | custom-call | flops 536870912 | bytes 1048576 | tf_op jit(solution)/shard_map/more_last/pallas_call | solution.py:226
  59.7 1.6 %collective-permute-start.12 = (bf16[4,128,512]{2,1,0:T(8,128)(2,1)S(1)}, bf16[4,128,512]{2,1,0:T(8,128)(2,1)S(1)}, u32[]{:S(2)}, u32[]{:S(2)}) collective-permute-start(bf16[4,128,512]{2,1,0:T(8,128)(2,1)S(1)} %more_last.3), channel_id=1, source_target_pairs={{0,1},{1,0},{2,3},{3,2},{4,5},{5,4},{6,7},{7,6},{8,9},{9,8},{10,11... | collective-permute-start | bytes 1572872 | tf_op jit(solution)/shard_map/ppermute | solution.py:266
  61.3 12.5 %collective-permute-done.12 = bf16[4,128,512]{2,1,0:T(8,128)(2,1)S(1)} collective-permute-done((bf16[4,128,512]{2,1,0:T(8,128)(2,1)S(1)}, bf16[4,128,512]{2,1,0:T(8,128)(2,1)S(1)}, u32[]{:S(2)}, u32[]{:S(2)}) %collective-permute-start.12) | collective-permute-done | bytes 524320 | tf_op jit(solution)/shard_map/ppermute | solution.py:266
  73.9 1.0 %pad_maximum_fusion.1 = bf16[4,256,512]{2,1,0:T(8,128)(2,1)} fusion(bf16[4,128,512]{2,1,0:T(8,128)(2,1)S(1)} %get-tuple-element.28, bf16[4,128,512]{2,1,0:T(8,128)(2,1)S(1)} %get-tuple-element.27), kind=kLoop, calls=%fused_computation.1 | loop fusion | flops 2097152 | bytes 2097152 | tf_op jit(solution)/shard_map/concatenate | solution.py:337
  (51 shorter events, 2.1 us)
Async XLA Ops:
  0.0 5.1 %copy-start.1 = (bf16[4,256,512]{2,1,0:T(8,128)(2,1)S(1)}, bf16[4,256,512]{2,1,0:T(8,128)(2,1)}, u32[]{:S(2)}) copy-start(bf16[4,256,512]{2,1,0:T(8,128)(2,1)} %refs_3_.2) | copy-start | bytes 3145732
  2.8 5.2 %copy-start.3 = (f32[2,1024]{1,0:T(2,128)S(1)}, f32[2,1024]{1,0:T(2,128)}, u32[]{:S(2)}) copy-start(f32[2,1024]{1,0:T(2,128)} %b_up.3) | copy-start | bytes 24580
  3.6 10.4 %collective-permute-start.2 = (bf16[256,512]{1,0:T(8,128)(2,1)}, bf16[256,512]{1,0:T(8,128)(2,1)S(1)}, u32[]{:S(2)}, u32[]{:S(2)}) collective-permute-start(bf16[256,512]{1,0:T(8,128)(2,1)} %dynamic-slice_bitcast_fusion.3), channel_id=1, source_target_pairs={{0,1},{1,0},{2,3},{3,2},{4,5},{5,4},{6,7},{7,6},{8,9},{9,8},{10,11... | collective-permute-start | bytes 786440 | tf_op jit(solution)/shard_map/ppermute | solution.py:266
  5.3 9.2 %collective-permute-start = (bf16[3,144,512]{2,1,0:T(8,128)(2,1)S(1)}, bf16[3,144,512]{2,1,0:T(8,128)(2,1)S(1)}, u32[]{:S(2)}, u32[]{:S(2)}) collective-permute-start(bf16[3,144,512]{2,1,0:T(8,128)(2,1)S(1)} %get-tuple-element.30), channel_id=1, source_target_pairs={{0,2},{2,0},{4,6},{6,4},{8,10},{10,8},{12,14},{14,12},{16,18},{18,... | collective-permute-start | bytes 1327112 | tf_op jit(solution)/shard_map/ppermute | solution.py:246
  5.4 14.4 %collective-permute-start.1 = (bf16[3,144,512]{2,1,0:T(8,128)(2,1)S(1)}, bf16[3,144,512]{2,1,0:T(8,128)(2,1)S(1)}, u32[]{:S(2)}, u32[]{:S(2)}) collective-permute-start(bf16[3,144,512]{2,1,0:T(8,128)(2,1)S(1)} %get-tuple-element.29), channel_id=1, source_target_pairs={{2,4},{6,8},{10,12},{14,16},{18,20},{22,24},{26,28},{4,2},{8,6},{1... | collective-permute-start | bytes 1327112 | tf_op jit(solution)/shard_map/ppermute | solution.py:245
  9.6 0.9 %copy-start.10 = (f32[2,7,7,512]{3,0,2,1:T(2,128)S(1)}, f32[2,7,7,512]{3,0,2,1:T(2,128)}, u32[]{:S(2)}) copy-start(f32[2,7,7,512]{3,0,2,1:T(2,128)} %param.11) | copy-start | bytes 602116
  9.7 0.9 %copy-start.4 = (f32[2,512]{1,0:T(2,128)S(1)}, f32[2,512]{1,0:T(2,128)}, u32[]{:S(2)}) copy-start(f32[2,512]{1,0:T(2,128)} %bias.3) | copy-start | bytes 12292
  9.8 16.5 %collective-permute-start.4 = (bf16[528,512]{1,0:T(8,128)(2,1)S(1)}, bf16[528,512]{1,0:T(8,128)(2,1)S(1)}, u32[]{:S(2)}, u32[]{:S(2)}) collective-permute-start(bf16[528,512]{1,0:T(8,128)(2,1)S(1)} %pad_maximum_fusion.2), channel_id=1, source_target_pairs={{0,1},{1,0},{2,3},{3,2},{4,5},{5,4},{6,7},{7,6},{8,9},{9,8},{10,11... | collective-permute-start | bytes 1622024 | tf_op jit(solution)/shard_map/ppermute | solution.py:266
  10.6 3.3 %copy-start.9 = (bf16[1,512,1024]{2,1,0:T(8,128)(2,1)S(1)}, bf16[1,512,1024]{2,1,0:T(8,128)(2,1)}, u32[]{:S(2)}) copy-start(bf16[1,512,1024]{2,1,0:T(8,128)(2,1)} %get-tuple-element.23) | copy-start | bytes 3145732
  13.9 5.9 %copy-start = (bf16[2,512,1024]{2,1,0:T(8,128)(2,1)S(1)}, bf16[2,512,1024]{2,1,0:T(8,128)(2,1)}, u32[]{:S(2)}) copy-start(bf16[2,512,1024]{2,1,0:T(8,128)(2,1)} %up.3) | copy-start | bytes 6291460
  13.9 5.9 %copy-start.5 = (f32[2,512]{1,0:T(2,128)S(1)}, f32[2,512]{1,0:T(2,128)}, u32[]{:S(2)}) copy-start(f32[2,512]{1,0:T(2,128)} %gain.3) | copy-start | bytes 12292
  13.9 5.9 %copy-start.6 = (f32[2,512]{1,0:T(2,128)S(1)}, f32[2,512]{1,0:T(2,128)}, u32[]{:S(2)}) copy-start(f32[2,512]{1,0:T(2,128)} %shift.3) | copy-start | bytes 12292
  14.1 14.2 %collective-permute-start.3 = (bf16[256,512]{1,0:T(8,128)(2,1)S(1)}, bf16[256,512]{1,0:T(8,128)(2,1)S(1)}, u32[]{:S(2)}, u32[]{:S(2)}) collective-permute-start(bf16[256,512]{1,0:T(8,128)(2,1)S(1)} %collective-permute-done.2.refs_0_), channel_id=1, source_target_pairs={{0,8},{2,10},{4,12},{6,14},{8,0},{10,2},{12,4},{14,6},{16,24},{18,... | collective-permute-start | bytes 786440 | tf_op jit(solution)/shard_map/ppermute | solution.py:270
  26.4 4.3 %collective-permute-start.7 = (bf16[528,512]{1,0:T(8,128)(2,1)S(1)}, bf16[528,512]{1,0:T(8,128)(2,1)S(1)}, u32[]{:S(2)}, u32[]{:S(2)}) collective-permute-start(bf16[528,512]{1,0:T(8,128)(2,1)S(1)} %collective-permute-done.4.refs_2_), channel_id=1, source_target_pairs={{0,2},{2,0},{4,6},{6,4},{8,10},{10,8},{12,14},{14,12},{16,18},{18,... | collective-permute-start | bytes 1622024 | tf_op jit(solution)/shard_map/ppermute | solution.py:270
  27.5 27.4 %collective-permute-start.10 = (bf16[1040,512]{1,0:T(8,128)(2,1)}, bf16[1040,512]{1,0:T(8,128)(2,1)}, u32[]{:S(2)}, u32[]{:S(2)}) collective-permute-start(bf16[1040,512]{1,0:T(8,128)(2,1)} %pad_maximum_fusion), channel_id=1, source_target_pairs={{0,1},{1,0},{2,3},{3,2},{4,5},{5,4},{6,7},{7,6},{8,9},{9,8},{10,11... | collective-permute-start | bytes 3194888 | tf_op jit(solution)/shard_map/ppermute | solution.py:266
  28.0 2.6 %collective-permute-start.5 = (bf16[256,512]{1,0:T(8,128)(2,1)S(1)}, bf16[256,512]{1,0:T(8,128)(2,1)S(1)}, u32[]{:S(2)}, u32[]{:S(2)}) collective-permute-start(bf16[256,512]{1,0:T(8,128)(2,1)S(1)} %collective-permute-done.2.refs_0_), channel_id=1, source_target_pairs={{0,2},{2,0},{4,6},{6,4},{8,10},{10,8},{12,14},{14,12},{16,18},{18,... | collective-permute-start | bytes 786440 | tf_op jit(solution)/shard_map/ppermute | solution.py:270
  28.2 2.4 %collective-permute-start.6 = (bf16[256,512]{1,0:T(8,128)(2,1)S(1)}, bf16[256,512]{1,0:T(8,128)(2,1)S(1)}, u32[]{:S(2)}, u32[]{:S(2)}) collective-permute-start(bf16[256,512]{1,0:T(8,128)(2,1)S(1)} %collective-permute-done.3.refs_1_), channel_id=1, source_target_pairs={{0,2},{2,0},{4,6},{6,4},{8,10},{10,8},{12,14},{14,12},{16,18},{18,... | collective-permute-start | bytes 786440 | tf_op jit(solution)/shard_map/ppermute | solution.py:270
  28.5 2.1 %copy-start.2 = (bf16[4,256,512]{2,1,0:T(8,128)(2,1)S(1)}, bf16[4,256,512]{2,1,0:T(8,128)(2,1)}, u32[]{:S(2)}) copy-start(bf16[4,256,512]{2,1,0:T(8,128)(2,1)} %refs_3_.2) | copy-start | bytes 3145732
  28.5 2.1 %copy-start.7 = (f32[2,512]{1,0:T(2,128)S(1)}, f32[2,512]{1,0:T(2,128)}, u32[]{:S(2)}) copy-start(f32[2,512]{1,0:T(2,128)} %refs_2_.1) | copy-start | bytes 12292
  28.5 2.1 %copy-start.8 = (f32[2,512]{1,0:T(2,128)S(1)}, f32[2,512]{1,0:T(2,128)}, u32[]{:S(2)}) copy-start(f32[2,512]{1,0:T(2,128)} %refs_3_.3) | copy-start | bytes 12292
  33.8 6.5 %collective-permute-start.8 = (bf16[3,144,512]{2,1,0:T(8,128)(2,1)}, bf16[3,144,512]{2,1,0:T(8,128)(2,1)S(1)}, u32[]{:S(2)}, u32[]{:S(2)}) collective-permute-start(bf16[3,144,512]{2,1,0:T(8,128)(2,1)} %get-tuple-element.32), channel_id=1, source_target_pairs={{0,2},{2,0},{4,6},{6,4},{8,10},{10,8},{12,14},{14,12},{16,18},{18,... | collective-permute-start | bytes 1327112 | tf_op jit(solution)/shard_map/ppermute | solution.py:246
  34.0 14.7 %collective-permute-start.9 = (bf16[3,144,512]{2,1,0:T(8,128)(2,1)}, bf16[3,144,512]{2,1,0:T(8,128)(2,1)}, u32[]{:S(2)}, u32[]{:S(2)}) collective-permute-start(bf16[3,144,512]{2,1,0:T(8,128)(2,1)} %get-tuple-element.31), channel_id=1, source_target_pairs={{2,4},{6,8},{10,12},{14,16},{18,20},{22,24},{26,28},{4,2},{8,6},{1... | collective-permute-start | bytes 1327112 | tf_op jit(solution)/shard_map/ppermute | solution.py:245
  54.9 3.0 %collective-permute-start.11 = (bf16[1040,512]{1,0:T(8,128)(2,1)}, bf16[1040,512]{1,0:T(8,128)(2,1)S(1)}, u32[]{:S(2)}, u32[]{:S(2)}) collective-permute-start(bf16[1040,512]{1,0:T(8,128)(2,1)} %collective-permute-done.10.refs_0_), channel_id=1, source_target_pairs={{0,2},{2,0},{4,6},{6,4},{8,10},{10,8},{12,14},{14,12},{16,18},{18,... | collective-permute-start | bytes 3194888 | tf_op jit(solution)/shard_map/ppermute | solution.py:270
  59.7 14.1 %collective-permute-start.12 = (bf16[4,128,512]{2,1,0:T(8,128)(2,1)S(1)}, bf16[4,128,512]{2,1,0:T(8,128)(2,1)S(1)}, u32[]{:S(2)}, u32[]{:S(2)}) collective-permute-start(bf16[4,128,512]{2,1,0:T(8,128)(2,1)S(1)} %more_last.3), channel_id=1, source_target_pairs={{0,1},{1,0},{2,3},{3,2},{4,5},{5,4},{6,7},{7,6},{8,9},{9,8},{10,11... | collective-permute-start | bytes 1572872 | tf_op jit(solution)/shard_map/ppermute | solution.py:266

commit v2 on v0

v2 whole, which is shorter than its diff:
```python
import functools

import jax
import jax.numpy as jnp
from jax import lax
from jax.experimental import pallas as pl
from jax.experimental.pallas import tpu as pltpu
from jax.sharding import PartitionSpec as P

LANES = 128
MARGIN = 16
LONG = 10**11
ERF = (
    0.7978842161099958,
    0.03633428353366734,
    -3.3130008237205104e-05,
    -5.524015421773868e-05,
    3.969108888631555e-06,
    -1.33446374821295e-07,
    1.8056156531812635e-09,
)
VMEM = pl.BlockSpec(memory_space=pltpu.VMEM)
SMEM = pl.BlockSpec(memory_space=pltpu.SMEM)
HBM = pl.BlockSpec(memory_space=pltpu.HBM)
PARAMS = pltpu.CompilerParams(vmem_limit_bytes=20 * 1024 * 1024)
COPIES = pltpu.CompilerParams(vmem_limit_bytes=60 * 1024 * 1024)


def gelu(u):
    v = u * u
    p = jnp.full_like(u, ERF[-1])
    for c in ERF[-2::-1]:
        p = p * v + c
    half = 0.5 * u
    return half * jnp.tanh(u * p) + half


def tile_of(width):
    return next(s for s in (48, 32, 16) if width % s == 0)


def row_of(place, d, rows):
    return jnp.where(place[4] * place[2] == 1, rows - 1 - d, d)


def tap_of(place, t, size):
    return jnp.where(place[2] == 1, size - 1 - t, t)


def convolve(b, place, sums, wide, inputs, outputs, taps, c, lanes, start, step):
    size = taps.shape[1]
    reach = size // 2
    for i, position in enumerate(inputs):
        used = [(n, position - d + reach) for n, d in enumerate(outputs)]
        used = [(n, tap_of(place, t, size)) for n, t in used if 0 <= t < size]
        if not used:
            continue
        for j in range(size):
            first = start + MARGIN + j - reach
            x = wide[c, i, first : first + step]
            for n, t in used:
                sums[n] = sums[n] + x * taps[b, t, j : j + 1, lanes]
    return sums


def own_kernel(b, place, own, near, taps, bias, out, wide):
    groups, rows, width, _ = out.shape
    reach = near.shape[0]
    fill_own(place, own, wide, rows)
    back = place[2] if b == 0 else 1
    sources = [(near, jnp.where(back == 1, reach - 1 - k, k)) for k in range(reach)]
    fill_halo(place, sources, wide, rows)
    step = tile_of(width)
    outputs = range(rows)
    inputs = range(rows + reach)

    def group(c, _):
        lanes = pl.ds(pl.multiple_of(c * LANES, LANES), LANES)
        for start in range(0, width, step):
            sums = [jnp.broadcast_to(bias[b : b + 1, lanes], (step, LANES)) for _ in range(rows)]
            sums = convolve(b, place, sums, wide, inputs, outputs, taps, c, lanes, start, step)
            for d in range(rows):
                out[c, d, start : start + step] = sums[d]
        return 0

    lax.fori_loop(0, groups, group, 0)


def fill_own(place, own, wide, rows):
    groups, _, columns, _ = wide.shape
    for k in range(columns // MARGIN):
        at = place[0] + (k - 1) * MARGIN
        inside = (at >= 0) & (at <= own.shape[1] - MARGIN)
        at = pl.multiple_of(jnp.clip(at, 0, own.shape[1] - MARGIN), MARGIN)
        for d in range(rows):
            for c in range(groups):
                x = own[row_of(place, d, rows), pl.ds(at, MARGIN), c * LANES : (c + 1) * LANES]
                x = jnp.where(inside, x.astype(jnp.float32), 0.0)
                wide[c, d, k * MARGIN : (k + 1) * MARGIN] = x


def fill_halo(place, sources, wide, first):
    groups, _, columns, _ = wide.shape
    size = sources[0][0].shape[1]
    at = pl.ds(pl.multiple_of(place[1], 8), size)
    for i, (ref, row) in enumerate(sources):
        for c in range(groups):
            zeros = jnp.zeros((2 * MARGIN, LANES), jnp.float32)
            wide[c, first + i, : 2 * MARGIN] = zeros
            wide[c, first + i, columns - 2 * MARGIN :] = zeros
            x = ref[row, :, c * LANES : (c + 1) * LANES].astype(jnp.float32)
            wide[c, first + i, at] = x


def add_far(b, place, chosen, far, before, taps, conv, wide):
    groups, _, width, _ = before.shape
    reach = taps.shape[1] // 2
    rows = [(ref, k) for ref in far for k in range(ref.shape[0])]
    if b == 0:
        rows = [(far[0], jnp.where(place[2] == 1, k, reach - 1 - k)) for k in range(reach)]
    rows = rows[: max(0, reach - min(chosen))]
    inputs = [-1 - k for k in range(len(rows))]
    fill_halo(place, rows, wide, 0)
    step = tile_of(width)

    def group(c, _):
        lanes = pl.ds(pl.multiple_of(c * LANES, LANES), LANES)
        for start in range(0, width, step):
            sums = [before[c, d, start : start + step] for d in chosen]
            sums = convolve(b, place, sums, wide, inputs, chosen, taps, c, lanes, start, step)
            for n in range(len(chosen)):
                conv[c, n, start : start + step] = sums[n]
        return 0

    lax.fori_loop(0, groups, group, 0)


def normalise(b, conv, gain, shift, out):
    groups, rows, width, _ = conv.shape
    channels = groups * LANES
    for r in range(rows):
        x = [conv[c, r].astype(jnp.bfloat16).astype(jnp.float32) for c in range(groups)]
        mean = jnp.sum(functools.reduce(jnp.add, x), axis=1, keepdims=True) * (1.0 / channels)
        x = [v - mean for v in x]
        var = jnp.sum(functools.reduce(jnp.add, [v * v for v in x]), axis=1, keepdims=True)
        scale = lax.rsqrt(var * (1.0 / channels) + 1e-06)
        for c in range(groups):
            lanes = slice(c * LANES, (c + 1) * LANES)
            y = x[c] * scale * gain[b : b + 1, lanes] + shift[b : b + 1, lanes]
            out[r * width : (r + 1) * width, lanes] = y.astype(out.dtype)


def project(x, up, b_up, down, total, before=None):
    hidden = down.shape[0]
    part = 256 if hidden % 256 == 0 else 128
    for k in range(0, hidden, part):
        u = jnp.dot(x[...], up[:, k : k + part], preferred_element_type=jnp.float32)
        h = gelu(u + b_up[:, k : k + part]).astype(jnp.bfloat16)
        y = jnp.dot(h, down[k : k + part, :], preferred_element_type=jnp.float32)
        if k:
            total[...] += y
        else:
            total[...] = y if before is None else before[...] + y


def rest_kernel(b, chosen, number, place, *refs):
    far, refs = refs[:number], refs[number:]
    before, taps, gain, shift, up, b_up, down, normed, total, conv, wide = refs
    add_far(b, place, chosen, far, before, taps, conv, wide)
    normalise(b, conv, gain, shift, normed)
    project(normed, up.at[b], b_up.at[b : b + 1], down.at[b], total)


def more_kernel(b, chosen, kind, number, final, place, x, before, *refs):
    channels = x.shape[1]
    refs = list(refs)
    parts = [refs.pop(0) for _ in range(number)]
    state, b_down, scale = (refs.pop(0) for _ in range(3))
    out = refs.pop(0)
    sends = [] if final else [refs.pop(0) for _ in range(2)]
    total = refs.pop(0)
    odd, parity = place[2], place[3]
    pieces = []
    if kind == "plain":
        pieces = [(parts[n], parts[n + 1][...], parts[n + 2]) for n in range(0, number, 3)]
    else:
        if kind == "joined":
            views = [(p.at[:channels], p.at[channels : p.shape[0] - MARGIN], p.at[p.shape[0] - MARGIN :]) for p in parts]
        else:
            views = [(p.at[:channels], q, p.at[channels:]) for p, q in zip(parts[::2], parts[1::2])]
        for up, down, bias in views:
            terms = bias[...].astype(jnp.float32)
            pieces.append((up, terms[0:1] + terms[1:2], down))
    first = before
    for piece in pieces:
        project(x, *piece, total, first)
        first = total
    count, width, _ = out.shape
    rows = state.shape[0]
    for n, d in enumerate(chosen):
        at = pl.ds(pl.multiple_of(place[0], MARGIN), width)
        s = state[row_of(place, d, rows), at, :].astype(jnp.float32)
        y = first[n * width : (n + 1) * width, :] + b_down[b : b + 1]
        s = s + scale[b : b + 1] * y
        if final:
            out[jnp.where(odd == 1, count - 1 - n, n)] = s.astype(out.dtype)
            continue
        out[n] = s.astype(out.dtype)
        total[n * width : (n + 1) * width, :] = s
        far, near = sends
        size = near.shape[1]
        s = total[pl.ds(pl.multiple_of(n * width + place[5], 8), size), :].astype(out.dtype)
        reach = near.shape[0]
        if d < reach:
            far[d] = s
        if d >= rows - reach:
            near[d - (rows - reach)] = s


def take(b, place, weights, parts, up, down, bias, terms):
    w_up, b_up, w_down = weights
    hidden = w_up.shape[2] // parts
    at = place[2] * (w_up.shape[2] // 2) + (place[3] * hidden if parts == 4 else 0)
    at = pl.ds(pl.multiple_of(at, hidden), hidden)
    value = b_up[b : b + 1, at]
    high = value.astype(jnp.bfloat16).astype(jnp.float32)
    low = (value - high).astype(jnp.bfloat16).astype(jnp.float32)
    row = lax.broadcasted_iota(jnp.int32, (MARGIN, hidden), 0)
    terms[...] = jnp.where(row == 0, high, jnp.where(row == 1, low, 0.0)).astype(terms.dtype)
    return [(w_up.at[b, :, at], up), (w_down.at[b, at, :], down), (terms, bias)]


def carry(copies, sems):
    copies = [pltpu.make_async_copy(*copy, sems.at[n]) for n, copy in enumerate(copies)]
    for copy in copies:
        copy.start()
    for copy in copies:
        copy.wait()


def prepare_kernel(place, features, *refs):
    weights, refs = refs[: 3 if len(refs) > 3 else 0], refs[3 if len(refs) > 3 else 0 :]
    outer, inner, *refs = refs
    reach, size, _ = outer.shape
    last = features.shape[0] - reach
    at = pl.ds(pl.multiple_of(place[6], MARGIN), size)
    copies = [
        (features.at[pl.ds(place[2] * last, reach), at], outer),
        (features.at[pl.ds((1 - place[2]) * last, reach), at], inner),
    ]
    if weights:
        up, down, terms, _ = refs
        channels = features.shape[2]
        copies += take(0, place, weights, 4, up.at[:channels], down, up.at[channels:], terms)
    carry(copies, refs[-1])


def pack_kernel(b, place, w_up, b_up, w_down, out, terms, sems):
    channels, last = w_up.shape[1], out.shape[0] - MARGIN
    outs = out.at[:channels], out.at[channels:last], out.at[last:]
    carry(take(b, place, (w_up, b_up, w_down), 2, *outs, terms), sems)


def cost(flops):
    return pl.CostEstimate(flops=flops, bytes_accessed=0, transcendentals=0)


def prepare(place, features, reach, size, weights=()):
    channels = features.shape[2]
    shapes = [jax.ShapeDtypeStruct((reach, size, channels), jnp.bfloat16)] * 2
    scratch = [pltpu.SemaphoreType.DMA((5,))]
    if weights:
        hidden = weights[0].shape[2] // 4
        sizes = [(channels + MARGIN, hidden), (hidden, channels)]
        shapes += [jax.ShapeDtypeStruct(size, jnp.bfloat16) for size in sizes]
        scratch.insert(0, pltpu.VMEM((MARGIN, hidden), jnp.bfloat16))
    return pl.pallas_call(
        prepare_kernel,
        out_shape=shapes,
        in_specs=[SMEM, HBM] + ([HBM, VMEM, HBM] if weights else []),
        out_specs=[VMEM] * len(shapes),
        scratch_shapes=scratch,
        compiler_params=COPIES,
        cost_estimate=cost(1),
        name="prepare",
    )(place, features, *weights)


def pack(b, place, weights):
    _, channels, hidden = weights[0].shape
    hidden //= 2
    shape = (channels + hidden + MARGIN, channels)
    return pl.pallas_call(
        functools.partial(pack_kernel, b),
        out_shape=jax.ShapeDtypeStruct(shape, jnp.bfloat16),
        in_specs=[SMEM, HBM, VMEM, HBM],
        out_specs=VMEM,
        scratch_shapes=[
            pltpu.VMEM((MARGIN, hidden), jnp.bfloat16),
            pltpu.SemaphoreType.DMA((3,)),
        ],
        compiler_params=PARAMS,
        cost_estimate=cost(1),
        name="pack",
    )(place, *weights)


def conv_own(b, place, own, near, width, taps, bias):
    rows, _, channels = own.shape
    groups, reach = channels // LANES, near.shape[0]
    return pl.pallas_call(
        functools.partial(own_kernel, b),
        out_shape=jax.ShapeDtypeStruct((groups, rows, width, LANES), jnp.float32),
        in_specs=[SMEM] + [VMEM] * 4,
        out_specs=VMEM,
        scratch_shapes=[
            pltpu.VMEM((groups, rows + reach, width + 2 * MARGIN, LANES), jnp.float32)
        ],
        compiler_params=PARAMS,
        cost_estimate=cost(1),
        name="conv_own",
    )(place, own, near, taps, bias)


def conv_rest(b, chosen, place, far, before, taps, gain, shift, up, b_up, down):
    groups, _, width, _ = before.shape
    channels, reach = groups * LANES, taps.shape[1] // 2
    positions = len(chosen) * width
    args = [place, *far, before, taps, gain, shift, up, b_up, down]
    return pl.pallas_call(
        functools.partial(rest_kernel, b, chosen, len(far)),
        out_shape=(
            jax.ShapeDtypeStruct((positions, channels), jnp.bfloat16),
            jax.ShapeDtypeStruct((positions, channels), jnp.float32),
        ),
        in_specs=[SMEM] + [VMEM] * (len(args) - 1),
        out_specs=(VMEM, VMEM),
        scratch_shapes=[
            pltpu.VMEM((groups, len(chosen), width, LANES), jnp.float32),
            pltpu.VMEM((groups, reach, width + 2 * MARGIN, LANES), jnp.float32),
        ],
        compiler_params=PARAMS,
        cost_estimate=cost(LONG if min(chosen) else 1),
        name="conv_rest",
    )(*args)


def more(b, chosen, place, x, before, kind, parts, state, b_down, scale, halo_shape):
    positions, channels = x.shape
    final = halo_shape is None
    args = [place, x, before, *parts, state, b_down, scale]
    shapes = [(len(chosen), positions // len(chosen), channels)]
    if not final:
        reach, size = halo_shape
        shapes += [(reach, size, channels)] * 2
    return pl.pallas_call(
        functools.partial(more_kernel, b, chosen, kind, len(parts), final),
        out_shape=[jax.ShapeDtypeStruct(shape, jnp.bfloat16) for shape in shapes],
        in_specs=[SMEM] + [VMEM] * (len(args) - 1),
        out_specs=[VMEM] * len(shapes),
        scratch_shapes=[pltpu.VMEM((positions, channels), jnp.float32)],
        compiler_params=PARAMS,
        cost_estimate=cost(1),
        name="more",
    )(*args)


def within(array):
    return lax.ppermute(array, "row", [(i, i ^ 1) for i in range(lax.axis_size("row"))])


def across(array):
    pairs = [(i, i + 1) for i in range(1, lax.axis_size("row") - 1, 2)]
    return lax.ppermute(array, "row", pairs + [(target, source) for source, target in pairs])


def swap_hid(array):
    return lax.ppermute(array, "hid", [(0, 1), (1, 0)])


def swap_row(array, bit):
    return lax.ppermute(array, "row", [(i, i ^ bit) for i in range(lax.axis_size("row"))])


def after(array, *earlier):
    return lax.optimization_barrier((array, *earlier))[0]


def gather(w_up, b_up, w_down):
    number, me = lax.axis_size("hid"), lax.axis_index("hid")
    arrays = [lax.all_gather(a, "hid") for a in (w_up, b_up.reshape(1, -1), w_down)]
    pick = lambda a, k: lax.dynamic_index_in_dim(a, lax.rem(me + k, number), 0, keepdims=False)
    return [pick(a, k) for k in range(1, number) for a in arrays]


def shards(features, dw_weight, dw_bias, ln_gain, ln_bias, w_up, b_up, w_down, b_down, layer_scale):
    blocks, reach = dw_weight.shape[0], dw_weight.shape[1] // 2
    rows, columns, channels = features.shape
    number, me = lax.axis_size("hid"), lax.axis_index("hid")
    row, count = lax.axis_index("row"), lax.axis_size("row")
    odd, parity = lax.rem(row, 2), lax.rem(row // 4, 2)
    width = columns // number
    pairs = number == 2 and w_up.shape[2] == 2 * channels and count % 8 == 0

    def window(reach, unit):
        extra = -(-reach // unit) * unit
        size = min(columns, width + (extra if number == 2 else 2 * extra))
        return jnp.clip(me * width - extra, 0, columns - size), size

    def edge(b):
        return window(reach * (blocks - b), 8 if b else MARGIN)

    def place_of(b):
        to, _ = window(reach * (blocks - 1 - b), MARGIN)
        start = window(reach * (blocks - b), MARGIN)[0] if b else 0
        halo, _ = edge(b)
        later, _ = edge(b + 1)
        values = [to - start, halo - to + MARGIN, odd, parity, int(b == 0), later - to, halo]
        return jnp.stack([jnp.int32(v) for v in values])

    places = [place_of(b) for b in range(blocks)]
    everything = tuple(range(rows))
    weights = (w_up, b_up, w_down)

    outer, inner, *first = prepare(
        places[0], features, reach, edge(0)[1], weights if pairs else ()
    )
    far, near = [across(outer)], within(inner)
    state = features
    if pairs:
        up, down = swap_hid(first[0]), swap_hid(first[1])
    for b in range(blocks):
        place, final = places[b], b == blocks - 1
        _, size = window(reach * (blocks - 1 - b), MARGIN)
        before = conv_own(b, place, state, near, size, dw_weight, dw_bias)
        rest = lambda chosen, far, before: conv_rest(
            b, chosen, place, far, before, dw_weight, ln_gain, ln_bias, *weights
        )
        add = lambda chosen, work, parts: more(
            b, chosen, place, *work, kind, parts, state, b_down, layer_scale,
            None if final else (reach, edge(b + 1)[1]),
        )
        if pairs and not final:
            later = swap_hid(pack(b + 1, places[b + 1], weights))
        if pairs and b == 0:
            up = after(up, before)
            up_other, down_other = swap_row(up, 4), swap_row(down, 4)
        elif pairs:
            joined = after(joined, before)
            kind, parts = "joined", [joined, within(joined)]
        halves = (everything[rows // 2 :], everything[: rows // 2]) if final else (everything,)
        work = [rest(chosen, far, before) for chosen in halves]
        if pairs and b == 0:
            up_other, down_other = (after(a, work[0][1]) for a in (up_other, down_other))
            parts = [up, down, up_other, down_other]
            kind, parts = "pairs", parts + [within(a) for a in parts]
        elif not pairs:
            kind, parts = "plain", gather(w_up[b], b_up[b], w_down[b])
        results = [add(chosen, w, parts) for chosen, w in zip(halves, work)]
        if not final:
            state, outer, inner = results[0]
            far, near = [across(outer)], within(inner)
            if pairs:
                joined = later
    inner, outer = (r[0] for r in results)
    if number == 1:
        columns_of = lambda a: a
    elif number == 2:
        def columns_of(a):
            other = swap_hid(a)
            return jnp.concatenate(
                [jnp.where(me == 0, a, other), jnp.where(me == 0, other, a)], axis=1
            )
    else:
        columns_of = lambda a: lax.all_gather(a, "hid", axis=1, tiled=True)
    inner, outer = columns_of(inner), columns_of(outer)
    return jnp.concatenate([jnp.where(odd == 1, inner, outer), jnp.where(odd == 1, outer, inner)])


def solution(mesh):
    return jax.shard_map(
        shards,
        mesh=mesh,
        in_specs=(
            P("row", None, None),
            P(),
            P(),
            P(),
            P(),
            P(None, None, "hid"),
            P(None, "hid"),
            P(None, "hid", None),
            P(),
            P(),
        ),
        out_specs=P("row", None, None),
        check_vma=False,
    )
```

time: 207 us -> 67.3 us (0.33)
  waiting for transfers between devices: 112 us -> 21.2 us
  other arithmetic: 40.2 us -> 1.34 us
  Pallas kernels: 0 us -> 27.5 us
  matrix products: 24.3 us -> 0 us
  between operations: 13.8 us -> 0.26 us
  starting transfers between devices: 11.5 us -> 14.3 us
    psum x2 -> x0, waiting for transfers between devices: 80 us -> none  [shards(): lax.psum(partial_sum.astype(jnp.bfloat16), 'hid').astype(jnp.float32)]
    reduce_sum x4 -> x0, other arithmetic: 33.4 us -> none  [the longest x2 32.3 us: expand(): mean = jnp.mean(values, axis=1, keepdims=True)]
    pallas_call x0 -> x10, Pallas kernels: none -> 27.5 us  [the longest x3 9.63 us: conv_rest(): pl.pallas_call(functools.partial(rest_kernel, b, chosen, len(far)), out_s...]
    dot_general x4 -> x0, matrix products: 24.3 us -> none  [the longest x2 19.9 us: expand(): jnp.dot(normed, w_first, preferred_element_type=jnp.float32) + b_first]
    ppermute x4 -> x16, waiting for transfers between devices: 31.6 us -> 21.2 us  [the longest x5 7.96 us: swap_hid(): return lax.ppermute(array, 'hid', [(0, 1), (1, 0)])]
    convert_element_type x4 -> x0, other arithmetic: 5.12 us -> none  [the longest x2 4.17 us: shards(): (state.astype(jnp.float32) + layer_scale[b] * (summed + b_down[b])).astyp...]
    ppermute x4 -> x16, starting transfers between devices: 11.4 us -> 14.3 us  [the longest x5 5.81 us: swap_hid(): return lax.ppermute(array, 'hid', [(0, 1), (1, 0)])]
    slice x15 -> x0, local copies, waits for them, and re-layouts: 2.15 us -> none  [the longest x2 1.78 us: extended(): lax.slice_in_dim(block, block.shape[dim] - width, None, axis=dim)]
  transfers between devices with their start and end apart: 6 -> 16, of which waited for: 4 -> 7; matrix products, arithmetic and copies ran while one was open for 0% -> 0% of each run, Pallas kernels for 0% -> 34%
where the time goes in v2:
time: 67.3 us; the launch traced here: 67.1 us
  Pallas kernels  27.5 us (41%)
  waiting for transfers between devices  21.2 us (32%)
  starting transfers between devices  14.3 us (21%)
  local copies, waits for them, and re-layouts  2.44 us (4%)
  other arithmetic  1.34 us (2%)
    pallas_call x3, Pallas kernels, conv_rest(): pl.pallas_call(functools.partial(rest_kernel, b, chosen, len(far)), out_s...  9.63 us
    ppermute x5, waiting for transfers between devices, swap_hid(): return lax.ppermute(array, 'hid', [(0, 1), (1, 0)])  7.96 us
    pallas_call x2, Pallas kernels, conv_own(): pl.pallas_call(functools.partial(own_kernel, b), out_shape=jax.ShapeDtype...  7.38 us
    ppermute x2, waiting for transfers between devices, across(): lax.ppermute(array, 'row', pairs + [(target, source) for source, target i...  7.15 us
    pallas_call x3, Pallas kernels, more(): pl.pallas_call(functools.partial(more_kernel, b, chosen, kind, len(parts)...  6.53 us
    ppermute x5, starting transfers between devices, swap_hid(): return lax.ppermute(array, 'hid', [(0, 1), (1, 0)])  5.81 us
    ppermute x2, waiting for transfers between devices, swap_row(): lax.ppermute(array, 'row', [(i, i ^ bit) for i in range(lax.axis_size('ro...  4.9 us
    ppermute x2, starting transfers between devices, across(): lax.ppermute(array, 'row', pairs + [(target, source) for source, target i...  4.86 us
  transfers between devices with their start and end apart: 16, of which 7 were waited for; matrix products, arithmetic and copies ran while one was open for 0% of the time, Pallas kernels for 34%

profile of v2, /device:TPU:12, one launch (start us, length us, event | category | flops | bytes accessed | tf_op | source)
XLA Modules:
  0.0 67.1 jit_solution(504322911806924529)
XLA Ops:
  0.7 3.3 %prepare.1 = (bf16[3,144,512]{2,1,0:T(8,128)(2,1)}, bf16[3,144,512]{2,1,0:T(8,128)(2,1)}, bf16[528,256]{1,0:T(8,128)(2,1)}, bf16[256,512]{1,0:T(8,128)(2,1)}) custom-call(s32[7]{0:T(128)} %stack.40.place, bf16[4,256,512]{2,1,0:T(8,128)(2,1)} %refs_8_.1, bf16[2,512,1024]{2,1,0:T(8,128)(2,1)} %refs_5_.5, f32[2,1024]{1,0:T(2,128)} %refs_6_.5, ...), custom_call_target="tpu_custom_call" | custom-call | flops 1 | tf_op jit(solution)/shard_map/prepare/pallas_call | solution.py:277
  4.1 1.6 %collective-permute-start.2 = (bf16[528,256]{1,0:T(8,128)(2,1)}, bf16[528,256]{1,0:T(8,128)(2,1)S(1)}, u32[]{:S(2)}, u32[]{:S(2)}) collective-permute-start(bf16[528,256]{1,0:T(8,128)(2,1)} %get-tuple-element.26), channel_id=1, source_target_pairs={{0,1},{1,0},{2,3},{3,2},{4,5},{5,4},{6,7},{7,6},{8,9},{9,8},{10,11... | collective-permute-start | bytes 811016 | tf_op jit(solution)/shard_map/ppermute | solution.py:378
  6.2 1.9 %collective-permute-start = (bf16[3,144,512]{2,1,0:T(8,128)(2,1)}, bf16[3,144,512]{2,1,0:T(8,128)(2,1)S(1)}, u32[]{:S(2)}, u32[]{:S(2)}) collective-permute-start(bf16[3,144,512]{2,1,0:T(8,128)(2,1)} %get-tuple-element.22), channel_id=1, source_target_pairs={{2,4},{6,8},{10,12},{14,16},{18,20},{22,24},{26,28},{4,2},{8,6},{1... | collective-permute-start | bytes 1327112 | tf_op jit(solution)/shard_map/ppermute | solution.py:374
  8.2 1.6 %copy-done.1 = bf16[2,1024,512]{2,1,0:T(8,128)(2,1)S(1)} copy-done((bf16[2,1024,512]{2,1,0:T(8,128)(2,1)S(1)}, bf16[2,1024,512]{2,1,0:T(8,128)(2,1)}, u32[]{:S(2)}) %copy-start.1) | copy-done | bytes 2097176
  10.5 1.6 %collective-permute-start.12 = (bf16[1040,512]{1,0:T(8,128)(2,1)S(1)}, bf16[1040,512]{1,0:T(8,128)(2,1)S(1)}, u32[]{:S(2)}, u32[]{:S(2)}) collective-permute-start(bf16[1040,512]{1,0:T(8,128)(2,1)S(1)} %pack.1), channel_id=1, source_target_pairs={{0,1},{1,0},{2,3},{3,2},{4,5},{5,4},{6,7},{7,6},{8,9},{9,8},{10,11... | collective-permute-start | bytes 3194888 | tf_op jit(solution)/shard_map/ppermute | solution.py:378
  12.2 3.9 %conv_own.2.refs_1_ = f32[4,4,144,128]{3,2,1,0:T(8,128)S(1)} custom-call(s32[7]{0:T(128)S(1)} %copy-done.10, bf16[4,256,512]{2,1,0:T(8,128)(2,1)S(1)} %copy-done.3, bf16[3,144,512]{2,1,0:T(8,128)(2,1)S(1)} %collective-permute-done.1.near, f32[2,7,7,512]{3,2,1,0:T(8,128)S(1)} %copy.11.taps.refs_2_, f32[2,512]{1,0:T(2,128)S(1)} %copy-done.7), custom_call_target="tpu_custom_call" | custom-call | flops 1 | tf_op jit(solution)/shard_map/conv_own/pallas_call | solution.py:311
  16.6 2.6 %collective-permute-done.3.refs_1_ = bf16[256,512]{1,0:T(8,128)(2,1)S(1)} collective-permute-done((bf16[256,512]{1,0:T(8,128)(2,1)}, bf16[256,512]{1,0:T(8,128)(2,1)S(1)}, u32[]{:S(2)}, u32[]{:S(2)}) %collective-permute-start.3) | collective-permute-done | bytes 262176 | tf_op jit(solution)/shard_map/ppermute | solution.py:378
  19.7 1.0 %collective-permute-done.refs_0_ = bf16[3,144,512]{2,1,0:T(8,128)(2,1)S(1)} collective-permute-done((bf16[3,144,512]{2,1,0:T(8,128)(2,1)}, bf16[3,144,512]{2,1,0:T(8,128)(2,1)S(1)}, u32[]{:S(2)}, u32[]{:S(2)}) %collective-permute-start) | collective-permute-done | bytes 442400 | tf_op jit(solution)/shard_map/ppermute | solution.py:374
  20.7 4.6 %conv_rest.3 = (bf16[576,512]{1,0:T(8,128)(2,1)S(1)}, f32[576,512]{1,0:T(8,128)S(1)}) custom-call(s32[7]{0:T(128)S(1)} %copy-done.10, bf16[3,144,512]{2,1,0:T(8,128)(2,1)S(1)} %collective-permute-done.refs_0_, f32[4,4,144,128]{3,2,1,0:T(8,128)S(1)} %conv_own.2.refs_1_, f32[2,7,7,512]{3,2,1,0:T(8,128)S(1)} %copy.11.taps.refs_2_, f32[2,512]{1,0:T(2,128)S(1)} %copy-done.8, ...), custom_call_target="tpu_custom_call" | custom-call | flops 1 | tf_op jit(solution)/shard_map/conv_rest/pallas_call | solution.py:330
  25.9 4.9 %collective-permute-done.5.refs_3_ = bf16[256,512]{1,0:T(8,128)(2,1)S(1)} collective-permute-done((bf16[256,512]{1,0:T(8,128)(2,1)S(1)}, bf16[256,512]{1,0:T(8,128)(2,1)S(1)}, u32[]{:S(2)}, u32[]{:S(2)}) %collective-permute-start.5) | collective-permute-done | bytes 262176 | tf_op jit(solution)/shard_map/ppermute | solution.py:382
  31.3 1.2 %collective-permute-done.9.refs_7_ = bf16[256,512]{1,0:T(8,128)(2,1)S(1)} collective-permute-done((bf16[256,512]{1,0:T(8,128)(2,1)S(1)}, bf16[256,512]{1,0:T(8,128)(2,1)S(1)}, u32[]{:S(2)}, u32[]{:S(2)}) %collective-permute-start.9) | collective-permute-done | bytes 262176 | tf_op jit(solution)/shard_map/ppermute | solution.py:369
  32.4 3.1 %more.3 = (bf16[4,144,512]{2,1,0:T(8,128)(2,1)S(1)}, bf16[3,136,512]{2,1,0:T(8,128)(2,1)S(1)}, bf16[3,136,512]{2,1,0:T(8,128)(2,1)S(1)}) custom-call(s32[7]{0:T(128)S(1)} %copy-done.10, bf16[576,512]{1,0:T(8,128)(2,1)S(1)} %get-tuple-element.24.x, f32[576,512]{1,0:T(8,128)S(1)} %get-tuple-element.25.before, ...), custom_call_target="tpu_custom_call" | custom-call | flops 1 | tf_op jit(solution)/shard_map/more/pallas_call | solution.py:356
  36.0 3.0 %collective-permute-start.10 = (bf16[3,136,512]{2,1,0:T(8,128)(2,1)S(1)}, bf16[3,136,512]{2,1,0:T(8,128)(2,1)S(1)}, u32[]{:S(2)}, u32[]{:S(2)}) collective-permute-start(bf16[3,136,512]{2,1,0:T(8,128)(2,1)S(1)} %get-tuple-element.31), channel_id=1, source_target_pairs={{2,4},{6,8},{10,12},{14,16},{18,20},{22,24},{26,28},{4,2},{8,6},{1... | collective-permute-start | bytes 1253384 | tf_op jit(solution)/shard_map/ppermute | solution.py:374
  39.0 3.5 %conv_own.3.refs_1_ = f32[4,4,128,128]{3,2,1,0:T(8,128)S(1)} custom-call(s32[7]{0:T(128)S(1)} %stack.37.place, bf16[4,144,512]{2,1,0:T(8,128)(2,1)S(1)} %get-tuple-element.32.own.refs_2_, bf16[3,136,512]{2,1,0:T(8,128)(2,1)S(1)} %collective-permute-done.11.near, f32[2,7,7,512]{3,2,1,0:T(8,128)S(1)} %copy.11.taps.refs_2_, f32[2,512]{1,0:T(2,128)S(1)} %copy-done.7), custom_call_target="tpu_custom_call" | custom-call | flops 1 | tf_op jit(solution)/shard_map/conv_own/pallas_call | solution.py:311
  42.5 1.2 %collective-permute-start.13 = (bf16[1040,512]{1,0:T(8,128)(2,1)S(1)}, bf16[1040,512]{1,0:T(8,128)(2,1)S(1)}, u32[]{:S(2)}, u32[]{:S(2)}) collective-permute-start(bf16[1040,512]{1,0:T(8,128)(2,1)S(1)} %collective-permute-done.12.refs_0_), channel_id=1, source_target_pairs={{0,2},{2,0},{4,6},{6,4},{8,10},{10,8},{12,14},{14,12},{16,18},{18,... | collective-permute-start | bytes 3194888 | tf_op jit(solution)/shard_map/ppermute | solution.py:369
  43.7 6.1 %collective-permute-done.10.refs_0_ = bf16[3,136,512]{2,1,0:T(8,128)(2,1)S(1)} collective-permute-done((bf16[3,136,512]{2,1,0:T(8,128)(2,1)S(1)}, bf16[3,136,512]{2,1,0:T(8,128)(2,1)S(1)}, u32[]{:S(2)}, u32[]{:S(2)}) %collective-permute-start.10) | collective-permute-done | bytes 417824 | tf_op jit(solution)/shard_map/ppermute | solution.py:374
  49.8 2.2 %conv_rest.4 = (bf16[256,512]{1,0:T(8,128)(2,1)S(1)}, f32[256,512]{1,0:T(8,128)S(1)}) custom-call(s32[7]{0:T(128)S(1)} %stack.37.place, bf16[3,136,512]{2,1,0:T(8,128)(2,1)S(1)} %collective-permute-done.10.refs_0_, f32[4,4,128,128]{3,2,1,0:T(8,128)S(1)} %conv_own.3.refs_1_, f32[2,7,7,512]{3,2,1,0:T(8,128)S(1)} %copy.11.taps.refs_2_, f32[2,512]{1,0:T(2,128)S(1)} %copy-done.8, ...), custom_call_target="tpu_custom_call" | custom-call | flops 99999997952 | tf_op jit(solution)/shard_map/conv_rest/pallas_call | solution.py:330
  52.0 1.7 %more.4 = bf16[2,128,512]{2,1,0:T(8,128)(2,1)S(1)} custom-call(s32[7]{0:T(128)S(1)} %stack.37.place, bf16[256,512]{1,0:T(8,128)(2,1)S(1)} %get-tuple-element.34.x, f32[256,512]{1,0:T(8,128)S(1)} %get-tuple-element.35.before, bf16[1040,512]{1,0:T(8,128)(2,1)S(1)} %collective-permute-done.12.refs_0_, bf16[1040,512]{1,0:T(8,128)(2,1)S(1)} %collective-permute-done.13.refs_1_, ...), custom_call_target="tpu_custom_call" | custom-call | flops 1 | tf_op jit(solution)/shard_map/more/pallas_call | solution.py:356
  54.3 2.8 %conv_rest.5 = (bf16[256,512]{1,0:T(8,128)(2,1)S(1)}, f32[256,512]{1,0:T(8,128)S(1)}) custom-call(s32[7]{0:T(128)S(1)} %stack.37.place, bf16[3,136,512]{2,1,0:T(8,128)(2,1)S(1)} %collective-permute-done.10.refs_0_, f32[4,4,128,128]{3,2,1,0:T(8,128)S(1)} %conv_own.3.refs_1_, f32[2,7,7,512]{3,2,1,0:T(8,128)S(1)} %copy.11.taps.refs_2_, f32[2,512]{1,0:T(2,128)S(1)} %copy-done.8, ...), custom_call_target="tpu_custom_call" | custom-call | flops 1 | tf_op jit(solution)/shard_map/conv_rest/pallas_call | solution.py:330
  57.2 1.7 %more.5 = bf16[2,128,512]{2,1,0:T(8,128)(2,1)S(1)} custom-call(s32[7]{0:T(128)S(1)} %stack.37.place, bf16[256,512]{1,0:T(8,128)(2,1)S(1)} %get-tuple-element.37.x, f32[256,512]{1,0:T(8,128)S(1)} %get-tuple-element.38.before, bf16[1040,512]{1,0:T(8,128)(2,1)S(1)} %collective-permute-done.12.refs_0_, bf16[1040,512]{1,0:T(8,128)(2,1)S(1)} %collective-permute-done.13.refs_1_, ...), custom_call_target="tpu_custom_call" | custom-call | flops 1 | tf_op jit(solution)/shard_map/more/pallas_call | solution.py:356
  58.9 1.6 %collective-permute-start.15 = (bf16[2,128,512]{2,1,0:T(8,128)(2,1)S(1)}, bf16[2,128,512]{2,1,0:T(8,128)(2,1)S(1)}, u32[]{:S(2)}, u32[]{:S(2)}) collective-permute-start(bf16[2,128,512]{2,1,0:T(8,128)(2,1)S(1)} %more.5), channel_id=1, source_target_pairs={{0,1},{1,0},{2,3},{3,2},{4,5},{5,4},{6,7},{7,6},{8,9},{9,8},{10,11... | collective-permute-start | bytes 786440 | tf_op jit(solution)/shard_map/ppermute | solution.py:378
  60.4 2.1 %collective-permute-done.14 = bf16[2,128,512]{2,1,0:T(8,128)(2,1)S(1)} collective-permute-done((bf16[2,128,512]{2,1,0:T(8,128)(2,1)S(1)}, bf16[2,128,512]{2,1,0:T(8,128)(2,1)S(1)}, u32[]{:S(2)}, u32[]{:S(2)}) %collective-permute-start.14) | collective-permute-done | bytes 262176 | tf_op jit(solution)/shard_map/ppermute | solution.py:378
  62.6 3.2 %collective-permute-done.15 = bf16[2,128,512]{2,1,0:T(8,128)(2,1)S(1)} collective-permute-done((bf16[2,128,512]{2,1,0:T(8,128)(2,1)S(1)}, bf16[2,128,512]{2,1,0:T(8,128)(2,1)S(1)}, u32[]{:S(2)}, u32[]{:S(2)}) %collective-permute-start.15) | collective-permute-done | bytes 262176 | tf_op jit(solution)/shard_map/ppermute | solution.py:378
  66.0 1.1 %pad_maximum_fusion = bf16[4,256,512]{2,1,0:T(8,128)(2,1)} fusion(bf16[2,256,512]{2,1,0:T(8,128)(2,1)S(1)} %get-tuple-element.40, bf16[2,256,512]{2,1,0:T(8,128)(2,1)S(1)} %get-tuple-element.39), kind=kLoop, calls=%fused_computation | loop fusion | flops 524288 | bytes 2097152 | tf_op jit(solution)/shard_map/concatenate | solution.py:477
  (49 shorter events, 5.5 us)
Async XLA Ops:
  0.7 7.5 %copy-start = (bf16[2,512,1024]{2,1,0:T(8,128)(2,1)S(1)}, bf16[2,512,1024]{2,1,0:T(8,128)(2,1)}, u32[]{:S(2)}) copy-start(bf16[2,512,1024]{2,1,0:T(8,128)(2,1)} %refs_5_.5) | copy-start | bytes 6291460
  0.7 7.5 %copy-start.4 = (f32[2,1024]{1,0:T(2,128)S(1)}, f32[2,1024]{1,0:T(2,128)}, u32[]{:S(2)}) copy-start(f32[2,1024]{1,0:T(2,128)} %refs_6_.5) | copy-start | bytes 24580
  4.0 8.2 %collective-permute-start.1 = (bf16[3,144,512]{2,1,0:T(8,128)(2,1)}, bf16[3,144,512]{2,1,0:T(8,128)(2,1)S(1)}, u32[]{:S(2)}, u32[]{:S(2)}) collective-permute-start(bf16[3,144,512]{2,1,0:T(8,128)(2,1)} %get-tuple-element.23), channel_id=1, source_target_pairs={{0,2},{2,0},{4,6},{6,4},{8,10},{10,8},{12,14},{14,12},{16,18},{18,... | collective-permute-start | bytes 1327112 | tf_op jit(solution)/shard_map/ppermute | solution.py:369
  4.1 12.0 %collective-permute-start.2 = (bf16[528,256]{1,0:T(8,128)(2,1)}, bf16[528,256]{1,0:T(8,128)(2,1)S(1)}, u32[]{:S(2)}, u32[]{:S(2)}) collective-permute-start(bf16[528,256]{1,0:T(8,128)(2,1)} %get-tuple-element.26), channel_id=1, source_target_pairs={{0,1},{1,0},{2,3},{3,2},{4,5},{5,4},{6,7},{7,6},{8,9},{9,8},{10,11... | collective-permute-start | bytes 811016 | tf_op jit(solution)/shard_map/ppermute | solution.py:378
  5.6 13.6 %collective-permute-start.3 = (bf16[256,512]{1,0:T(8,128)(2,1)}, bf16[256,512]{1,0:T(8,128)(2,1)S(1)}, u32[]{:S(2)}, u32[]{:S(2)}) collective-permute-start(bf16[256,512]{1,0:T(8,128)(2,1)} %get-tuple-element.28), channel_id=1, source_target_pairs={{0,1},{1,0},{2,3},{3,2},{4,5},{5,4},{6,7},{7,6},{8,9},{9,8},{10,11... | collective-permute-start | bytes 786440 | tf_op jit(solution)/shard_map/ppermute | solution.py:378
  6.2 14.6 %collective-permute-start = (bf16[3,144,512]{2,1,0:T(8,128)(2,1)}, bf16[3,144,512]{2,1,0:T(8,128)(2,1)S(1)}, u32[]{:S(2)}, u32[]{:S(2)}) collective-permute-start(bf16[3,144,512]{2,1,0:T(8,128)(2,1)} %get-tuple-element.22), channel_id=1, source_target_pairs={{2,4},{6,8},{10,12},{14,16},{18,20},{22,24},{26,28},{4,2},{8,6},{1... | collective-permute-start | bytes 1327112 | tf_op jit(solution)/shard_map/ppermute | solution.py:374
  9.8 2.4 %copy-start.10 = (s32[7]{0:T(128)S(1)}, s32[7]{0:T(128)}, u32[]{:S(2)}) copy-start(s32[7]{0:T(128)} %stack.40.place) | copy-start | bytes 88
  10.5 32.0 %collective-permute-start.12 = (bf16[1040,512]{1,0:T(8,128)(2,1)S(1)}, bf16[1040,512]{1,0:T(8,128)(2,1)S(1)}, u32[]{:S(2)}, u32[]{:S(2)}) collective-permute-start(bf16[1040,512]{1,0:T(8,128)(2,1)S(1)} %pack.1), channel_id=1, source_target_pairs={{0,1},{1,0},{2,3},{3,2},{4,5},{5,4},{6,7},{7,6},{8,9},{9,8},{10,11... | collective-permute-start | bytes 3194888 | tf_op jit(solution)/shard_map/ppermute | solution.py:378
  12.1 8.6 %copy-start.2 = (bf16[2,1024,512]{2,1,0:T(8,128)(2,1)S(1)}, bf16[2,1024,512]{2,1,0:T(8,128)(2,1)}, u32[]{:S(2)}) copy-start(bf16[2,1024,512]{2,1,0:T(8,128)(2,1)} %refs_7_.5) | copy-start | bytes 6291460
  12.1 8.6 %copy-start.8 = (f32[2,512]{1,0:T(2,128)S(1)}, f32[2,512]{1,0:T(2,128)}, u32[]{:S(2)}) copy-start(f32[2,512]{1,0:T(2,128)} %refs_3_.8) | copy-start | bytes 12292
  12.1 8.6 %copy-start.9 = (f32[2,512]{1,0:T(2,128)S(1)}, f32[2,512]{1,0:T(2,128)}, u32[]{:S(2)}) copy-start(f32[2,512]{1,0:T(2,128)} %refs_4_.8) | copy-start | bytes 12292
  16.1 16.4 %copy-start.5 = (f32[2,512]{1,0:T(2,128)S(1)}, f32[2,512]{1,0:T(2,128)}, u32[]{:S(2)}) copy-start(f32[2,512]{1,0:T(2,128)} %refs_3_.9) | copy-start | bytes 12292
  16.1 16.3 %copy-start.6 = (f32[2,512]{1,0:T(2,128)S(1)}, f32[2,512]{1,0:T(2,128)}, u32[]{:S(2)}) copy-start(f32[2,512]{1,0:T(2,128)} %refs_4_.9) | copy-start | bytes 12292
  16.1 9.3 %collective-permute-start.4 = (bf16[528,256]{1,0:T(8,128)(2,1)S(1)}, bf16[528,256]{1,0:T(8,128)(2,1)S(1)}, u32[]{:S(2)}, u32[]{:S(2)}) collective-permute-start(bf16[528,256]{1,0:T(8,128)(2,1)S(1)} %collective-permute-done.2.refs_0_), channel_id=1, source_target_pairs={{0,8},{2,10},{4,12},{6,14},{8,0},{10,2},{12,4},{14,6},{16,24},{18,... | collective-permute-start | bytes 811016 | tf_op jit(solution)/shard_map/ppermute | solution.py:382
  19.2 11.6 %collective-permute-start.5 = (bf16[256,512]{1,0:T(8,128)(2,1)S(1)}, bf16[256,512]{1,0:T(8,128)(2,1)S(1)}, u32[]{:S(2)}, u32[]{:S(2)}) collective-permute-start(bf16[256,512]{1,0:T(8,128)(2,1)S(1)} %collective-permute-done.3.refs_1_), channel_id=1, source_target_pairs={{0,8},{2,10},{4,12},{6,14},{8,0},{10,2},{12,4},{14,6},{16,24},{18,... | collective-permute-start | bytes 786440 | tf_op jit(solution)/shard_map/ppermute | solution.py:382
  19.7 11.6 %collective-permute-start.6 = (bf16[528,256]{1,0:T(8,128)(2,1)S(1)}, bf16[528,256]{1,0:T(8,128)(2,1)S(1)}, u32[]{:S(2)}, u32[]{:S(2)}) collective-permute-start(bf16[528,256]{1,0:T(8,128)(2,1)S(1)} %collective-permute-done.2.refs_0_), channel_id=1, source_target_pairs={{0,2},{2,0},{4,6},{6,4},{8,10},{10,8},{12,14},{14,12},{16,18},{18,... | collective-permute-start | bytes 811016 | tf_op jit(solution)/shard_map/ppermute | solution.py:369
  25.4 7.0 %collective-permute-start.8 = (bf16[528,256]{1,0:T(8,128)(2,1)S(1)}, bf16[528,256]{1,0:T(8,128)(2,1)S(1)}, u32[]{:S(2)}, u32[]{:S(2)}) collective-permute-start(bf16[528,256]{1,0:T(8,128)(2,1)S(1)} %collective-permute-done.4.refs_2_), channel_id=1, source_target_pairs={{0,2},{2,0},{4,6},{6,4},{8,10},{10,8},{12,14},{14,12},{16,18},{18,... | collective-permute-start | bytes 811016 | tf_op jit(solution)/shard_map/ppermute | solution.py:369
  25.9 5.3 %collective-permute-start.7 = (bf16[256,512]{1,0:T(8,128)(2,1)S(1)}, bf16[256,512]{1,0:T(8,128)(2,1)S(1)}, u32[]{:S(2)}, u32[]{:S(2)}) collective-permute-start(bf16[256,512]{1,0:T(8,128)(2,1)S(1)} %collective-permute-done.3.refs_1_), channel_id=1, source_target_pairs={{0,2},{2,0},{4,6},{6,4},{8,10},{10,8},{12,14},{14,12},{16,18},{18,... | collective-permute-start | bytes 786440 | tf_op jit(solution)/shard_map/ppermute | solution.py:369
  30.9 1.6 %collective-permute-start.9 = (bf16[256,512]{1,0:T(8,128)(2,1)S(1)}, bf16[256,512]{1,0:T(8,128)(2,1)S(1)}, u32[]{:S(2)}, u32[]{:S(2)}) collective-permute-start(bf16[256,512]{1,0:T(8,128)(2,1)S(1)} %collective-permute-done.5.refs_3_), channel_id=1, source_target_pairs={{0,2},{2,0},{4,6},{6,4},{8,10},{10,8},{12,14},{14,12},{16,18},{18,... | collective-permute-start | bytes 786440 | tf_op jit(solution)/shard_map/ppermute | solution.py:369
  35.6 3.4 %collective-permute-start.11 = (bf16[3,136,512]{2,1,0:T(8,128)(2,1)S(1)}, bf16[3,136,512]{2,1,0:T(8,128)(2,1)S(1)}, u32[]{:S(2)}, u32[]{:S(2)}) collective-permute-start(bf16[3,136,512]{2,1,0:T(8,128)(2,1)S(1)} %get-tuple-element.33), channel_id=1, source_target_pairs={{0,2},{2,0},{4,6},{6,4},{8,10},{10,8},{12,14},{14,12},{16,18},{18,... | collective-permute-start | bytes 1253384 | tf_op jit(solution)/shard_map/ppermute | solution.py:369
  36.0 13.8 %collective-permute-start.10 = (bf16[3,136,512]{2,1,0:T(8,128)(2,1)S(1)}, bf16[3,136,512]{2,1,0:T(8,128)(2,1)S(1)}, u32[]{:S(2)}, u32[]{:S(2)}) collective-permute-start(bf16[3,136,512]{2,1,0:T(8,128)(2,1)S(1)} %get-tuple-element.31), channel_id=1, source_target_pairs={{2,4},{6,8},{10,12},{14,16},{18,20},{22,24},{26,28},{4,2},{8,6},{1... | collective-permute-start | bytes 1253384 | tf_op jit(solution)/shard_map/ppermute | solution.py:374
  42.5 9.5 %collective-permute-start.13 = (bf16[1040,512]{1,0:T(8,128)(2,1)S(1)}, bf16[1040,512]{1,0:T(8,128)(2,1)S(1)}, u32[]{:S(2)}, u32[]{:S(2)}) collective-permute-start(bf16[1040,512]{1,0:T(8,128)(2,1)S(1)} %collective-permute-done.12.refs_0_), channel_id=1, source_target_pairs={{0,2},{2,0},{4,6},{6,4},{8,10},{10,8},{12,14},{14,12},{16,18},{18,... | collective-permute-start | bytes 3194888 | tf_op jit(solution)/shard_map/ppermute | solution.py:369
  53.7 8.8 %collective-permute-start.14 = (bf16[2,128,512]{2,1,0:T(8,128)(2,1)S(1)}, bf16[2,128,512]{2,1,0:T(8,128)(2,1)S(1)}, u32[]{:S(2)}, u32[]{:S(2)}) collective-permute-start(bf16[2,128,512]{2,1,0:T(8,128)(2,1)S(1)} %more.4), channel_id=1, source_target_pairs={{0,1},{1,0},{2,3},{3,2},{4,5},{5,4},{6,7},{7,6},{8,9},{9,8},{10,11... | collective-permute-start | bytes 786440 | tf_op jit(solution)/shard_map/ppermute | solution.py:378
  58.9 6.9 %collective-permute-start.15 = (bf16[2,128,512]{2,1,0:T(8,128)(2,1)S(1)}, bf16[2,128,512]{2,1,0:T(8,128)(2,1)S(1)}, u32[]{:S(2)}, u32[]{:S(2)}) collective-permute-start(bf16[2,128,512]{2,1,0:T(8,128)(2,1)S(1)} %more.5), channel_id=1, source_target_pairs={{0,1},{1,0},{2,3},{3,2},{4,5},{5,4},{6,7},{7,6},{8,9},{9,8},{10,11... | collective-permute-start | bytes 786440 | tf_op jit(solution)/shard_map/ppermute | solution.py:378
  (4 other events, 8.7 us)

commit v3 on v2

--- a/solution.py
+++ b/solution.py
@@ -20,7 +20,6 @@
     1.8056156531812635e-09,
 )
 VMEM = pl.BlockSpec(memory_space=pltpu.VMEM)
-SMEM = pl.BlockSpec(memory_space=pltpu.SMEM)
 HBM = pl.BlockSpec(memory_space=pltpu.HBM)
 PARAMS = pltpu.CompilerParams(vmem_limit_bytes=20 * 1024 * 1024)
 COPIES = pltpu.CompilerParams(vmem_limit_bytes=60 * 1024 * 1024)
@@ -37,6 +36,36 @@
 
 def tile_of(width):
     return next(s for s in (48, 32, 16) if width % s == 0)
+
+
+class Layout:
+    def __init__(self, features, kernels):
+        self.blocks, self.reach = kernels.shape[0], kernels.shape[1] // 2
+        self.rows, self.columns, self.channels = features.shape
+        self.number = lax.axis_size("hid")
+        self.width = self.columns // self.number
+
+    def size(self, reach, unit):
+        extra = -(-reach // unit) * unit
+        return extra, min(self.columns, self.width + (1 if self.number == 2 else 2) * extra)
+
+    def start(self, reach, unit):
+        extra, size = self.size(reach, unit)
+        return jnp.clip(lax.axis_index("hid") * self.width - extra, 0, self.columns - size)
+
+    def window(self, b):
+        return self.reach * (self.blocks - 1 - b), MARGIN
+
+    def edge(self, b):
+        return self.reach * (self.blocks - b), 8 if b else MARGIN
+
+    def place(self, b):
+        to, halo = self.start(*self.window(b)), self.start(*self.edge(b))
+        start = self.start(*self.window(b - 1)) if b else 0
+        later = self.start(*self.edge(b + 1))
+        row = lax.axis_index("row")
+        odd, parity = lax.rem(row, 2), lax.rem(lax.div(row, 4), 2)
+        return to - start, halo - to + MARGIN, odd, parity, int(b == 0), later - to, halo
 
 
 def row_of(place, d, rows):
@@ -63,7 +92,8 @@
     return sums
 
 
-def own_kernel(b, place, own, near, taps, bias, out, wide):
+def own_kernel(b, layout, own, near, taps, bias, out, wide):
+    place = layout.place(b)
     groups, rows, width, _ = out.shape
     reach = near.shape[0]
     fill_own(place, own, wide, rows)
@@ -163,7 +193,8 @@
             total[...] = y if before is None else before[...] + y
 
 
-def rest_kernel(b, chosen, number, place, *refs):
+def rest_kernel(b, layout, chosen, number, *refs):
+    place = layout.place(b)
     far, refs = refs[:number], refs[number:]
     before, taps, gain, shift, up, b_up, down, normed, total, conv, wide = refs
     add_far(b, place, chosen, far, before, taps, conv, wide)
@@ -171,7 +202,8 @@
     project(normed, up.at[b], b_up.at[b : b + 1], down.at[b], total)
 
 
-def more_kernel(b, chosen, kind, number, final, place, x, before, *refs):
+def more_kernel(b, layout, chosen, kind, number, final, x, before, *refs):
+    place = layout.place(b)
     channels = x.shape[1]
     refs = list(refs)
     parts = [refs.pop(0) for _ in range(number)]
@@ -217,101 +249,127 @@
             near[d - (rows - reach)] = s
 
 
-def take(b, place, weights, parts, up, down, bias, terms):
-    w_up, b_up, w_down = weights
+def take(b, place, weights, parts, up, down):
+    w_up, _, w_down = weights
     hidden = w_up.shape[2] // parts
     at = place[2] * (w_up.shape[2] // 2) + (place[3] * hidden if parts == 4 else 0)
     at = pl.ds(pl.multiple_of(at, hidden), hidden)
-    value = b_up[b : b + 1, at]
+    return at, [(w_up.at[b, :, at], up), (w_down.at[b, at, :], down)]
+
+
+def in_two_terms(value, terms):
     high = value.astype(jnp.bfloat16).astype(jnp.float32)
     low = (value - high).astype(jnp.bfloat16).astype(jnp.float32)
-    row = lax.broadcasted_iota(jnp.int32, (MARGIN, hidden), 0)
+    row = lax.broadcasted_iota(jnp.int32, terms.shape, 0)
     terms[...] = jnp.where(row == 0, high, jnp.where(row == 1, low, 0.0)).astype(terms.dtype)
-    return [(w_up.at[b, :, at], up), (w_down.at[b, at, :], down), (terms, bias)]
-
-
-def carry(copies, sems):
+
+
+def start(copies, sems):
     copies = [pltpu.make_async_copy(*copy, sems.at[n]) for n, copy in enumerate(copies)]
     for copy in copies:
         copy.start()
+    return copies
+
+
+def prepare_kernel(layout, features, *refs):
+    place = layout.place(0)
+    weights, refs = refs[: 3 if len(refs) > 5 else 0], refs[3 if len(refs) > 5 else 0 :]
+    *refs, sems = refs
+    if weights:
+        *refs, bias, terms = refs
+    outs, stages = list(refs[: len(refs) // 2]), list(refs[len(refs) // 2 :])
+    reach, size, _ = outs[0].shape
+    last = layout.rows - reach
+    at = pl.ds(pl.multiple_of(place[6], MARGIN), size)
+    sources = [
+        features.at[pl.ds(place[2] * last, reach), at],
+        features.at[pl.ds((1 - place[2]) * last, reach), at],
+    ]
+    if weights:
+        channels = layout.channels
+        hidden, taken = take(0, place, weights, 4, stages[2].at[:channels], stages[3])
+        first = start([*taken, (weights[1], bias)], sems.at[0])
+        rest = start(list(zip(sources, stages)), sems.at[1])
+        first[2].wait()
+        in_two_terms(bias[0:1, hidden], terms)
+        first[0].wait()
+        legs = [(stages[2].at[:channels], outs[2].at[:channels]), (terms, outs[2].at[channels:])]
+        legs = start(legs, sems.at[2])
+        first[1].wait()
+        legs += start([(stages[3], outs[3])], sems.at[3])
+    else:
+        rest = start(list(zip(sources, stages)), sems.at[1])
+        legs = []
+    for n, copy in enumerate(rest):
+        copy.wait()
+        legs += start([(stages[n], outs[n])], sems.at[4 + n])
+    for copy in legs:
+        copy.wait()
+
+
+def pack_kernel(b, layout, w_up, b_up, w_down, out, terms, sems):
+    channels, last = layout.channels, out.shape[0] - MARGIN
+    outs = out.at[:channels], out.at[channels:last]
+    hidden, copies = take(b, layout.place(b), (w_up, b_up, w_down), 2, *outs)
+    copies = start(copies, sems.at[0])
+    in_two_terms(b_up[b : b + 1, hidden], terms)
+    copies += start([(terms, out.at[last:])], sems.at[1])
     for copy in copies:
         copy.wait()
 
 
-def prepare_kernel(place, features, *refs):
-    weights, refs = refs[: 3 if len(refs) > 3 else 0], refs[3 if len(refs) > 3 else 0 :]
-    outer, inner, *refs = refs
-    reach, size, _ = outer.shape
-    last = features.shape[0] - reach
-    at = pl.ds(pl.multiple_of(place[6], MARGIN), size)
-    copies = [
-        (features.at[pl.ds(place[2] * last, reach), at], outer),
-        (features.at[pl.ds((1 - place[2]) * last, reach), at], inner),
-    ]
-    if weights:
-        up, down, terms, _ = refs
-        channels = features.shape[2]
-        copies += take(0, place, weights, 4, up.at[:channels], down, up.at[channels:], terms)
-    carry(copies, refs[-1])
-
-
-def pack_kernel(b, place, w_up, b_up, w_down, out, terms, sems):
-    channels, last = w_up.shape[1], out.shape[0] - MARGIN
-    outs = out.at[:channels], out.at[channels:last], out.at[last:]
-    carry(take(b, place, (w_up, b_up, w_down), 2, *outs, terms), sems)
-
-
 def cost(flops):
     return pl.CostEstimate(flops=flops, bytes_accessed=0, transcendentals=0)
 
 
-def prepare(place, features, reach, size, weights=()):
-    channels = features.shape[2]
-    shapes = [jax.ShapeDtypeStruct((reach, size, channels), jnp.bfloat16)] * 2
-    scratch = [pltpu.SemaphoreType.DMA((5,))]
+def prepare(layout, features, weights=()):
+    _, size = layout.size(*layout.edge(0))
+    channels = layout.channels
+    shapes = [(layout.reach, size, channels)] * 2
+    scratch = [pltpu.SemaphoreType.DMA((6, 3))]
     if weights:
         hidden = weights[0].shape[2] // 4
-        sizes = [(channels + MARGIN, hidden), (hidden, channels)]
-        shapes += [jax.ShapeDtypeStruct(size, jnp.bfloat16) for size in sizes]
+        shapes += [(channels + MARGIN, hidden), (hidden, channels)]
         scratch.insert(0, pltpu.VMEM((MARGIN, hidden), jnp.bfloat16))
+        scratch.insert(0, pltpu.VMEM(weights[1].shape, jnp.float32))
     return pl.pallas_call(
-        prepare_kernel,
-        out_shape=shapes,
-        in_specs=[SMEM, HBM] + ([HBM, VMEM, HBM] if weights else []),
-        out_specs=[VMEM] * len(shapes),
-        scratch_shapes=scratch,
+        functools.partial(prepare_kernel, layout),
+        out_shape=[jax.ShapeDtypeStruct(shape, jnp.bfloat16) for shape in shapes],
+        in_specs=[HBM] + [HBM] * len(weights),
+        out_specs=[HBM] * len(shapes),
+        scratch_shapes=[pltpu.VMEM(shape, jnp.bfloat16) for shape in shapes] + scratch,
         compiler_params=COPIES,
         cost_estimate=cost(1),
         name="prepare",
-    )(place, features, *weights)
-
-
-def pack(b, place, weights):
+    )(features, *weights)
+
+
+def pack(b, layout, weights):
     _, channels, hidden = weights[0].shape
     hidden //= 2
     shape = (channels + hidden + MARGIN, channels)
     return pl.pallas_call(
-        functools.partial(pack_kernel, b),
+        functools.partial(pack_kernel, b, layout),
         out_shape=jax.ShapeDtypeStruct(shape, jnp.bfloat16),
-        in_specs=[SMEM, HBM, VMEM, HBM],
+        in_specs=[HBM, VMEM, HBM],
         out_specs=VMEM,
         scratch_shapes=[
             pltpu.VMEM((MARGIN, hidden), jnp.bfloat16),
-            pltpu.SemaphoreType.DMA((3,)),
+            pltpu.SemaphoreType.DMA((2, 2)),
         ],
         compiler_params=PARAMS,
         cost_estimate=cost(1),
         name="pack",
-    )(place, *weights)
-
-
-def conv_own(b, place, own, near, width, taps, bias):
+    )(*weights)
+
+
+def conv_own(b, layout, own, near, width, taps, bias):
     rows, _, channels = own.shape
     groups, reach = channels // LANES, near.shape[0]
     return pl.pallas_call(
-        functools.partial(own_kernel, b),
+        functools.partial(own_kernel, b, layout),
         out_shape=jax.ShapeDtypeStruct((groups, rows, width, LANES), jnp.float32),
-        in_specs=[SMEM] + [VMEM] * 4,
+        in_specs=[VMEM] * 4,
         out_specs=VMEM,
         scratch_shapes=[
             pltpu.VMEM((groups, rows + reach, width + 2 * MARGIN, LANES), jnp.float32)
@@ -319,21 +377,21 @@
         compiler_params=PARAMS,
         cost_estimate=cost(1),
         name="conv_own",
-    )(place, own, near, taps, bias)
-
-
-def conv_rest(b, chosen, place, far, before, taps, gain, shift, up, b_up, down):
+    )(own, near, taps, bias)
+
+
+def conv_rest(b, layout, chosen, far, before, taps, gain, shift, up, b_up, down):
     groups, _, width, _ = before.shape
     channels, reach = groups * LANES, taps.shape[1] // 2
     positions = len(chosen) * width
-    args = [place, *far, before, taps, gain, shift, up, b_up, down]
+    args = [*far, before, taps, gain, shift, up, b_up, down]
     return pl.pallas_call(
-        functools.partial(rest_kernel, b, chosen, len(far)),
+        functools.partial(rest_kernel, b, layout, chosen, len(far)),
         out_shape=(
             jax.ShapeDtypeStruct((positions, channels), jnp.bfloat16),
             jax.ShapeDtypeStruct((positions, channels), jnp.float32),
         ),
-        in_specs=[SMEM] + [VMEM] * (len(args) - 1),
+        in_specs=[VMEM] * len(args),
         out_specs=(VMEM, VMEM),
         scratch_shapes=[
             pltpu.VMEM((groups, len(chosen), width, LANES), jnp.float32),
@@ -345,18 +403,18 @@
     )(*args)
 
 
-def more(b, chosen, place, x, before, kind, parts, state, b_down, scale, halo_shape):
+def more(b, layout, chosen, x, before, kind, parts, state, b_down, scale, halo_shape):
     positions, channels = x.shape
     final = halo_shape is None
-    args = [place, x, before, *parts, state, b_down, scale]
+    args = [x, before, *parts, state, b_down, scale]
     shapes = [(len(chosen), positions // len(chosen), channels)]
     if not final:
         reach, size = halo_shape
         shapes += [(reach, size, channels)] * 2
     return pl.pallas_call(
-        functools.partial(more_kernel, b, chosen, kind, len(parts), final),
+        functools.partial(more_kernel, b, layout, chosen, kind, len(parts), final),
         out_shape=[jax.ShapeDtypeStruct(shape, jnp.bfloat16) for shape in shapes],
-        in_specs=[SMEM] + [VMEM] * (len(args) - 1),
+        in_specs=[VMEM] * len(args),
         out_specs=[VMEM] * len(shapes),
         scratch_shapes=[pltpu.VMEM((positions, channels), jnp.float32)],
         compiler_params=PARAMS,
@@ -394,56 +452,34 @@
 
 
 def shards(features, dw_weight, dw_bias, ln_gain, ln_bias, w_up, b_up, w_down, b_down, layer_scale):
-    blocks, reach = dw_weight.shape[0], dw_weight.shape[1] // 2
-    rows, columns, channels = features.shape
-    number, me = lax.axis_size("hid"), lax.axis_index("hid")
-    row, count = lax.axis_index("row"), lax.axis_size("row")
-    odd, parity = lax.rem(row, 2), lax.rem(row // 4, 2)
-    width = columns // number
-    pairs = number == 2 and w_up.shape[2] == 2 * channels and count % 8 == 0
-
-    def window(reach, unit):
-        extra = -(-reach // unit) * unit
-        size = min(columns, width + (extra if number == 2 else 2 * extra))
-        return jnp.clip(me * width - extra, 0, columns - size), size
-
-    def edge(b):
-        return window(reach * (blocks - b), 8 if b else MARGIN)
-
-    def place_of(b):
-        to, _ = window(reach * (blocks - 1 - b), MARGIN)
-        start = window(reach * (blocks - b), MARGIN)[0] if b else 0
-        halo, _ = edge(b)
-        later, _ = edge(b + 1)
-        values = [to - start, halo - to + MARGIN, odd, parity, int(b == 0), later - to, halo]
-        return jnp.stack([jnp.int32(v) for v in values])
-
-    places = [place_of(b) for b in range(blocks)]
+    layout = Layout(features, dw_weight)
+    blocks, rows, number = layout.blocks, layout.rows, layout.number
+    me, row, count = lax.axis_index("hid"), lax.axis_index("row"), lax.axis_size("row")
+    odd = lax.rem(row, 2)
+    pairs = number == 2 and w_up.shape[2] == 2 * layout.channels and count % 8 == 0
     everything = tuple(range(rows))
     weights = (w_up, b_up, w_down)
 
-    outer, inner, *first = prepare(
-        places[0], features, reach, edge(0)[1], weights if pairs else ()
-    )
+    outer, inner, *packed = prepare(layout, features, weights if pairs else ())
     far, near = [across(outer)], within(inner)
     state = features
     if pairs:
-        up, down = swap_hid(first[0]), swap_hid(first[1])
+        up, down = swap_hid(packed[0]), swap_hid(packed[1])
     for b in range(blocks):
-        place, final = places[b], b == blocks - 1
-        _, size = window(reach * (blocks - 1 - b), MARGIN)
-        before = conv_own(b, place, state, near, size, dw_weight, dw_bias)
+        final = b == blocks - 1
+        _, size = layout.size(*layout.window(b))
+        before = conv_own(b, layout, state, near, size, dw_weight, dw_bias)
         rest = lambda chosen, far, before: conv_rest(
-            b, chosen, place, far, before, dw_weight, ln_gain, ln_bias, *weights
+            b, layout, chosen, far, before, dw_weight, ln_gain, ln_bias, *weights
         )
         add = lambda chosen, work, parts: more(
-            b, chosen, place, *work, kind, parts, state, b_down, layer_scale,
-            None if final else (reach, edge(b + 1)[1]),
+            b, layout, chosen, *work, kind, parts, state, b_down, layer_scale,
+            None if final else (layout.reach, layout.size(*layout.edge(b + 1))[1]),
         )
         if pairs and not final:
-            later = swap_hid(pack(b + 1, places[b + 1], weights))
+            later = swap_hid(pack(b + 1, layout, weights))
         if pairs and b == 0:
-            up = after(up, before)
+            down = after(down, before)
             up_other, down_other = swap_row(up, 4), swap_row(down, 4)
         elif pairs:
             joined = after(joined, before)
@@ -463,14 +499,13 @@
             if pairs:
                 joined = later
     inner, outer = (r[0] for r in results)
-    if number == 1:
-        columns_of = lambda a: a
-    elif number == 2:
+    if number == 2:
         def columns_of(a):
             other = swap_hid(a)
-            return jnp.concatenate(
-                [jnp.where(me == 0, a, other), jnp.where(me == 0, other, a)], axis=1
-            )
+            left, right = jnp.where(me == 0, a, other), jnp.where(me == 0, other, a)
+            return jnp.concatenate([left, right], axis=1)
+    elif number == 1:
+        columns_of = lambda a: a
     else:
         columns_of = lambda a: lax.all_gather(a, "hid", axis=1, tiled=True)
     inner, outer = columns_of(inner), columns_of(outer)

time: 67.3 us -> 61 us (0.906)
  Pallas kernels: 27.5 us -> 21.7 us
  starting transfers between devices: 14.3 us -> 11.4 us
  waiting for transfers between devices: 21.2 us -> 23.9 us
  local copies, waits for them, and re-layouts: 2.44 us -> 1.68 us
    ppermute x5, waiting for transfers between devices: 7.96 us -> 15.1 us  [swap_hid(): return lax.ppermute(array, 'hid', [(0, 1), (1, 0)])]
    pallas_call x10, Pallas kernels: 27.5 us -> 21.7 us  [the longest x3 7.8 us: conv_rest(): pl.pallas_call(functools.partial(rest_kernel, b, layout, chosen, len(far)...]
    ppermute x2, waiting for transfers between devices: 4.9 us -> 2.03 us  [swap_row(): lax.ppermute(array, 'row', [(i, i ^ bit) for i in range(lax.axis_size('ro...]
    ppermute x2, waiting for transfers between devices: 7.15 us -> 5.26 us  [across(): lax.ppermute(array, 'row', pairs + [(target, source) for source, target i...]
    ppermute x7, starting transfers between devices: 2.7 us -> 0.85 us  [within(): lax.ppermute(array, 'row', [(i, i ^ 1) for i in range(lax.axis_size('row'...]
    ppermute x2, starting transfers between devices: 4.86 us -> 4 us  [across(): lax.ppermute(array, 'row', pairs + [(target, source) for source, target i...]
    another operation x2 -> x0, local copies, waits for them, and re-layouts: 0.75 us -> none  [place_of(): return jnp.stack([jnp.int32(v) for v in values])]
    unnamed x25 -> x23, local copies, waits for them, and re-layouts: 1.69 us -> 1.68 us
  transfers between devices with their start and end apart: 16 -> 16, of which waited for: 7 -> 9; matrix products, arithmetic and copies ran while one was open for 0% -> 0% of each run, Pallas kernels for 34% -> 30%
where the time goes in v3:
time: 61 us; the launch traced here: 60.4 us
  waiting for transfers between devices  23.9 us (39%)
  Pallas kernels  21.7 us (36%)
  starting transfers between devices  11.4 us (19%)
  local copies, waits for them, and re-layouts  1.68 us (3%)
  other arithmetic  1.34 us (2%)
    ppermute x5, waiting for transfers between devices, swap_hid(): return lax.ppermute(array, 'hid', [(0, 1), (1, 0)])  15.1 us
    pallas_call x3, Pallas kernels, conv_rest(): pl.pallas_call(functools.partial(rest_kernel, b, layout, chosen, len(far)...  7.8 us
    pallas_call x2, Pallas kernels, conv_own(): pl.pallas_call(functools.partial(own_kernel, b, layout), out_shape=jax.Sh...  6.17 us
    ppermute x5, starting transfers between devices, swap_hid(): return lax.ppermute(array, 'hid', [(0, 1), (1, 0)])  5.8 us
    ppermute x2, waiting for transfers between devices, across(): lax.ppermute(array, 'row', pairs + [(target, source) for source, target i...  5.26 us
    pallas_call x3, Pallas kernels, more(): pl.pallas_call(functools.partial(more_kernel, b, layout, chosen, kind, le...  5.12 us
    ppermute x2, starting transfers between devices, across(): lax.ppermute(array, 'row', pairs + [(target, source) for source, target i...  4 us
    pallas_call x1, Pallas kernels, prepare(): pl.pallas_call(functools.partial(prepare_kernel, layout), out_shape=[jax....  2.46 us
  transfers between devices with their start and end apart: 16, of which 9 were waited for; matrix products, arithmetic and copies ran while one was open for 0% of the time, Pallas kernels for 30%

profile of v3, /device:TPU:12, one launch (start us, length us, event | category | flops | bytes accessed | tf_op | source)
XLA Modules:
  0.0 60.4 jit_solution(2459100080361457913)
XLA Ops:
  0.0 2.5 %prepare.1 = (bf16[3,144,512]{2,1,0:T(8,128)(2,1)}, bf16[3,144,512]{2,1,0:T(8,128)(2,1)}, bf16[528,256]{1,0:T(8,128)(2,1)}, bf16[256,512]{1,0:T(8,128)(2,1)}) custom-call(bf16[4,256,512]{2,1,0:T(8,128)(2,1)} %refs_8_.1, bf16[2,512,1024]{2,1,0:T(8,128)(2,1)} %refs_5_.5, f32[2,1024]{1,0:T(2,128)} %refs_6_.5, bf16[2,1024,512]{2,1,0:T(8,128)(2,1)} %refs_7_.5), custom_call_target="tpu_custom_call" | custom-call | flops 1 | tf_op jit(solution)/shard_map/prepare/pallas_call | solution.py:335
  2.6 1.6 %collective-permute-start.2 = (bf16[528,256]{1,0:T(8,128)(2,1)}, bf16[528,256]{1,0:T(8,128)(2,1)S(1)}, u32[]{:S(2)}, u32[]{:S(2)}) collective-permute-start(bf16[528,256]{1,0:T(8,128)(2,1)} %get-tuple-element.26), channel_id=1, source_target_pairs={{0,1},{1,0},{2,3},{3,2},{4,5},{5,4},{6,7},{7,6},{8,9},{9,8},{10,11... | collective-permute-start | bytes 811016 | tf_op jit(solution)/shard_map/ppermute | solution.py:436
  4.6 1.9 %collective-permute-start = (bf16[3,144,512]{2,1,0:T(8,128)(2,1)}, bf16[3,144,512]{2,1,0:T(8,128)(2,1)S(1)}, u32[]{:S(2)}, u32[]{:S(2)}) collective-permute-start(bf16[3,144,512]{2,1,0:T(8,128)(2,1)} %get-tuple-element.22), channel_id=1, source_target_pairs={{2,4},{6,8},{10,12},{14,16},{18,20},{22,24},{26,28},{4,2},{8,6},{1... | collective-permute-start | bytes 1327112 | tf_op jit(solution)/shard_map/ppermute | solution.py:432
  6.6 1.6 %copy-done.1 = bf16[2,1024,512]{2,1,0:T(8,128)(2,1)S(1)} copy-done((bf16[2,1024,512]{2,1,0:T(8,128)(2,1)S(1)}, bf16[2,1024,512]{2,1,0:T(8,128)(2,1)}, u32[]{:S(2)}) %copy-start.1) | copy-done | bytes 2097176
  8.4 1.6 %collective-permute-start.12 = (bf16[1040,512]{1,0:T(8,128)(2,1)S(1)}, bf16[1040,512]{1,0:T(8,128)(2,1)S(1)}, u32[]{:S(2)}, u32[]{:S(2)}) collective-permute-start(bf16[1040,512]{1,0:T(8,128)(2,1)S(1)} %pack.1), channel_id=1, source_target_pairs={{0,1},{1,0},{2,3},{3,2},{4,5},{5,4},{6,7},{7,6},{8,9},{9,8},{10,11... | collective-permute-start | bytes 3194888 | tf_op jit(solution)/shard_map/ppermute | solution.py:436
  9.9 2.2 %collective-permute-done.2.refs_0_ = bf16[528,256]{1,0:T(8,128)(2,1)S(1)} collective-permute-done((bf16[528,256]{1,0:T(8,128)(2,1)}, bf16[528,256]{1,0:T(8,128)(2,1)S(1)}, u32[]{:S(2)}, u32[]{:S(2)}) %collective-permute-start.2) | collective-permute-done | bytes 270368 | tf_op jit(solution)/shard_map/ppermute | solution.py:436
  12.6 3.3 %conv_own.2.refs_1_ = f32[4,4,144,128]{3,2,1,0:T(8,128)S(1)} custom-call(bf16[4,256,512]{2,1,0:T(8,128)(2,1)S(1)} %copy-done.3, bf16[3,144,512]{2,1,0:T(8,128)(2,1)S(1)} %collective-permute-done.1.near, f32[2,7,7,512]{3,2,1,0:T(8,128)S(1)} %copy.11.taps.refs_2_, f32[2,512]{1,0:T(2,128)S(1)} %copy-done.7), custom_call_target="tpu_custom_call" | custom-call | flops 1 | tf_op jit(solution)/shard_map/conv_own/pallas_call | solution.py:369
  15.9 1.8 %collective-permute-done.3.refs_1_ = bf16[256,512]{1,0:T(8,128)(2,1)S(1)} collective-permute-done((bf16[256,512]{1,0:T(8,128)(2,1)}, bf16[256,512]{1,0:T(8,128)(2,1)S(1)}, u32[]{:S(2)}, u32[]{:S(2)}) %collective-permute-start.3) | collective-permute-done | bytes 262176 | tf_op jit(solution)/shard_map/ppermute | solution.py:436
  18.1 1.1 %collective-permute-done.refs_0_ = bf16[3,144,512]{2,1,0:T(8,128)(2,1)S(1)} collective-permute-done((bf16[3,144,512]{2,1,0:T(8,128)(2,1)}, bf16[3,144,512]{2,1,0:T(8,128)(2,1)S(1)}, u32[]{:S(2)}, u32[]{:S(2)}) %collective-permute-start) | collective-permute-done | bytes 442400 | tf_op jit(solution)/shard_map/ppermute | solution.py:432
  19.2 4.0 %conv_rest.3 = (bf16[576,512]{1,0:T(8,128)(2,1)S(1)}, f32[576,512]{1,0:T(8,128)S(1)}) custom-call(bf16[3,144,512]{2,1,0:T(8,128)(2,1)S(1)} %collective-permute-done.refs_0_, f32[4,4,144,128]{3,2,1,0:T(8,128)S(1)} %conv_own.2.refs_1_, f32[2,7,7,512]{3,2,1,0:T(8,128)S(1)} %copy.11.taps.refs_2_, f32[2,512]{1,0:T(2,128)S(1)} %copy-done.8, ...), custom_call_target="tpu_custom_call" | custom-call | flops 1 | tf_op jit(solution)/shard_map/conv_rest/pallas_call | solution.py:388
  23.8 2.0 %collective-permute-done.5.refs_3_ = bf16[256,512]{1,0:T(8,128)(2,1)S(1)} collective-permute-done((bf16[256,512]{1,0:T(8,128)(2,1)S(1)}, bf16[256,512]{1,0:T(8,128)(2,1)S(1)}, u32[]{:S(2)}, u32[]{:S(2)}) %collective-permute-start.5) | collective-permute-done | bytes 262176 | tf_op jit(solution)/shard_map/ppermute | solution.py:440
  25.9 1.5 %collective-permute-done.9.refs_7_ = bf16[256,512]{1,0:T(8,128)(2,1)S(1)} collective-permute-done((bf16[256,512]{1,0:T(8,128)(2,1)S(1)}, bf16[256,512]{1,0:T(8,128)(2,1)S(1)}, u32[]{:S(2)}, u32[]{:S(2)}) %collective-permute-start.9) | collective-permute-done | bytes 262176 | tf_op jit(solution)/shard_map/ppermute | solution.py:427
  27.4 2.8 %more.3 = (bf16[4,144,512]{2,1,0:T(8,128)(2,1)S(1)}, bf16[3,136,512]{2,1,0:T(8,128)(2,1)S(1)}, bf16[3,136,512]{2,1,0:T(8,128)(2,1)S(1)}) custom-call(bf16[576,512]{1,0:T(8,128)(2,1)S(1)} %get-tuple-element.24.x, f32[576,512]{1,0:T(8,128)S(1)} %get-tuple-element.25.before, bf16[528,256]{1,0:T(8,128)(2,1)S(1)} %collective-permute-done.2.refs_0_, ...), custom_call_target="tpu_custom_call" | custom-call | flops 1 | tf_op jit(solution)/shard_map/more/pallas_call | solution.py:414
  30.5 2.1 %collective-permute-start.10 = (bf16[3,136,512]{2,1,0:T(8,128)(2,1)S(1)}, bf16[3,136,512]{2,1,0:T(8,128)(2,1)S(1)}, u32[]{:S(2)}, u32[]{:S(2)}) collective-permute-start(bf16[3,136,512]{2,1,0:T(8,128)(2,1)S(1)} %get-tuple-element.31), channel_id=1, source_target_pairs={{2,4},{6,8},{10,12},{14,16},{18,20},{22,24},{26,28},{4,2},{8,6},{1... | collective-permute-start | bytes 1253384 | tf_op jit(solution)/shard_map/ppermute | solution.py:432
  32.6 2.9 %conv_own.3.refs_1_ = f32[4,4,128,128]{3,2,1,0:T(8,128)S(1)} custom-call(bf16[4,144,512]{2,1,0:T(8,128)(2,1)S(1)} %get-tuple-element.32.own.refs_2_, bf16[3,136,512]{2,1,0:T(8,128)(2,1)S(1)} %collective-permute-done.11.near, f32[2,7,7,512]{3,2,1,0:T(8,128)S(1)} %copy.11.taps.refs_2_, f32[2,512]{1,0:T(2,128)S(1)} %copy-done.7), custom_call_target="tpu_custom_call" | custom-call | flops 1 | tf_op jit(solution)/shard_map/conv_own/pallas_call | solution.py:369
  35.5 4.6 %collective-permute-done.12.refs_0_ = bf16[1040,512]{1,0:T(8,128)(2,1)S(1)} collective-permute-done((bf16[1040,512]{1,0:T(8,128)(2,1)S(1)}, bf16[1040,512]{1,0:T(8,128)(2,1)S(1)}, u32[]{:S(2)}, u32[]{:S(2)}) %collective-permute-start.12) | collective-permute-done | bytes 1064992 | tf_op jit(solution)/shard_map/ppermute | solution.py:436
  40.1 4.2 %collective-permute-done.10.refs_0_ = bf16[3,136,512]{2,1,0:T(8,128)(2,1)S(1)} collective-permute-done((bf16[3,136,512]{2,1,0:T(8,128)(2,1)S(1)}, bf16[3,136,512]{2,1,0:T(8,128)(2,1)S(1)}, u32[]{:S(2)}, u32[]{:S(2)}) %collective-permute-start.10) | collective-permute-done | bytes 417824 | tf_op jit(solution)/shard_map/ppermute | solution.py:432
  44.3 1.6 %conv_rest.4 = (bf16[256,512]{1,0:T(8,128)(2,1)S(1)}, f32[256,512]{1,0:T(8,128)S(1)}) custom-call(bf16[3,136,512]{2,1,0:T(8,128)(2,1)S(1)} %collective-permute-done.10.refs_0_, f32[4,4,128,128]{3,2,1,0:T(8,128)S(1)} %conv_own.3.refs_1_, f32[2,7,7,512]{3,2,1,0:T(8,128)S(1)} %copy.11.taps.refs_2_, f32[2,512]{1,0:T(2,128)S(1)} %copy-done.8, ...), custom_call_target="tpu_custom_call" | custom-call | flops 99999997952 | tf_op jit(solution)/shard_map/conv_rest/pallas_call | solution.py:388
  45.9 1.1 %more.4 = bf16[2,128,512]{2,1,0:T(8,128)(2,1)S(1)} custom-call(bf16[256,512]{1,0:T(8,128)(2,1)S(1)} %get-tuple-element.34.x, f32[256,512]{1,0:T(8,128)S(1)} %get-tuple-element.35.before, bf16[1040,512]{1,0:T(8,128)(2,1)S(1)} %collective-permute-done.12.refs_0_, bf16[1040,512]{1,0:T(8,128)(2,1)S(1)} %collective-permute-done.13.refs_1_, ...), custom_call_target="tpu_custom_call" | custom-call | flops 1 | tf_op jit(solution)/shard_map/more/pallas_call | solution.py:414
  47.0 1.6 %collective-permute-start.14 = (bf16[2,128,512]{2,1,0:T(8,128)(2,1)S(1)}, bf16[2,128,512]{2,1,0:T(8,128)(2,1)S(1)}, u32[]{:S(2)}, u32[]{:S(2)}) collective-permute-start(bf16[2,128,512]{2,1,0:T(8,128)(2,1)S(1)} %more.4), channel_id=1, source_target_pairs={{0,1},{1,0},{2,3},{3,2},{4,5},{5,4},{6,7},{7,6},{8,9},{9,8},{10,11... | collective-permute-start | bytes 786440 | tf_op jit(solution)/shard_map/ppermute | solution.py:436
  48.6 2.2 %conv_rest.5 = (bf16[256,512]{1,0:T(8,128)(2,1)S(1)}, f32[256,512]{1,0:T(8,128)S(1)}) custom-call(bf16[3,136,512]{2,1,0:T(8,128)(2,1)S(1)} %collective-permute-done.10.refs_0_, f32[4,4,128,128]{3,2,1,0:T(8,128)S(1)} %conv_own.3.refs_1_, f32[2,7,7,512]{3,2,1,0:T(8,128)S(1)} %copy.11.taps.refs_2_, f32[2,512]{1,0:T(2,128)S(1)} %copy-done.8, ...), custom_call_target="tpu_custom_call" | custom-call | flops 1 | tf_op jit(solution)/shard_map/conv_rest/pallas_call | solution.py:388
  50.8 1.1 %more.5 = bf16[2,128,512]{2,1,0:T(8,128)(2,1)S(1)} custom-call(bf16[256,512]{1,0:T(8,128)(2,1)S(1)} %get-tuple-element.37.x, f32[256,512]{1,0:T(8,128)S(1)} %get-tuple-element.38.before, bf16[1040,512]{1,0:T(8,128)(2,1)S(1)} %collective-permute-done.12.refs_0_, bf16[1040,512]{1,0:T(8,128)(2,1)S(1)} %collective-permute-done.13.refs_1_, ...), custom_call_target="tpu_custom_call" | custom-call | flops 1 | tf_op jit(solution)/shard_map/more/pallas_call | solution.py:414
  52.5 3.0 %collective-permute-done.14 = bf16[2,128,512]{2,1,0:T(8,128)(2,1)S(1)} collective-permute-done((bf16[2,128,512]{2,1,0:T(8,128)(2,1)S(1)}, bf16[2,128,512]{2,1,0:T(8,128)(2,1)S(1)}, u32[]{:S(2)}, u32[]{:S(2)}) %collective-permute-start.14) | collective-permute-done | bytes 262176 | tf_op jit(solution)/shard_map/ppermute | solution.py:436
  55.6 3.5 %collective-permute-done.15 = bf16[2,128,512]{2,1,0:T(8,128)(2,1)S(1)} collective-permute-done((bf16[2,128,512]{2,1,0:T(8,128)(2,1)S(1)}, bf16[2,128,512]{2,1,0:T(8,128)(2,1)S(1)}, u32[]{:S(2)}, u32[]{:S(2)}) %collective-permute-start.15) | collective-permute-done | bytes 262176 | tf_op jit(solution)/shard_map/ppermute | solution.py:436
  (45 shorter events, 4.4 us)
Async XLA Ops:
  0.0 6.6 %copy-start.4 = (f32[2,1024]{1,0:T(2,128)S(1)}, f32[2,1024]{1,0:T(2,128)}, u32[]{:S(2)}) copy-start(f32[2,1024]{1,0:T(2,128)} %refs_6_.5) | copy-start | bytes 24580
  0.0 6.6 %copy-start = (bf16[2,512,1024]{2,1,0:T(8,128)(2,1)S(1)}, bf16[2,512,1024]{2,1,0:T(8,128)(2,1)}, u32[]{:S(2)}) copy-start(bf16[2,512,1024]{2,1,0:T(8,128)(2,1)} %refs_5_.5) | copy-start | bytes 6291460
  2.5 10.1 %collective-permute-start.1 = (bf16[3,144,512]{2,1,0:T(8,128)(2,1)}, bf16[3,144,512]{2,1,0:T(8,128)(2,1)S(1)}, u32[]{:S(2)}, u32[]{:S(2)}) collective-permute-start(bf16[3,144,512]{2,1,0:T(8,128)(2,1)} %get-tuple-element.23), channel_id=1, source_target_pairs={{0,2},{2,0},{4,6},{6,4},{8,10},{10,8},{12,14},{14,12},{16,18},{18,... | collective-permute-start | bytes 1327112 | tf_op jit(solution)/shard_map/ppermute | solution.py:427
  2.6 9.6 %collective-permute-start.2 = (bf16[528,256]{1,0:T(8,128)(2,1)}, bf16[528,256]{1,0:T(8,128)(2,1)S(1)}, u32[]{:S(2)}, u32[]{:S(2)}) collective-permute-start(bf16[528,256]{1,0:T(8,128)(2,1)} %get-tuple-element.26), channel_id=1, source_target_pairs={{0,1},{1,0},{2,3},{3,2},{4,5},{5,4},{6,7},{7,6},{8,9},{9,8},{10,11... | collective-permute-start | bytes 811016 | tf_op jit(solution)/shard_map/ppermute | solution.py:436
  4.1 13.6 %collective-permute-start.3 = (bf16[256,512]{1,0:T(8,128)(2,1)}, bf16[256,512]{1,0:T(8,128)(2,1)S(1)}, u32[]{:S(2)}, u32[]{:S(2)}) collective-permute-start(bf16[256,512]{1,0:T(8,128)(2,1)} %get-tuple-element.27), channel_id=1, source_target_pairs={{0,1},{1,0},{2,3},{3,2},{4,5},{5,4},{6,7},{7,6},{8,9},{9,8},{10,11... | collective-permute-start | bytes 786440 | tf_op jit(solution)/shard_map/ppermute | solution.py:436
  4.6 14.6 %collective-permute-start = (bf16[3,144,512]{2,1,0:T(8,128)(2,1)}, bf16[3,144,512]{2,1,0:T(8,128)(2,1)S(1)}, u32[]{:S(2)}, u32[]{:S(2)}) collective-permute-start(bf16[3,144,512]{2,1,0:T(8,128)(2,1)} %get-tuple-element.22), channel_id=1, source_target_pairs={{2,4},{6,8},{10,12},{14,16},{18,20},{22,24},{26,28},{4,2},{8,6},{1... | collective-permute-start | bytes 1327112 | tf_op jit(solution)/shard_map/ppermute | solution.py:432
  8.2 4.4 %copy-start.7 = (f32[2,512]{1,0:T(2,128)S(1)}, f32[2,512]{1,0:T(2,128)}, u32[]{:S(2)}) copy-start(f32[2,512]{1,0:T(2,128)} %bias.3) | copy-start | bytes 12292
  8.4 31.7 %collective-permute-start.12 = (bf16[1040,512]{1,0:T(8,128)(2,1)S(1)}, bf16[1040,512]{1,0:T(8,128)(2,1)S(1)}, u32[]{:S(2)}, u32[]{:S(2)}) collective-permute-start(bf16[1040,512]{1,0:T(8,128)(2,1)S(1)} %pack.1), channel_id=1, source_target_pairs={{0,1},{1,0},{2,3},{3,2},{4,5},{5,4},{6,7},{7,6},{8,9},{9,8},{10,11... | collective-permute-start | bytes 3194888 | tf_op jit(solution)/shard_map/ppermute | solution.py:436
  12.1 11.1 %collective-permute-start.4 = (bf16[528,256]{1,0:T(8,128)(2,1)S(1)}, bf16[528,256]{1,0:T(8,128)(2,1)S(1)}, u32[]{:S(2)}, u32[]{:S(2)}) collective-permute-start(bf16[528,256]{1,0:T(8,128)(2,1)S(1)} %collective-permute-done.2.refs_0_), channel_id=1, source_target_pairs={{0,8},{2,10},{4,12},{6,14},{8,0},{10,2},{12,4},{14,6},{16,24},{18,... | collective-permute-start | bytes 811016 | tf_op jit(solution)/shard_map/ppermute | solution.py:440
  12.6 6.6 %copy-start.2 = (bf16[2,1024,512]{2,1,0:T(8,128)(2,1)S(1)}, bf16[2,1024,512]{2,1,0:T(8,128)(2,1)}, u32[]{:S(2)}) copy-start(bf16[2,1024,512]{2,1,0:T(8,128)(2,1)} %refs_7_.5) | copy-start | bytes 6291460
  12.6 6.6 %copy-start.8 = (f32[2,512]{1,0:T(2,128)S(1)}, f32[2,512]{1,0:T(2,128)}, u32[]{:S(2)}) copy-start(f32[2,512]{1,0:T(2,128)} %refs_3_.8) | copy-start | bytes 12292
  12.6 6.6 %copy-start.9 = (f32[2,512]{1,0:T(2,128)S(1)}, f32[2,512]{1,0:T(2,128)}, u32[]{:S(2)}) copy-start(f32[2,512]{1,0:T(2,128)} %refs_4_.8) | copy-start | bytes 12292
  15.9 11.5 %copy-start.5 = (f32[2,512]{1,0:T(2,128)S(1)}, f32[2,512]{1,0:T(2,128)}, u32[]{:S(2)}) copy-start(f32[2,512]{1,0:T(2,128)} %refs_3_.9) | copy-start | bytes 12292
  15.9 11.5 %copy-start.6 = (f32[2,512]{1,0:T(2,128)S(1)}, f32[2,512]{1,0:T(2,128)}, u32[]{:S(2)}) copy-start(f32[2,512]{1,0:T(2,128)} %refs_4_.9) | copy-start | bytes 12292
  17.7 8.1 %collective-permute-start.5 = (bf16[256,512]{1,0:T(8,128)(2,1)S(1)}, bf16[256,512]{1,0:T(8,128)(2,1)S(1)}, u32[]{:S(2)}, u32[]{:S(2)}) collective-permute-start(bf16[256,512]{1,0:T(8,128)(2,1)S(1)} %collective-permute-done.3.refs_1_), channel_id=1, source_target_pairs={{0,8},{2,10},{4,12},{6,14},{8,0},{10,2},{12,4},{14,6},{16,24},{18,... | collective-permute-start | bytes 786440 | tf_op jit(solution)/shard_map/ppermute | solution.py:440
  18.1 7.7 %collective-permute-start.6 = (bf16[528,256]{1,0:T(8,128)(2,1)S(1)}, bf16[528,256]{1,0:T(8,128)(2,1)S(1)}, u32[]{:S(2)}, u32[]{:S(2)}) collective-permute-start(bf16[528,256]{1,0:T(8,128)(2,1)S(1)} %collective-permute-done.2.refs_0_), channel_id=1, source_target_pairs={{0,2},{2,0},{4,6},{6,4},{8,10},{10,8},{12,14},{14,12},{16,18},{18,... | collective-permute-start | bytes 811016 | tf_op jit(solution)/shard_map/ppermute | solution.py:427
  23.3 2.6 %collective-permute-start.8 = (bf16[528,256]{1,0:T(8,128)(2,1)S(1)}, bf16[528,256]{1,0:T(8,128)(2,1)S(1)}, u32[]{:S(2)}, u32[]{:S(2)}) collective-permute-start(bf16[528,256]{1,0:T(8,128)(2,1)S(1)} %collective-permute-done.4.refs_2_), channel_id=1, source_target_pairs={{0,2},{2,0},{4,6},{6,4},{8,10},{10,8},{12,14},{14,12},{16,18},{18,... | collective-permute-start | bytes 811016 | tf_op jit(solution)/shard_map/ppermute | solution.py:427
  23.3 2.5 %collective-permute-start.7 = (bf16[256,512]{1,0:T(8,128)(2,1)S(1)}, bf16[256,512]{1,0:T(8,128)(2,1)S(1)}, u32[]{:S(2)}, u32[]{:S(2)}) collective-permute-start(bf16[256,512]{1,0:T(8,128)(2,1)S(1)} %collective-permute-done.3.refs_1_), channel_id=1, source_target_pairs={{0,2},{2,0},{4,6},{6,4},{8,10},{10,8},{12,14},{14,12},{16,18},{18,... | collective-permute-start | bytes 786440 | tf_op jit(solution)/shard_map/ppermute | solution.py:427
  25.9 1.5 %collective-permute-start.9 = (bf16[256,512]{1,0:T(8,128)(2,1)S(1)}, bf16[256,512]{1,0:T(8,128)(2,1)S(1)}, u32[]{:S(2)}, u32[]{:S(2)}) collective-permute-start(bf16[256,512]{1,0:T(8,128)(2,1)S(1)} %collective-permute-done.5.refs_3_), channel_id=1, source_target_pairs={{0,2},{2,0},{4,6},{6,4},{8,10},{10,8},{12,14},{14,12},{16,18},{18,... | collective-permute-start | bytes 786440 | tf_op jit(solution)/shard_map/ppermute | solution.py:427
  30.3 2.3 %collective-permute-start.11 = (bf16[3,136,512]{2,1,0:T(8,128)(2,1)S(1)}, bf16[3,136,512]{2,1,0:T(8,128)(2,1)S(1)}, u32[]{:S(2)}, u32[]{:S(2)}) collective-permute-start(bf16[3,136,512]{2,1,0:T(8,128)(2,1)S(1)} %get-tuple-element.33), channel_id=1, source_target_pairs={{0,2},{2,0},{4,6},{6,4},{8,10},{10,8},{12,14},{14,12},{16,18},{18,... | collective-permute-start | bytes 1253384 | tf_op jit(solution)/shard_map/ppermute | solution.py:427
  30.5 13.8 %collective-permute-start.10 = (bf16[3,136,512]{2,1,0:T(8,128)(2,1)S(1)}, bf16[3,136,512]{2,1,0:T(8,128)(2,1)S(1)}, u32[]{:S(2)}, u32[]{:S(2)}) collective-permute-start(bf16[3,136,512]{2,1,0:T(8,128)(2,1)S(1)} %get-tuple-element.31), channel_id=1, source_target_pairs={{2,4},{6,8},{10,12},{14,16},{18,20},{22,24},{26,28},{4,2},{8,6},{1... | collective-permute-start | bytes 1253384 | tf_op jit(solution)/shard_map/ppermute | solution.py:432
  40.1 5.8 %collective-permute-start.13 = (bf16[1040,512]{1,0:T(8,128)(2,1)S(1)}, bf16[1040,512]{1,0:T(8,128)(2,1)S(1)}, u32[]{:S(2)}, u32[]{:S(2)}) collective-permute-start(bf16[1040,512]{1,0:T(8,128)(2,1)S(1)} %collective-permute-done.12.refs_0_), channel_id=1, source_target_pairs={{0,2},{2,0},{4,6},{6,4},{8,10},{10,8},{12,14},{14,12},{16,18},{18,... | collective-permute-start | bytes 3194888 | tf_op jit(solution)/shard_map/ppermute | solution.py:427
  47.0 8.6 %collective-permute-start.14 = (bf16[2,128,512]{2,1,0:T(8,128)(2,1)S(1)}, bf16[2,128,512]{2,1,0:T(8,128)(2,1)S(1)}, u32[]{:S(2)}, u32[]{:S(2)}) collective-permute-start(bf16[2,128,512]{2,1,0:T(8,128)(2,1)S(1)} %more.4), channel_id=1, source_target_pairs={{0,1},{1,0},{2,3},{3,2},{4,5},{5,4},{6,7},{7,6},{8,9},{9,8},{10,11... | collective-permute-start | bytes 786440 | tf_op jit(solution)/shard_map/ppermute | solution.py:436
  51.9 7.1 %collective-permute-start.15 = (bf16[2,128,512]{2,1,0:T(8,128)(2,1)S(1)}, bf16[2,128,512]{2,1,0:T(8,128)(2,1)S(1)}, u32[]{:S(2)}, u32[]{:S(2)}) collective-permute-start(bf16[2,128,512]{2,1,0:T(8,128)(2,1)S(1)} %more.5), channel_id=1, source_target_pairs={{0,1},{1,0},{2,3},{3,2},{4,5},{5,4},{6,7},{7,6},{8,9},{9,8},{10,11... | collective-permute-start | bytes 786440 | tf_op jit(solution)/shard_map/ppermute | solution.py:436
  (3 other events, 10.4 us)

commit v4 on v3

--- a/solution.py
+++ b/solution.py
@@ -11,13 +11,11 @@
 MARGIN = 16
 LONG = 10**11
 ERF = (
-    0.7978842161099958,
-    0.03633428353366734,
-    -3.3130008237205104e-05,
-    -5.524015421773868e-05,
-    3.969108888631555e-06,
-    -1.33446374821295e-07,
-    1.8056156531812635e-09,
+    0.7978275766866006,
+    0.036469930744144466,
+    -0.00012547620415072412,
+    -3.0467196783772113e-05,
+    1.1126315774795922e-06,
 )
 VMEM = pl.BlockSpec(memory_space=pltpu.VMEM)
 HBM = pl.BlockSpec(memory_space=pltpu.HBM)
@@ -25,13 +23,12 @@
 COPIES = pltpu.CompilerParams(vmem_limit_bytes=60 * 1024 * 1024)
 
 
-def gelu(u):
+def twice_gelu(u):
     v = u * u
     p = jnp.full_like(u, ERF[-1])
     for c in ERF[-2::-1]:
         p = p * v + c
-    half = 0.5 * u
-    return half * jnp.tanh(u * p) + half
+    return u + u * jnp.tanh(u * p)
 
 
 def tile_of(width):
@@ -59,17 +56,36 @@
     def edge(self, b):
         return self.reach * (self.blocks - b), 8 if b else MARGIN
 
+    def extra(self, b):
+        same = self.size(*self.window(0)) == self.size(*self.edge(0))
+        return int(b == 0 and self.blocks > 1 and self.rows > self.reach and same)
+
+    def own_rows(self, b):
+        return range(-self.extra(b - 1), self.rows)
+
+    def result_rows(self, b):
+        return range(-self.extra(b), self.rows)
+
+    def far_rows(self, b):
+        return range(self.extra(b - 1), self.reach + self.extra(b))
+
     def place(self, b):
         to, halo = self.start(*self.window(b)), self.start(*self.edge(b))
         start = self.start(*self.window(b - 1)) if b else 0
         later = self.start(*self.edge(b + 1))
         row = lax.axis_index("row")
         odd, parity = lax.rem(row, 2), lax.rem(lax.div(row, 4), 2)
-        return to - start, halo - to + MARGIN, odd, parity, int(b == 0), later - to, halo
-
-
-def row_of(place, d, rows):
-    return jnp.where(place[4] * place[2] == 1, rows - 1 - d, d)
+        there = jnp.where(odd == 1, row < lax.axis_size("row") - 1, row > 0)
+        return to - start, halo - to + MARGIN, odd, parity, there, later - to, halo
+
+
+def own_row(layout, b, place, d):
+    return d + layout.extra(b - 1) if b else jnp.where(place[2] == 1, layout.rows - 1 - d, d)
+
+
+def far_row(layout, b, place, k):
+    rows = layout.far_rows(b)
+    return k - rows[0] if b else jnp.where(place[2] == 1, k, len(rows) - 1 - k)
 
 
 def tap_of(place, t, size):
@@ -92,41 +108,45 @@
     return sums
 
 
-def own_kernel(b, layout, own, near, taps, bias, out, wide):
+def own_kernel(b, layout, complete, own, near, taps, bias, *refs):
     place = layout.place(b)
-    groups, rows, width, _ = out.shape
+    out, *conv, wide = refs
+    groups, _, width, _ = out.shape
     reach = near.shape[0]
-    fill_own(place, own, wide, rows)
+    rows, outputs = layout.own_rows(b), layout.result_rows(b)
+    fill_own(layout, b, place, own, wide)
     back = place[2] if b == 0 else 1
     sources = [(near, jnp.where(back == 1, reach - 1 - k, k)) for k in range(reach)]
-    fill_halo(place, sources, wide, rows)
+    fill_halo(place, sources, wide, len(rows))
     step = tile_of(width)
-    outputs = range(rows)
-    inputs = range(rows + reach)
+    inputs = range(rows[0], layout.rows + reach)
 
     def group(c, _):
         lanes = pl.ds(pl.multiple_of(c * LANES, LANES), LANES)
         for start in range(0, width, step):
-            sums = [jnp.broadcast_to(bias[b : b + 1, lanes], (step, LANES)) for _ in range(rows)]
+            sums = [jnp.broadcast_to(bias[b : b + 1, lanes], (step, LANES)) for _ in outputs]
             sums = convolve(b, place, sums, wide, inputs, outputs, taps, c, lanes, start, step)
-            for d in range(rows):
-                out[c, d, start : start + step] = sums[d]
+            for n, d in enumerate(outputs):
+                if d in complete:
+                    conv[0][c, d - complete[0], start : start + step] = sums[n]
+                else:
+                    out[c, n, start : start + step] = sums[n]
         return 0
 
     lax.fori_loop(0, groups, group, 0)
 
 
-def fill_own(place, own, wide, rows):
+def fill_own(layout, b, place, own, wide):
     groups, _, columns, _ = wide.shape
     for k in range(columns // MARGIN):
         at = place[0] + (k - 1) * MARGIN
         inside = (at >= 0) & (at <= own.shape[1] - MARGIN)
         at = pl.multiple_of(jnp.clip(at, 0, own.shape[1] - MARGIN), MARGIN)
-        for d in range(rows):
+        for n, d in enumerate(layout.own_rows(b)):
             for c in range(groups):
-                x = own[row_of(place, d, rows), pl.ds(at, MARGIN), c * LANES : (c + 1) * LANES]
+                x = own[own_row(layout, b, place, d), pl.ds(at, MARGIN), c * LANES : (c + 1) * LANES]
                 x = jnp.where(inside, x.astype(jnp.float32), 0.0)
-                wide[c, d, k * MARGIN : (k + 1) * MARGIN] = x
+                wide[c, n, k * MARGIN : (k + 1) * MARGIN] = x
 
 
 def fill_halo(place, sources, wide, first):
@@ -142,21 +162,17 @@
             wide[c, first + i, at] = x
 
 
-def add_far(b, place, chosen, far, before, taps, conv, wide):
+def add_far(b, layout, place, chosen, far, before, taps, conv, wide):
     groups, _, width, _ = before.shape
-    reach = taps.shape[1] // 2
-    rows = [(ref, k) for ref in far for k in range(ref.shape[0])]
-    if b == 0:
-        rows = [(far[0], jnp.where(place[2] == 1, k, reach - 1 - k)) for k in range(reach)]
-    rows = rows[: max(0, reach - min(chosen))]
-    inputs = [-1 - k for k in range(len(rows))]
-    fill_halo(place, rows, wide, 0)
+    rows = layout.far_rows(b)
+    fill_halo(place, [(far, far_row(layout, b, place, k)) for k in rows], wide, 0)
     step = tile_of(width)
+    inputs = [-1 - k for k in rows]
 
     def group(c, _):
         lanes = pl.ds(pl.multiple_of(c * LANES, LANES), LANES)
         for start in range(0, width, step):
-            sums = [before[c, d, start : start + step] for d in chosen]
+            sums = [before[c, n, start : start + step] for n in range(len(chosen))]
             sums = convolve(b, place, sums, wide, inputs, chosen, taps, c, lanes, start, step)
             for n in range(len(chosen)):
                 conv[c, n, start : start + step] = sums[n]
@@ -185,7 +201,7 @@
     part = 256 if hidden % 256 == 0 else 128
     for k in range(0, hidden, part):
         u = jnp.dot(x[...], up[:, k : k + part], preferred_element_type=jnp.float32)
-        h = gelu(u + b_up[:, k : k + part]).astype(jnp.bfloat16)
+        h = twice_gelu(u + b_up[:, k : k + part]).astype(jnp.bfloat16)
         y = jnp.dot(h, down[k : k + part, :], preferred_element_type=jnp.float32)
         if k:
             total[...] += y
@@ -193,58 +209,89 @@
             total[...] = y if before is None else before[...] + y
 
 
-def rest_kernel(b, layout, chosen, number, *refs):
+def rest_kernel(b, layout, chosen, whole, *refs):
     place = layout.place(b)
-    far, refs = refs[:number], refs[number:]
-    before, taps, gain, shift, up, b_up, down, normed, total, conv, wide = refs
-    add_far(b, place, chosen, far, before, taps, conv, wide)
-    normalise(b, conv, gain, shift, normed)
-    project(normed, up.at[b], b_up.at[b : b + 1], down.at[b], total)
-
-
-def more_kernel(b, layout, chosen, kind, number, final, x, before, *refs):
+    refs = list(refs)
+    far = refs.pop(0) if chosen[0] < layout.reach - layout.extra(b - 1) else None
+    before, gain, shift, *refs = refs
+    if far is None:
+        conv = before
+    else:
+        taps, *refs, conv, wide = refs
+        add_far(b, layout, place, chosen, far, before, taps, conv, wide)
+    if whole:
+        up, b_up, down, normed, total = refs
+        normalise(b, conv, gain, shift, normed)
+        project(normed, up.at[b], b_up.at[b : b + 1], down.at[b], total)
+    else:
+        normalise(b, conv, gain, shift, refs[0])
+
+
+def pieces_of(kind, channels, parts):
+    if kind == "plain":
+        return [(parts[n], parts[n + 1][...], parts[n + 2]) for n in range(0, len(parts), 3)]
+    pieces = []
+    if kind == "joined":
+        for part in parts:
+            last = part.shape[0] - MARGIN
+            terms = part[last:, :].astype(jnp.float32)
+            pieces.append((part.at[:channels], terms[0:1] + terms[1:2], part.at[channels:last]))
+        return pieces
+    for part, down in zip(parts[::2], parts[1::2]):
+        terms = part[channels:, :].astype(jnp.float32)
+        pieces.append((part.at[:channels], terms[0:1] + terms[1:2], down))
+    return pieces
+
+
+def add_kernel(kind, channels, x, before, *refs):
+    for piece in pieces_of(kind, channels, refs[:-1]):
+        project(x, *piece, refs[-1], before)
+        before = refs[-1]
+
+
+def more_kernel(b, layout, chosen, kind, number, begun, x, *refs):
     place = layout.place(b)
-    channels = x.shape[1]
+    channels, final = layout.channels, b == layout.blocks - 1
     refs = list(refs)
-    parts = [refs.pop(0) for _ in range(number)]
-    state, b_down, scale = (refs.pop(0) for _ in range(3))
+    take = lambda count: [refs.pop(0) for _ in range(count)]
+    pieces, first = [], None
+    if begun:
+        first = refs.pop(0)
+    else:
+        up, b_up, down = take(3)
+        pieces.append((up.at[b], b_up.at[b : b + 1], down.at[b]))
+    parts = take(number)
+    state, b_down, scale = take(3)
+    far_state = None if final else refs.pop(0)
     out = refs.pop(0)
-    sends = [] if final else [refs.pop(0) for _ in range(2)]
+    sends = [] if final else take(2)
     total = refs.pop(0)
-    odd, parity = place[2], place[3]
-    pieces = []
-    if kind == "plain":
-        pieces = [(parts[n], parts[n + 1][...], parts[n + 2]) for n in range(0, number, 3)]
-    else:
-        if kind == "joined":
-            views = [(p.at[:channels], p.at[channels : p.shape[0] - MARGIN], p.at[p.shape[0] - MARGIN :]) for p in parts]
-        else:
-            views = [(p.at[:channels], q, p.at[channels:]) for p, q in zip(parts[::2], parts[1::2])]
-        for up, down, bias in views:
-            terms = bias[...].astype(jnp.float32)
-            pieces.append((up, terms[0:1] + terms[1:2], down))
-    first = before
+    pieces += pieces_of(kind, channels, parts)
     for piece in pieces:
         project(x, *piece, total, first)
         first = total
     count, width, _ = out.shape
-    rows = state.shape[0]
+    rows, reach = layout.rows, layout.reach
     for n, d in enumerate(chosen):
-        at = pl.ds(pl.multiple_of(place[0], MARGIN), width)
-        s = state[row_of(place, d, rows), at, :].astype(jnp.float32)
-        y = first[n * width : (n + 1) * width, :] + b_down[b : b + 1]
+        if d < 0:
+            s = far_state[far_row(layout, b, place, -1 - d), :, :].astype(jnp.float32)
+        else:
+            at = pl.ds(pl.multiple_of(place[0], MARGIN), width)
+            s = state[own_row(layout, b, place, d), at, :].astype(jnp.float32)
+        y = 0.5 * first[n * width : (n + 1) * width, :] + b_down[b : b + 1]
         s = s + scale[b : b + 1] * y
         if final:
-            out[jnp.where(odd == 1, count - 1 - n, n)] = s.astype(out.dtype)
+            out[jnp.where(place[2] == 1, count - 1 - n, n)] = s.astype(out.dtype)
             continue
+        if d < 0:
+            s = jnp.where(place[4], s, 0.0)
         out[n] = s.astype(out.dtype)
         total[n * width : (n + 1) * width, :] = s
         far, near = sends
         size = near.shape[1]
         s = total[pl.ds(pl.multiple_of(n * width + place[5], 8), size), :].astype(out.dtype)
-        reach = near.shape[0]
-        if d < reach:
-            far[d] = s
+        if d in layout.far_rows(b + 1):
+            far[d - layout.far_rows(b + 1)[0]] = s
         if d >= rows - reach:
             near[d - (rows - reach)] = s
 
@@ -278,13 +325,11 @@
     if weights:
         *refs, bias, terms = refs
     outs, stages = list(refs[: len(refs) // 2]), list(refs[len(refs) // 2 :])
-    reach, size, _ = outs[0].shape
-    last = layout.rows - reach
-    at = pl.ds(pl.multiple_of(place[6], MARGIN), size)
-    sources = [
-        features.at[pl.ds(place[2] * last, reach), at],
-        features.at[pl.ds((1 - place[2]) * last, reach), at],
-    ]
+    at = pl.ds(pl.multiple_of(place[6], MARGIN), outs[0].shape[1])
+    sources = []
+    for side, out in zip((place[2], 1 - place[2]), outs):
+        count = out.shape[0]
+        sources.append(features.at[pl.ds(side * (layout.rows - count), count), at])
     if weights:
         channels = layout.channels
         hidden, taken = take(0, place, weights, 4, stages[2].at[:channels], stages[3])
@@ -325,7 +370,7 @@
 def prepare(layout, features, weights=()):
     _, size = layout.size(*layout.edge(0))
     channels = layout.channels
-    shapes = [(layout.reach, size, channels)] * 2
+    shapes = [(count, size, channels) for count in (len(layout.far_rows(0)), layout.reach)]
     scratch = [pltpu.SemaphoreType.DMA((6, 3))]
     if weights:
         hidden = weights[0].shape[2] // 4
@@ -363,56 +408,73 @@
     )(*weights)
 
 
-def conv_own(b, layout, own, near, width, taps, bias):
-    rows, _, channels = own.shape
-    groups, reach = channels // LANES, near.shape[0]
+def conv_own(b, layout, own, near, taps, bias):
+    groups = layout.channels // LANES
+    _, width = layout.size(*layout.window(b))
+    final = b == layout.blocks - 1
+    complete = range(layout.reach - layout.extra(b - 1), layout.rows) if final else range(0)
+    counts = [len(layout.result_rows(b)) - len(complete)] + [len(complete)] * final
+    lines = len(layout.own_rows(b)) + layout.reach
     return pl.pallas_call(
-        functools.partial(own_kernel, b, layout),
-        out_shape=jax.ShapeDtypeStruct((groups, rows, width, LANES), jnp.float32),
+        functools.partial(own_kernel, b, layout, complete),
+        out_shape=[jax.ShapeDtypeStruct((groups, n, width, LANES), jnp.float32) for n in counts],
         in_specs=[VMEM] * 4,
+        out_specs=[VMEM] * len(counts),
+        scratch_shapes=[pltpu.VMEM((groups, lines, width + 2 * MARGIN, LANES), jnp.float32)],
+        compiler_params=PARAMS,
+        cost_estimate=cost(1 if final else LONG),
+        name="conv_own",
+    )(own, near, taps, bias)
+
+
+def conv_rest(b, layout, chosen, far, before, taps, gain, shift, weights=()):
+    groups, rows, width, _ = before.shape
+    channels = layout.channels
+    args = [before, gain, shift]
+    shapes = [jax.ShapeDtypeStruct((rows * width, channels), jnp.bfloat16)]
+    scratch = []
+    if far is not None:
+        args = [far, *args, taps]
+        lines = len(layout.far_rows(b))
+        scratch.append(pltpu.VMEM((groups, rows, width, LANES), jnp.float32))
+        scratch.append(pltpu.VMEM((groups, lines, width + 2 * MARGIN, LANES), jnp.float32))
+    if weights:
+        args += weights
+        shapes.append(jax.ShapeDtypeStruct((rows * width, channels), jnp.float32))
+    return pl.pallas_call(
+        functools.partial(rest_kernel, b, layout, chosen, bool(weights)),
+        out_shape=shapes,
+        in_specs=[VMEM] * len(args),
+        out_specs=[VMEM] * len(shapes),
+        scratch_shapes=scratch,
+        compiler_params=PARAMS,
+        cost_estimate=cost(1 if weights else LONG),
+        name="conv_rest",
+    )(*args)
+
+
+def add(x, before, kind, parts):
+    return pl.pallas_call(
+        functools.partial(add_kernel, kind, x.shape[1]),
+        out_shape=jax.ShapeDtypeStruct(before.shape, jnp.float32),
+        in_specs=[VMEM] * (2 + len(parts)),
         out_specs=VMEM,
-        scratch_shapes=[
-            pltpu.VMEM((groups, rows + reach, width + 2 * MARGIN, LANES), jnp.float32)
-        ],
         compiler_params=PARAMS,
         cost_estimate=cost(1),
-        name="conv_own",
-    )(own, near, taps, bias)
-
-
-def conv_rest(b, layout, chosen, far, before, taps, gain, shift, up, b_up, down):
-    groups, _, width, _ = before.shape
-    channels, reach = groups * LANES, taps.shape[1] // 2
-    positions = len(chosen) * width
-    args = [*far, before, taps, gain, shift, up, b_up, down]
+        name="add",
+    )(x, before, *parts)
+
+
+def more(b, layout, chosen, x, begun, kind, parts, state, b_down, scale, far=None):
+    positions, channels = x.shape
+    args = [x, *begun, *parts, state, b_down, scale]
+    shapes = [(len(chosen), positions // len(chosen), channels)]
+    if far is not None:
+        args.append(far)
+        _, size = layout.size(*layout.edge(b + 1))
+        shapes += [(n, size, channels) for n in (len(layout.far_rows(b + 1)), layout.reach)]
     return pl.pallas_call(
-        functools.partial(rest_kernel, b, layout, chosen, len(far)),
-        out_shape=(
-            jax.ShapeDtypeStruct((positions, channels), jnp.bfloat16),
-            jax.ShapeDtypeStruct((positions, channels), jnp.float32),
-        ),
-        in_specs=[VMEM] * len(args),
-        out_specs=(VMEM, VMEM),
-        scratch_shapes=[
-            pltpu.VMEM((groups, len(chosen), width, LANES), jnp.float32),
-            pltpu.VMEM((groups, reach, width + 2 * MARGIN, LANES), jnp.float32),
-        ],
-        compiler_params=PARAMS,
-        cost_estimate=cost(LONG if min(chosen) else 1),
-        name="conv_rest",
-    )(*args)
-
-
-def more(b, layout, chosen, x, before, kind, parts, state, b_down, scale, halo_shape):
-    positions, channels = x.shape
-    final = halo_shape is None
-    args = [x, before, *parts, state, b_down, scale]
-    shapes = [(len(chosen), positions // len(chosen), channels)]
-    if not final:
-        reach, size = halo_shape
-        shapes += [(reach, size, channels)] * 2
-    return pl.pallas_call(
-        functools.partial(more_kernel, b, layout, chosen, kind, len(parts), final),
+        functools.partial(more_kernel, b, layout, chosen, kind, len(parts), len(begun) == 1),
         out_shape=[jax.ShapeDtypeStruct(shape, jnp.bfloat16) for shape in shapes],
         in_specs=[VMEM] * len(args),
         out_specs=[VMEM] * len(shapes),
@@ -457,48 +519,52 @@
     me, row, count = lax.axis_index("hid"), lax.axis_index("row"), lax.axis_size("row")
     odd = lax.rem(row, 2)
     pairs = number == 2 and w_up.shape[2] == 2 * layout.channels and count % 8 == 0
-    everything = tuple(range(rows))
     weights = (w_up, b_up, w_down)
+    norm, ending = (ln_gain, ln_bias), (b_down, layer_scale)
 
     outer, inner, *packed = prepare(layout, features, weights if pairs else ())
-    far, near = [across(outer)], within(inner)
+    far, near = across(outer), within(inner)
     state = features
     if pairs:
         up, down = swap_hid(packed[0]), swap_hid(packed[1])
     for b in range(blocks):
-        final = b == blocks - 1
-        _, size = layout.size(*layout.window(b))
-        before = conv_own(b, layout, state, near, size, dw_weight, dw_bias)
-        rest = lambda chosen, far, before: conv_rest(
-            b, layout, chosen, far, before, dw_weight, ln_gain, ln_bias, *weights
-        )
-        add = lambda chosen, work, parts: more(
-            b, layout, chosen, *work, kind, parts, state, b_down, layer_scale,
-            None if final else (layout.reach, layout.size(*layout.edge(b + 1))[1]),
-        )
-        if pairs and not final:
-            later = swap_hid(pack(b + 1, layout, weights))
+        before, *complete = conv_own(b, layout, state, near, dw_weight, dw_bias)
+        if not pairs:
+            kind, parts = "plain", gather(w_up[b], b_up[b], w_down[b])
+        if b < blocks - 1:
+            if pairs:
+                later = swap_hid(pack(b + 1, layout, weights))
+            if pairs and b == 0:
+                down = after(down, before)
+                up_other, down_other = swap_row(up, 4), swap_row(down, 4)
+            chosen = layout.result_rows(b)
+            x, total = conv_rest(b, layout, chosen, far, before, dw_weight, *norm, weights)
+            if pairs and b == 0:
+                up_other, down_other = after(up_other, total), after(down_other, total)
+                mine = [up, down, up_other, down_other]
+                kind, parts = "pairs", [within(a) for a in mine]
+                total = add(x, total, kind, mine)
+            elif pairs:
+                kind, parts = "joined", [joined, within(joined)]
+            state, outer, inner = more(
+                b, layout, chosen, x, (total,), kind, parts, state, *ending, far
+            )
+            far, near = across(outer), within(inner)
+            if pairs:
+                joined = later
+            continue
+        first, last = tuple(range(before.shape[1])), tuple(range(before.shape[1], rows))
         if pairs and b == 0:
-            down = after(down, before)
-            up_other, down_other = swap_row(up, 4), swap_row(down, 4)
+            kind, parts = "plain", gather(w_up[b], b_up[b], w_down[b])
         elif pairs:
             joined = after(joined, before)
             kind, parts = "joined", [joined, within(joined)]
-        halves = (everything[rows // 2 :], everything[: rows // 2]) if final else (everything,)
-        work = [rest(chosen, far, before) for chosen in halves]
-        if pairs and b == 0:
-            up_other, down_other = (after(a, work[0][1]) for a in (up_other, down_other))
-            parts = [up, down, up_other, down_other]
-            kind, parts = "pairs", parts + [within(a) for a in parts]
-        elif not pairs:
-            kind, parts = "plain", gather(w_up[b], b_up[b], w_down[b])
-        results = [add(chosen, w, parts) for chosen, w in zip(halves, work)]
-        if not final:
-            state, outer, inner = results[0]
-            far, near = [across(outer)], within(inner)
-            if pairs:
-                joined = later
-    inner, outer = (r[0] for r in results)
+        x, total = conv_rest(b, layout, last, None, complete[0], dw_weight, *norm, weights)
+        before = after(before, total)
+        x_first, = conv_rest(b, layout, first, far, before, dw_weight, *norm)
+        total = after(total, x_first)
+        inner, = more(b, layout, last, x, (total,), kind, parts, state, *ending)
+        outer, = more(b, layout, first, x_first, weights, kind, parts, state, *ending)
     if number == 2:
         def columns_of(a):
             other = swap_hid(a)
@@ -509,7 +575,9 @@
     else:
         columns_of = lambda a: lax.all_gather(a, "hid", axis=1, tiled=True)
     inner, outer = columns_of(inner), columns_of(outer)
-    return jnp.concatenate([jnp.where(odd == 1, inner, outer), jnp.where(odd == 1, outer, inner)])
+    if inner.shape == outer.shape:
+        return jnp.concatenate([jnp.where(odd == 1, inner, outer), jnp.where(odd == 1, outer, inner)])
+    return jnp.where(odd == 1, jnp.concatenate([inner, outer]), jnp.concatenate([outer, inner]))
 
 
 def solution(mesh):

time: 61 us -> 60.5 us (level)
  waiting for transfers between devices: 23.9 us -> 20.6 us
  starting transfers between devices: 11.4 us -> 13.3 us
  Pallas kernels: 21.7 us -> 22.5 us
    ppermute x2, waiting for transfers between devices: 2.03 us -> 0.01 us  [swap_row(): lax.ppermute(array, 'row', [(i, i ^ bit) for i in range(lax.axis_size('ro...]
    pallas_call x5 -> x6, Pallas kernels: 14 us -> 15.4 us  [the longest x2 7.16 us: conv_own(): pl.pallas_call(functools.partial(own_kernel, b, layout, complete), out_sh...]
    ppermute x7, waiting for transfers between devices: 1.53 us -> 0.29 us  [within(): lax.ppermute(array, 'row', [(i, i ^ 1) for i in range(lax.axis_size('row'...]
    ppermute x2, starting transfers between devices: 4 us -> 4.82 us  [across(): lax.ppermute(array, 'row', pairs + [(target, source) for source, target i...]
    ppermute x7, starting transfers between devices: 0.85 us -> 1.66 us  [within(): lax.ppermute(array, 'row', [(i, i ^ 1) for i in range(lax.axis_size('row'...]
    pallas_call x3, Pallas kernels: 5.12 us -> 4.4 us  [more(): pl.pallas_call(functools.partial(more_kernel, b, layout, chosen, kind, le...]
  transfers between devices with their start and end apart: 16 -> 16, of which waited for: 9 -> 9; matrix products, arithmetic and copies ran while one was open for 0% -> 0% of each run, Pallas kernels for 30% -> 32%
where the time goes in v4:
time: 60.5 us; the launch traced here: 59.6 us
  Pallas kernels  22.5 us (37%)
  waiting for transfers between devices  20.6 us (34%)
  starting transfers between devices  13.3 us (22%)
  local copies, waits for them, and re-layouts  1.68 us (3%)
  other arithmetic  1.34 us (2%)
    ppermute x5, waiting for transfers between devices, swap_hid(): return lax.ppermute(array, 'hid', [(0, 1), (1, 0)])  15.2 us
    pallas_call x2, Pallas kernels, conv_own(): pl.pallas_call(functools.partial(own_kernel, b, layout, complete), out_sh...  7.16 us
    pallas_call x3, Pallas kernels, conv_rest(): pl.pallas_call(functools.partial(rest_kernel, b, layout, chosen, bool(wei...  6.76 us
    ppermute x5, starting transfers between devices, swap_hid(): return lax.ppermute(array, 'hid', [(0, 1), (1, 0)])  5.88 us
    ppermute x2, waiting for transfers between devices, across(): lax.ppermute(array, 'row', pairs + [(target, source) for source, target i...  5.07 us
    ppermute x2, starting transfers between devices, across(): lax.ppermute(array, 'row', pairs + [(target, source) for source, target i...  4.82 us
    pallas_call x3, Pallas kernels, more(): pl.pallas_call(functools.partial(more_kernel, b, layout, chosen, kind, le...  4.4 us
    pallas_call x1, Pallas kernels, prepare(): pl.pallas_call(functools.partial(prepare_kernel, layout), out_shape=[jax....  2.5 us
  transfers between devices with their start and end apart: 16, of which 9 were waited for; matrix products, arithmetic and copies ran while one was open for 0% of the time, Pallas kernels for 32%

profile of v4, /device:TPU:12, one launch (start us, length us, event | category | flops | bytes accessed | tf_op | source)
XLA Modules:
  0.0 59.6 jit_solution(9581389316472363794)
XLA Ops:
  0.0 2.5 %prepare.1 = (bf16[4,144,512]{2,1,0:T(8,128)(2,1)}, bf16[3,144,512]{2,1,0:T(8,128)(2,1)}, bf16[528,256]{1,0:T(8,128)(2,1)}, bf16[256,512]{1,0:T(8,128)(2,1)}) custom-call(bf16[4,256,512]{2,1,0:T(8,128)(2,1)} %refs_5_.5, bf16[2,512,1024]{2,1,0:T(8,128)(2,1)} %refs_0_.3, f32[2,1024]{1,0:T(2,128)} %refs_1_.5, bf16[2,1024,512]{2,1,0:T(8,128)(2,1)} %refs_2_.9), custom_call_target="tpu_custom_call" | custom-call | flops 1 | tf_op jit(solution)/shard_map/prepare/pallas_call | solution.py:380
  2.6 1.6 %collective-permute-start.2 = (bf16[528,256]{1,0:T(8,128)(2,1)}, bf16[528,256]{1,0:T(8,128)(2,1)S(1)}, u32[]{:S(2)}, u32[]{:S(2)}) collective-permute-start(bf16[528,256]{1,0:T(8,128)(2,1)} %get-tuple-element.28), channel_id=1, source_target_pairs={{0,1},{1,0},{2,3},{3,2},{4,5},{5,4},{6,7},{7,6},{8,9},{9,8},{10,11... | collective-permute-start | bytes 811016 | tf_op jit(solution)/shard_map/ppermute | solution.py:498
  4.2 2.2 %collective-permute-start = (bf16[4,144,512]{2,1,0:T(8,128)(2,1)}, bf16[4,144,512]{2,1,0:T(8,128)(2,1)S(1)}, u32[]{:S(2)}, u32[]{:S(2)}) collective-permute-start(bf16[4,144,512]{2,1,0:T(8,128)(2,1)} %get-tuple-element.24), channel_id=1, source_target_pairs={{2,4},{6,8},{10,12},{14,16},{18,20},{22,24},{26,28},{4,2},{8,6},{1... | collective-permute-start | bytes 1769480 | tf_op jit(solution)/shard_map/ppermute | solution.py:494
  6.9 1.6 %copy-done.1 = bf16[2,1024,512]{2,1,0:T(8,128)(2,1)S(1)} copy-done((bf16[2,1024,512]{2,1,0:T(8,128)(2,1)S(1)}, bf16[2,1024,512]{2,1,0:T(8,128)(2,1)}, u32[]{:S(2)}) %copy-start.1) | copy-done | bytes 2097176
  8.7 1.6 %collective-permute-start.12 = (bf16[1040,512]{1,0:T(8,128)(2,1)S(1)}, bf16[1040,512]{1,0:T(8,128)(2,1)S(1)}, u32[]{:S(2)}, u32[]{:S(2)}) collective-permute-start(bf16[1040,512]{1,0:T(8,128)(2,1)S(1)} %pack.1), channel_id=1, source_target_pairs={{0,1},{1,0},{2,3},{3,2},{4,5},{5,4},{6,7},{7,6},{8,9},{9,8},{10,11... | collective-permute-start | bytes 3194888 | tf_op jit(solution)/shard_map/ppermute | solution.py:498
  10.4 1.8 %collective-permute-done.2.refs_0_ = bf16[528,256]{1,0:T(8,128)(2,1)S(1)} collective-permute-done((bf16[528,256]{1,0:T(8,128)(2,1)}, bf16[528,256]{1,0:T(8,128)(2,1)S(1)}, u32[]{:S(2)}, u32[]{:S(2)}) %collective-permute-start.2) | collective-permute-done | bytes 270368 | tf_op jit(solution)/shard_map/ppermute | solution.py:498
  12.6 3.8 %conv_own.2.refs_1_ = f32[4,5,144,128]{3,2,1,0:T(8,128)S(1)} custom-call(bf16[4,256,512]{2,1,0:T(8,128)(2,1)S(1)} %copy-done.3, bf16[3,144,512]{2,1,0:T(8,128)(2,1)S(1)} %collective-permute-done.1.near, f32[2,7,7,512]{3,2,1,0:T(8,128)S(1)} %copy.11.taps.refs_4_, f32[2,512]{1,0:T(2,128)S(1)} %copy-done.9), custom_call_target="tpu_custom_call" | custom-call | flops 99999997952 | tf_op jit(solution)/shard_map/conv_own/pallas_call | solution.py:418
  16.4 1.3 %collective-permute-done.3.refs_1_ = bf16[256,512]{1,0:T(8,128)(2,1)S(1)} collective-permute-done((bf16[256,512]{1,0:T(8,128)(2,1)}, bf16[256,512]{1,0:T(8,128)(2,1)S(1)}, u32[]{:S(2)}, u32[]{:S(2)}) %collective-permute-start.3) | collective-permute-done | bytes 262176 | tf_op jit(solution)/shard_map/ppermute | solution.py:498
  18.2 3.6 %collective-permute-done.refs_0_.refs_8_ = bf16[4,144,512]{2,1,0:T(8,128)(2,1)S(1)} collective-permute-done((bf16[4,144,512]{2,1,0:T(8,128)(2,1)}, bf16[4,144,512]{2,1,0:T(8,128)(2,1)S(1)}, u32[]{:S(2)}, u32[]{:S(2)}) %collective-permute-start) | collective-permute-done | bytes 589856 | tf_op jit(solution)/shard_map/ppermute | solution.py:494
  21.9 4.8 %conv_rest.3 = (bf16[720,512]{1,0:T(8,128)(2,1)S(1)}, f32[720,512]{1,0:T(8,128)S(1)}) custom-call(bf16[4,144,512]{2,1,0:T(8,128)(2,1)S(1)} %collective-permute-done.refs_0_.refs_8_, f32[4,5,144,128]{3,2,1,0:T(8,128)S(1)} %conv_own.2.refs_1_, f32[2,512]{1,0:T(2,128)S(1)} %copy-done.7, f32[2,512]{1,0:T(2,128)S(1)} %copy-done.8, ...), custom_call_target="tpu_custom_call" | custom-call | flops 1 | tf_op jit(solution)/shard_map/conv_rest/pallas_call | solution.py:444
  27.4 1.5 %add.1.refs_0_ = f32[720,512]{1,0:T(8,128)S(1)} custom-call(bf16[720,512]{1,0:T(8,128)(2,1)S(1)} %get-tuple-element.26.x, f32[720,512]{1,0:T(8,128)S(1)} %get-tuple-element.27.before, bf16[528,256]{1,0:T(8,128)(2,1)S(1)} %collective-permute-done.2.refs_0_, bf16[256,512]{1,0:T(8,128)(2,1)S(1)} %collective-permute-done.3.refs_1_, ...), custom_call_target="tpu_custom_call" | custom-call | flops 1 | tf_op jit(solution)/shard_map/add/pallas_call | solution.py:457
  29.1 1.9 %more.3 = (bf16[5,144,512]{2,1,0:T(8,128)(2,1)S(1)}, bf16[2,136,512]{2,1,0:T(8,128)(2,1)S(1)}, bf16[3,136,512]{2,1,0:T(8,128)(2,1)S(1)}) custom-call(bf16[720,512]{1,0:T(8,128)(2,1)S(1)} %get-tuple-element.26.x, f32[720,512]{1,0:T(8,128)S(1)} %add.1.refs_0_, bf16[528,256]{1,0:T(8,128)(2,1)S(1)} %collective-permute-done.6.refs_1_, ...), custom_call_target="tpu_custom_call" | custom-call | flops 1 | tf_op jit(solution)/shard_map/more/pallas_call | solution.py:476
  31.3 2.6 %collective-permute-start.11 = (bf16[2,136,512]{2,1,0:T(8,128)(2,1)S(1)}, bf16[2,136,512]{2,1,0:T(8,128)(2,1)S(1)}, u32[]{:S(2)}, u32[]{:S(2)}) collective-permute-start(bf16[2,136,512]{2,1,0:T(8,128)(2,1)S(1)} %get-tuple-element.38), channel_id=1, source_target_pairs={{2,4},{6,8},{10,12},{14,16},{18,20},{22,24},{26,28},{4,2},{8,6},{1... | collective-permute-start | bytes 835592 | tf_op jit(solution)/shard_map/ppermute | solution.py:494
  34.0 3.3 %conv_own.3 = (f32[4,2,128,128]{3,2,1,0:T(8,128)S(1)}, f32[4,2,128,128]{3,2,1,0:T(8,128)S(1)}) custom-call(bf16[5,144,512]{2,1,0:T(8,128)(2,1)S(1)} %get-tuple-element.33.own.refs_3_.refs_5_, bf16[3,136,512]{2,1,0:T(8,128)(2,1)S(1)} %collective-permute-done.10.near, f32[2,7,7,512]{3,2,1,0:T(8,128)S(1)} %copy.11.taps.refs_4_, f32[2,512]{1,0:T(2,128)S(1)} %copy-done.9), custom_call_target="tpu_custom_call" | custom-call | flops 1 | tf_op jit(solution)/shard_map/conv_own/pallas_call | solution.py:418
  37.3 1.2 %conv_rest.4 = (bf16[256,512]{1,0:T(8,128)(2,1)S(1)}, f32[256,512]{1,0:T(8,128)S(1)}) custom-call(f32[4,2,128,128]{3,2,1,0:T(8,128)S(1)} %get-tuple-element.35.refs_0_, f32[2,512]{1,0:T(2,128)S(1)} %copy-done.7, f32[2,512]{1,0:T(2,128)S(1)} %copy-done.8, bf16[2,512,1024]{2,1,0:T(8,128)(2,1)S(1)} %copy-done, f32[2,1024]{1,0:T(2,128)S(1)} %copy-done.4, ...), custom_call_target="tpu_custom_call" | custom-call | flops 1 | tf_op jit(solution)/shard_map/conv_rest/pallas_call | solution.py:444
  38.5 1.6 %collective-permute-done.12.refs_1_.refs_3_ = bf16[1040,512]{1,0:T(8,128)(2,1)S(1)} collective-permute-done((bf16[1040,512]{1,0:T(8,128)(2,1)S(1)}, bf16[1040,512]{1,0:T(8,128)(2,1)S(1)}, u32[]{:S(2)}, u32[]{:S(2)}) %collective-permute-start.12) | collective-permute-done | bytes 1064992 | tf_op jit(solution)/shard_map/ppermute | solution.py:498
  40.7 1.4 %collective-permute-done.11.refs_0_ = bf16[2,136,512]{2,1,0:T(8,128)(2,1)S(1)} collective-permute-done((bf16[2,136,512]{2,1,0:T(8,128)(2,1)S(1)}, bf16[2,136,512]{2,1,0:T(8,128)(2,1)S(1)}, u32[]{:S(2)}, u32[]{:S(2)}) %collective-permute-start.11) | collective-permute-done | bytes 278560 | tf_op jit(solution)/shard_map/ppermute | solution.py:494
  43.0 1.0 %more.4 = bf16[2,128,512]{2,1,0:T(8,128)(2,1)S(1)} custom-call(bf16[256,512]{1,0:T(8,128)(2,1)S(1)} %get-tuple-element.36.x, f32[256,512]{1,0:T(8,128)S(1)} %get-tuple-element.41.refs_0_, bf16[1040,512]{1,0:T(8,128)(2,1)S(1)} %collective-permute-done.12.refs_1_.refs_3_, bf16[1040,512]{1,0:T(8,128)(2,1)S(1)} %collective-permute-done.13.refs_2_.refs_4_, ...), custom_call_target="tpu_custom_call" | custom-call | flops 1 | tf_op jit(solution)/shard_map/more/pallas_call | solution.py:476
  44.0 1.4 %collective-permute-start.14 = (bf16[2,128,512]{2,1,0:T(8,128)(2,1)S(1)}, bf16[2,128,512]{2,1,0:T(8,128)(2,1)S(1)}, u32[]{:S(2)}, u32[]{:S(2)}) collective-permute-start(bf16[2,128,512]{2,1,0:T(8,128)(2,1)S(1)} %more.4), channel_id=1, source_target_pairs={{0,1},{1,0},{2,3},{3,2},{4,5},{5,4},{6,7},{7,6},{8,9},{9,8},{10,11... | collective-permute-start | bytes 786440 | tf_op jit(solution)/shard_map/ppermute | solution.py:498
  45.4 1.6 %more.5 = bf16[2,128,512]{2,1,0:T(8,128)(2,1)S(1)} custom-call(bf16[256,512]{1,0:T(8,128)(2,1)S(1)} %conv_rest.5.x, bf16[2,512,1024]{2,1,0:T(8,128)(2,1)S(1)} %copy-done, f32[2,1024]{1,0:T(2,128)S(1)} %copy-done.4, bf16[2,1024,512]{2,1,0:T(8,128)(2,1)S(1)} %copy-done.2, bf16[1040,512]{1,0:T(8,128)(2,1)S(1)} %collective-permute-done.12.refs_1_.refs_3_, ...), custom_call_target="tpu_custom_call" | custom-call | flops 1 | tf_op jit(solution)/shard_map/more/pallas_call | solution.py:476
  46.9 0.8 %collective-permute-start.15 = (bf16[2,128,512]{2,1,0:T(8,128)(2,1)S(1)}, bf16[2,128,512]{2,1,0:T(8,128)(2,1)S(1)}, u32[]{:S(2)}, u32[]{:S(2)}) collective-permute-start(bf16[2,128,512]{2,1,0:T(8,128)(2,1)S(1)} %more.5), channel_id=1, source_target_pairs={{0,1},{1,0},{2,3},{3,2},{4,5},{5,4},{6,7},{7,6},{8,9},{9,8},{10,11... | collective-permute-start | bytes 786440 | tf_op jit(solution)/shard_map/ppermute | solution.py:498
  47.7 5.4 %collective-permute-done.14 = bf16[2,128,512]{2,1,0:T(8,128)(2,1)S(1)} collective-permute-done((bf16[2,128,512]{2,1,0:T(8,128)(2,1)S(1)}, bf16[2,128,512]{2,1,0:T(8,128)(2,1)S(1)}, u32[]{:S(2)}, u32[]{:S(2)}) %collective-permute-start.14) | collective-permute-done | bytes 262176 | tf_op jit(solution)/shard_map/ppermute | solution.py:498
  53.2 5.0 %collective-permute-done.15 = bf16[2,128,512]{2,1,0:T(8,128)(2,1)S(1)} collective-permute-done((bf16[2,128,512]{2,1,0:T(8,128)(2,1)S(1)}, bf16[2,128,512]{2,1,0:T(8,128)(2,1)S(1)}, u32[]{:S(2)}, u32[]{:S(2)}) %collective-permute-start.15) | collective-permute-done | bytes 262176 | tf_op jit(solution)/shard_map/ppermute | solution.py:498
  58.5 1.1 %pad_maximum_fusion = bf16[4,256,512]{2,1,0:T(8,128)(2,1)} fusion(bf16[2,256,512]{2,1,0:T(8,128)(2,1)S(1)} %get-tuple-element.44, bf16[2,256,512]{2,1,0:T(8,128)(2,1)S(1)} %get-tuple-element.43), kind=kLoop, calls=%fused_computation | loop fusion | flops 524288 | bytes 2097152 | tf_op jit(solution)/shard_map/concatenate | solution.py:579
  (46 shorter events, 4.8 us)
Async XLA Ops:
  0.0 6.9 %copy-start = (bf16[2,512,1024]{2,1,0:T(8,128)(2,1)S(1)}, bf16[2,512,1024]{2,1,0:T(8,128)(2,1)}, u32[]{:S(2)}) copy-start(bf16[2,512,1024]{2,1,0:T(8,128)(2,1)} %refs_0_.3) | copy-start | bytes 6291460
  0.0 6.9 %copy-start.4 = (f32[2,1024]{1,0:T(2,128)S(1)}, f32[2,1024]{1,0:T(2,128)}, u32[]{:S(2)}) copy-start(f32[2,1024]{1,0:T(2,128)} %refs_1_.5) | copy-start | bytes 24580
  2.5 10.1 %collective-permute-start.1 = (bf16[3,144,512]{2,1,0:T(8,128)(2,1)}, bf16[3,144,512]{2,1,0:T(8,128)(2,1)S(1)}, u32[]{:S(2)}, u32[]{:S(2)}) collective-permute-start(bf16[3,144,512]{2,1,0:T(8,128)(2,1)} %get-tuple-element.25), channel_id=1, source_target_pairs={{0,2},{2,0},{4,6},{6,4},{8,10},{10,8},{12,14},{14,12},{16,18},{18,... | collective-permute-start | bytes 1327112 | tf_op jit(solution)/shard_map/ppermute | solution.py:489
  2.6 9.6 %collective-permute-start.2 = (bf16[528,256]{1,0:T(8,128)(2,1)}, bf16[528,256]{1,0:T(8,128)(2,1)S(1)}, u32[]{:S(2)}, u32[]{:S(2)}) collective-permute-start(bf16[528,256]{1,0:T(8,128)(2,1)} %get-tuple-element.28), channel_id=1, source_target_pairs={{0,1},{1,0},{2,3},{3,2},{4,5},{5,4},{6,7},{7,6},{8,9},{9,8},{10,11... | collective-permute-start | bytes 811016 | tf_op jit(solution)/shard_map/ppermute | solution.py:498
  4.2 17.7 %collective-permute-start = (bf16[4,144,512]{2,1,0:T(8,128)(2,1)}, bf16[4,144,512]{2,1,0:T(8,128)(2,1)S(1)}, u32[]{:S(2)}, u32[]{:S(2)}) collective-permute-start(bf16[4,144,512]{2,1,0:T(8,128)(2,1)} %get-tuple-element.24), channel_id=1, source_target_pairs={{2,4},{6,8},{10,12},{14,16},{18,20},{22,24},{26,28},{4,2},{8,6},{1... | collective-permute-start | bytes 1769480 | tf_op jit(solution)/shard_map/ppermute | solution.py:494
  6.3 11.4 %collective-permute-start.3 = (bf16[256,512]{1,0:T(8,128)(2,1)}, bf16[256,512]{1,0:T(8,128)(2,1)S(1)}, u32[]{:S(2)}, u32[]{:S(2)}) collective-permute-start(bf16[256,512]{1,0:T(8,128)(2,1)} %get-tuple-element.29), channel_id=1, source_target_pairs={{0,1},{1,0},{2,3},{3,2},{4,5},{5,4},{6,7},{7,6},{8,9},{9,8},{10,11... | collective-permute-start | bytes 786440 | tf_op jit(solution)/shard_map/ppermute | solution.py:498
  8.5 1.8 %copy-start.10 = (f32[2,7,7,512]{3,0,2,1:T(2,128)S(1)}, f32[2,7,7,512]{3,0,2,1:T(2,128)}, u32[]{:S(2)}) copy-start(f32[2,7,7,512]{3,0,2,1:T(2,128)} %param.11) | copy-start | bytes 602116
  8.5 4.1 %copy-start.3 = (bf16[4,256,512]{2,1,0:T(8,128)(2,1)S(1)}, bf16[4,256,512]{2,1,0:T(8,128)(2,1)}, u32[]{:S(2)}) copy-start(bf16[4,256,512]{2,1,0:T(8,128)(2,1)} %refs_5_.5) | copy-start | bytes 3145732
  8.5 4.1 %copy-start.9 = (f32[2,512]{1,0:T(2,128)S(1)}, f32[2,512]{1,0:T(2,128)}, u32[]{:S(2)}) copy-start(f32[2,512]{1,0:T(2,128)} %bias.3) | copy-start | bytes 12292
  8.7 31.4 %collective-permute-start.12 = (bf16[1040,512]{1,0:T(8,128)(2,1)S(1)}, bf16[1040,512]{1,0:T(8,128)(2,1)S(1)}, u32[]{:S(2)}, u32[]{:S(2)}) collective-permute-start(bf16[1040,512]{1,0:T(8,128)(2,1)S(1)} %pack.1), channel_id=1, source_target_pairs={{0,1},{1,0},{2,3},{3,2},{4,5},{5,4},{6,7},{7,6},{8,9},{9,8},{10,11... | collective-permute-start | bytes 3194888 | tf_op jit(solution)/shard_map/ppermute | solution.py:498
  10.3 11.5 %copy-start.2 = (bf16[2,1024,512]{2,1,0:T(8,128)(2,1)S(1)}, bf16[2,1024,512]{2,1,0:T(8,128)(2,1)}, u32[]{:S(2)}) copy-start(bf16[2,1024,512]{2,1,0:T(8,128)(2,1)} %refs_2_.9) | copy-start | bytes 6291460
  10.3 11.5 %copy-start.7 = (f32[2,512]{1,0:T(2,128)S(1)}, f32[2,512]{1,0:T(2,128)}, u32[]{:S(2)}) copy-start(f32[2,512]{1,0:T(2,128)} %refs_2_.8) | copy-start | bytes 12292
  10.4 11.5 %copy-start.8 = (f32[2,512]{1,0:T(2,128)S(1)}, f32[2,512]{1,0:T(2,128)}, u32[]{:S(2)}) copy-start(f32[2,512]{1,0:T(2,128)} %refs_3_.5) | copy-start | bytes 12292
  12.2 14.5 %collective-permute-start.4 = (bf16[528,256]{1,0:T(8,128)(2,1)S(1)}, bf16[528,256]{1,0:T(8,128)(2,1)S(1)}, u32[]{:S(2)}, u32[]{:S(2)}) collective-permute-start(bf16[528,256]{1,0:T(8,128)(2,1)S(1)} %collective-permute-done.2.refs_0_), channel_id=1, source_target_pairs={{0,8},{2,10},{4,12},{6,14},{8,0},{10,2},{12,4},{14,6},{16,24},{18,... | collective-permute-start | bytes 811016 | tf_op jit(solution)/shard_map/ppermute | solution.py:502
  17.8 9.5 %collective-permute-start.5 = (bf16[256,512]{1,0:T(8,128)(2,1)S(1)}, bf16[256,512]{1,0:T(8,128)(2,1)S(1)}, u32[]{:S(2)}, u32[]{:S(2)}) collective-permute-start(bf16[256,512]{1,0:T(8,128)(2,1)S(1)} %collective-permute-done.3.refs_1_), channel_id=1, source_target_pairs={{0,8},{2,10},{4,12},{6,14},{8,0},{10,2},{12,4},{14,6},{16,24},{18,... | collective-permute-start | bytes 786440 | tf_op jit(solution)/shard_map/ppermute | solution.py:502
  18.2 10.7 %collective-permute-start.6 = (bf16[528,256]{1,0:T(8,128)(2,1)S(1)}, bf16[528,256]{1,0:T(8,128)(2,1)S(1)}, u32[]{:S(2)}, u32[]{:S(2)}) collective-permute-start(bf16[528,256]{1,0:T(8,128)(2,1)S(1)} %collective-permute-done.2.refs_0_), channel_id=1, source_target_pairs={{0,2},{2,0},{4,6},{6,4},{8,10},{10,8},{12,14},{14,12},{16,18},{18,... | collective-permute-start | bytes 811016 | tf_op jit(solution)/shard_map/ppermute | solution.py:489
  26.7 2.2 %collective-permute-start.8 = (bf16[528,256]{1,0:T(8,128)(2,1)S(1)}, bf16[528,256]{1,0:T(8,128)(2,1)S(1)}, u32[]{:S(2)}, u32[]{:S(2)}) collective-permute-start(bf16[528,256]{1,0:T(8,128)(2,1)S(1)} %collective-permute-done.4.refs_2_), channel_id=1, source_target_pairs={{0,2},{2,0},{4,6},{6,4},{8,10},{10,8},{12,14},{14,12},{16,18},{18,... | collective-permute-start | bytes 811016 | tf_op jit(solution)/shard_map/ppermute | solution.py:489
  26.8 2.1 %collective-permute-start.7 = (bf16[256,512]{1,0:T(8,128)(2,1)S(1)}, bf16[256,512]{1,0:T(8,128)(2,1)S(1)}, u32[]{:S(2)}, u32[]{:S(2)}) collective-permute-start(bf16[256,512]{1,0:T(8,128)(2,1)S(1)} %collective-permute-done.3.refs_1_), channel_id=1, source_target_pairs={{0,2},{2,0},{4,6},{6,4},{8,10},{10,8},{12,14},{14,12},{16,18},{18,... | collective-permute-start | bytes 786440 | tf_op jit(solution)/shard_map/ppermute | solution.py:489
  27.3 1.8 %collective-permute-start.9 = (bf16[256,512]{1,0:T(8,128)(2,1)S(1)}, bf16[256,512]{1,0:T(8,128)(2,1)S(1)}, u32[]{:S(2)}, u32[]{:S(2)}) collective-permute-start(bf16[256,512]{1,0:T(8,128)(2,1)S(1)} %collective-permute-done.5.refs_3_), channel_id=1, source_target_pairs={{0,2},{2,0},{4,6},{6,4},{8,10},{10,8},{12,14},{14,12},{16,18},{18,... | collective-permute-start | bytes 786440 | tf_op jit(solution)/shard_map/ppermute | solution.py:489
  30.9 3.0 %collective-permute-start.10 = (bf16[3,136,512]{2,1,0:T(8,128)(2,1)S(1)}, bf16[3,136,512]{2,1,0:T(8,128)(2,1)S(1)}, u32[]{:S(2)}, u32[]{:S(2)}) collective-permute-start(bf16[3,136,512]{2,1,0:T(8,128)(2,1)S(1)} %get-tuple-element.34), channel_id=1, source_target_pairs={{0,2},{2,0},{4,6},{6,4},{8,10},{10,8},{12,14},{14,12},{16,18},{18,... | collective-permute-start | bytes 1253384 | tf_op jit(solution)/shard_map/ppermute | solution.py:489
  31.3 10.8 %collective-permute-start.11 = (bf16[2,136,512]{2,1,0:T(8,128)(2,1)S(1)}, bf16[2,136,512]{2,1,0:T(8,128)(2,1)S(1)}, u32[]{:S(2)}, u32[]{:S(2)}) collective-permute-start(bf16[2,136,512]{2,1,0:T(8,128)(2,1)S(1)} %get-tuple-element.38), channel_id=1, source_target_pairs={{2,4},{6,8},{10,12},{14,16},{18,20},{22,24},{26,28},{4,2},{8,6},{1... | collective-permute-start | bytes 835592 | tf_op jit(solution)/shard_map/ppermute | solution.py:494
  40.1 2.9 %collective-permute-start.13 = (bf16[1040,512]{1,0:T(8,128)(2,1)S(1)}, bf16[1040,512]{1,0:T(8,128)(2,1)S(1)}, u32[]{:S(2)}, u32[]{:S(2)}) collective-permute-start(bf16[1040,512]{1,0:T(8,128)(2,1)S(1)} %collective-permute-done.12.refs_1_.refs_3_), channel_id=1, source_target_pairs={{0,2},{2,0},{4,6},{6,4},{8,10},{10,8},{12,14},{14,12},{16,18},{18,... | collective-permute-start | bytes 3194888 | tf_op jit(solution)/shard_map/ppermute | solution.py:489
  44.0 9.2 %collective-permute-start.14 = (bf16[2,128,512]{2,1,0:T(8,128)(2,1)S(1)}, bf16[2,128,512]{2,1,0:T(8,128)(2,1)S(1)}, u32[]{:S(2)}, u32[]{:S(2)}) collective-permute-start(bf16[2,128,512]{2,1,0:T(8,128)(2,1)S(1)} %more.4), channel_id=1, source_target_pairs={{0,1},{1,0},{2,3},{3,2},{4,5},{5,4},{6,7},{7,6},{8,9},{9,8},{10,11... | collective-permute-start | bytes 786440 | tf_op jit(solution)/shard_map/ppermute | solution.py:498
  46.9 11.3 %collective-permute-start.15 = (bf16[2,128,512]{2,1,0:T(8,128)(2,1)S(1)}, bf16[2,128,512]{2,1,0:T(8,128)(2,1)S(1)}, u32[]{:S(2)}, u32[]{:S(2)}) collective-permute-start(bf16[2,128,512]{2,1,0:T(8,128)(2,1)S(1)} %more.5), channel_id=1, source_target_pairs={{0,1},{1,0},{2,3},{3,2},{4,5},{5,4},{6,7},{7,6},{8,9},{9,8},{10,11... | collective-permute-start | bytes 786440 | tf_op jit(solution)/shard_map/ppermute | solution.py:498
  (3 other events, 5.0 us)

commit v5 on v4

--- a/solution.py
+++ b/solution.py
@@ -20,7 +20,7 @@
 VMEM = pl.BlockSpec(memory_space=pltpu.VMEM)
 HBM = pl.BlockSpec(memory_space=pltpu.HBM)
 PARAMS = pltpu.CompilerParams(vmem_limit_bytes=20 * 1024 * 1024)
-COPIES = pltpu.CompilerParams(vmem_limit_bytes=60 * 1024 * 1024)
+COPIES = pltpu.CompilerParams(vmem_limit_bytes=61 * 1024 * 1024)
 
 
 def twice_gelu(u):
@@ -330,6 +330,8 @@
     for side, out in zip((place[2], 1 - place[2]), outs):
         count = out.shape[0]
         sources.append(features.at[pl.ds(side * (layout.rows - count), count), at])
+    if outs[0].shape[0] == layout.rows:
+        sources.pop()
     if weights:
         channels = layout.channels
         hidden, taken = take(0, place, weights, 4, stages[2].at[:channels], stages[3])
@@ -345,9 +347,13 @@
     else:
         rest = start(list(zip(sources, stages)), sems.at[1])
         legs = []
-    for n, copy in enumerate(rest):
-        copy.wait()
-        legs += start([(stages[n], outs[n])], sems.at[4 + n])
+    rest[0].wait()
+    if outs[0].shape[0] == layout.rows:
+        inner = stages[0].at[pl.ds((1 - place[2]) * (layout.rows - layout.reach), layout.reach)]
+    else:
+        rest[1].wait()
+        inner = stages[1]
+    legs += start([(stages[0], outs[0]), (inner, outs[1])], sems.at[4])
     for copy in legs:
         copy.wait()
 
@@ -482,6 +488,38 @@
         compiler_params=PARAMS,
         cost_estimate=cost(1),
         name="more",
+    )(*args)
+
+
+def assemble_kernel(layout, kinds, *refs):
+    *parts, out, sems = refs
+    parts = parts[len(parts) - len(kinds) :]
+    _, _, odd, *_ = layout.place(layout.blocks - 1)
+    copies = []
+    for part, (outer, other) in zip(parts, kinds):
+        count = part.shape[0]
+        row = jnp.where(odd == outer, layout.rows - count, 0)
+        me = lax.axis_index("hid")
+        column = pl.multiple_of((1 - me if other else me) * layout.width, MARGIN)
+        copies.append((part, out.at[pl.ds(row, count), pl.ds(column, layout.width)]))
+    for copy in start(copies, sems):
+        copy.wait()
+
+
+def assemble(layout, out, parts):
+    anywhere = pl.BlockSpec(memory_space=pl.ANY)
+    shape = (layout.rows, layout.columns, layout.channels)
+    args = ([] if out is None else [out]) + [part for part, *_ in parts]
+    return pl.pallas_call(
+        functools.partial(assemble_kernel, layout, [kind for _, *kind in parts]),
+        out_shape=jax.ShapeDtypeStruct(shape, jnp.bfloat16),
+        in_specs=([] if out is None else [anywhere]) + [VMEM] * len(parts),
+        out_specs=anywhere,
+        scratch_shapes=[pltpu.SemaphoreType.DMA((len(parts),))],
+        input_output_aliases={} if out is None else {0: 0},
+        compiler_params=PARAMS,
+        cost_estimate=cost(1),
+        name="assemble",
     )(*args)
 
 
@@ -554,27 +592,26 @@
                 joined = later
             continue
         first, last = tuple(range(before.shape[1])), tuple(range(before.shape[1], rows))
+        x, total = conv_rest(b, layout, last, None, complete[0], dw_weight, *norm, weights)
+        before, rest = after(before, total), parts if not pairs else None
         if pairs and b == 0:
             kind, parts = "plain", gather(w_up[b], b_up[b], w_down[b])
+            rest = parts
         elif pairs:
-            joined = after(joined, before)
-            kind, parts = "joined", [joined, within(joined)]
-        x, total = conv_rest(b, layout, last, None, complete[0], dw_weight, *norm, weights)
-        before = after(before, total)
+            joined = after(joined, total)
+            kind, rest = "joined", [within(joined)]
+            parts = [joined, *rest]
+            total = add(x, total, kind, [joined])
         x_first, = conv_rest(b, layout, first, far, before, dw_weight, *norm)
         total = after(total, x_first)
-        inner, = more(b, layout, last, x, (total,), kind, parts, state, *ending)
+        inner, = more(b, layout, last, x, (total,), kind, rest, state, *ending)
         outer, = more(b, layout, first, x_first, weights, kind, parts, state, *ending)
     if number == 2:
-        def columns_of(a):
-            other = swap_hid(a)
-            left, right = jnp.where(me == 0, a, other), jnp.where(me == 0, other, a)
-            return jnp.concatenate([left, right], axis=1)
-    elif number == 1:
-        columns_of = lambda a: a
-    else:
-        columns_of = lambda a: lax.all_gather(a, "hid", axis=1, tiled=True)
-    inner, outer = columns_of(inner), columns_of(outer)
+        later = swap_hid(inner), swap_hid(outer)
+        out = assemble(layout, None, [(inner, 0, 0), (outer, 1, 0), (later[0], 0, 1)])
+        return assemble(layout, out, [(later[1], 1, 1)])
+    if number > 2:
+        inner, outer = (lax.all_gather(a, "hid", axis=1, tiled=True) for a in (inner, outer))
     if inner.shape == outer.shape:
         return jnp.concatenate([jnp.where(odd == 1, inner, outer), jnp.where(odd == 1, outer, inner)])
     return jnp.where(odd == 1, jnp.concatenate([inner, outer]), jnp.concatenate([outer, inner]))

time: 60.5 us -> 59.8 us (0.988)
  Pallas kernels: 22.5 us -> 24.5 us
  waiting for transfers between devices: 20.6 us -> 19 us
  other arithmetic: 1.34 us -> 0 us
    pallas_call x0 -> x2, Pallas kernels: none -> 1.61 us  [assemble(): pl.pallas_call(functools.partial(assemble_kernel, layout, [kind for _, *k...]
    ppermute x5, waiting for transfers between devices: 15.2 us -> 13.8 us  [swap_hid(): return lax.ppermute(array, 'hid', [(0, 1), (1, 0)])]
    concatenate x1 -> x0, other arithmetic: 1.06 us -> none  [shards(): jnp.concatenate([jnp.where(odd == 1, inner, outer), jnp.where(odd == 1, o...]
    pallas_call x1 -> x2, Pallas kernels: 1.51 us -> 2.19 us  [add(): pl.pallas_call(functools.partial(add_kernel, kind, x.shape[1]), out_shape...]
  transfers between devices with their start and end apart: 16 -> 16, of which waited for: 9 -> 8; matrix products, arithmetic and copies ran while one was open for 0% -> 0% of each run, Pallas kernels for 32% -> 35%
where the time goes in v5:
time: 59.8 us; the launch traced here: 58.8 us
  Pallas kernels  24.5 us (41%)
  waiting for transfers between devices  19 us (32%)
  starting transfers between devices  13.3 us (22%)
  local copies, waits for them, and re-layouts  1.68 us (3%)
    ppermute x5, waiting for transfers between devices, swap_hid(): return lax.ppermute(array, 'hid', [(0, 1), (1, 0)])  13.8 us
    pallas_call x2, Pallas kernels, conv_own(): pl.pallas_call(functools.partial(own_kernel, b, layout, complete), out_sh...  7.16 us
    pallas_call x3, Pallas kernels, conv_rest(): pl.pallas_call(functools.partial(rest_kernel, b, layout, chosen, bool(wei...  6.77 us
    ppermute x5, starting transfers between devices, swap_hid(): return lax.ppermute(array, 'hid', [(0, 1), (1, 0)])  5.87 us
    ppermute x2, waiting for transfers between devices, across(): lax.ppermute(array, 'row', pairs + [(target, source) for source, target i...  5.07 us
    ppermute x2, starting transfers between devices, across(): lax.ppermute(array, 'row', pairs + [(target, source) for source, target i...  4.82 us
    pallas_call x3, Pallas kernels, more(): pl.pallas_call(functools.partial(more_kernel, b, layout, chosen, kind, le...  4.12 us
    pallas_call x1, Pallas kernels, prepare(): pl.pallas_call(functools.partial(prepare_kernel, layout), out_shape=[jax....  2.5 us
  transfers between devices with their start and end apart: 16, of which 8 were waited for; matrix products, arithmetic and copies ran while one was open for 0% of the time, Pallas kernels for 35%

profile of v5, /device:TPU:12, one launch (start us, length us, event | category | flops | bytes accessed | tf_op | source)
XLA Modules:
  0.0 58.8 jit_solution(16856372745561812800)
XLA Ops:
  0.0 2.5 %prepare.1 = (bf16[4,144,512]{2,1,0:T(8,128)(2,1)}, bf16[3,144,512]{2,1,0:T(8,128)(2,1)}, bf16[528,256]{1,0:T(8,128)(2,1)}, bf16[256,512]{1,0:T(8,128)(2,1)}) custom-call(bf16[4,256,512]{2,1,0:T(8,128)(2,1)} %refs_5_.4, bf16[2,512,1024]{2,1,0:T(8,128)(2,1)} %refs_0_.3, f32[2,1024]{1,0:T(2,128)} %refs_1_.5, bf16[2,1024,512]{2,1,0:T(8,128)(2,1)} %refs_2_.9), custom_call_target="tpu_custom_call" | custom-call | flops 1 | tf_op jit(solution)/shard_map/prepare/pallas_call | solution.py:386
  2.6 1.6 %collective-permute-start.2 = (bf16[528,256]{1,0:T(8,128)(2,1)}, bf16[528,256]{1,0:T(8,128)(2,1)S(1)}, u32[]{:S(2)}, u32[]{:S(2)}) collective-permute-start(bf16[528,256]{1,0:T(8,128)(2,1)} %get-tuple-element.28), channel_id=1, source_target_pairs={{0,1},{1,0},{2,3},{3,2},{4,5},{5,4},{6,7},{7,6},{8,9},{9,8},{10,11... | collective-permute-start | bytes 811016 | tf_op jit(solution)/shard_map/ppermute | solution.py:536
  4.1 2.2 %collective-permute-start = (bf16[4,144,512]{2,1,0:T(8,128)(2,1)}, bf16[4,144,512]{2,1,0:T(8,128)(2,1)S(1)}, u32[]{:S(2)}, u32[]{:S(2)}) collective-permute-start(bf16[4,144,512]{2,1,0:T(8,128)(2,1)} %get-tuple-element.24), channel_id=1, source_target_pairs={{2,4},{6,8},{10,12},{14,16},{18,20},{22,24},{26,28},{4,2},{8,6},{1... | collective-permute-start | bytes 1769480 | tf_op jit(solution)/shard_map/ppermute | solution.py:532
  6.9 1.6 %copy-done.1 = bf16[2,1024,512]{2,1,0:T(8,128)(2,1)S(1)} copy-done((bf16[2,1024,512]{2,1,0:T(8,128)(2,1)S(1)}, bf16[2,1024,512]{2,1,0:T(8,128)(2,1)}, u32[]{:S(2)}) %copy-start.1) | copy-done | bytes 2097176
  8.7 1.6 %collective-permute-start.11 = (bf16[1040,512]{1,0:T(8,128)(2,1)S(1)}, bf16[1040,512]{1,0:T(8,128)(2,1)S(1)}, u32[]{:S(2)}, u32[]{:S(2)}) collective-permute-start(bf16[1040,512]{1,0:T(8,128)(2,1)S(1)} %pack.1), channel_id=1, source_target_pairs={{0,1},{1,0},{2,3},{3,2},{4,5},{5,4},{6,7},{7,6},{8,9},{9,8},{10,11... | collective-permute-start | bytes 3194888 | tf_op jit(solution)/shard_map/ppermute | solution.py:536
  10.4 1.8 %collective-permute-done.2.refs_0_ = bf16[528,256]{1,0:T(8,128)(2,1)S(1)} collective-permute-done((bf16[528,256]{1,0:T(8,128)(2,1)}, bf16[528,256]{1,0:T(8,128)(2,1)S(1)}, u32[]{:S(2)}, u32[]{:S(2)}) %collective-permute-start.2) | collective-permute-done | bytes 270368 | tf_op jit(solution)/shard_map/ppermute | solution.py:536
  12.6 3.8 %conv_own.2.refs_1_ = f32[4,5,144,128]{3,2,1,0:T(8,128)S(1)} custom-call(bf16[4,256,512]{2,1,0:T(8,128)(2,1)S(1)} %copy-done.3, bf16[3,144,512]{2,1,0:T(8,128)(2,1)S(1)} %collective-permute-done.1.near, f32[2,7,7,512]{3,2,1,0:T(8,128)S(1)} %copy.12.taps.refs_4_, f32[2,512]{1,0:T(2,128)S(1)} %copy-done.9), custom_call_target="tpu_custom_call" | custom-call | flops 99999997952 | tf_op jit(solution)/shard_map/conv_own/pallas_call | solution.py:424
  16.4 1.3 %collective-permute-done.3.refs_1_ = bf16[256,512]{1,0:T(8,128)(2,1)S(1)} collective-permute-done((bf16[256,512]{1,0:T(8,128)(2,1)}, bf16[256,512]{1,0:T(8,128)(2,1)S(1)}, u32[]{:S(2)}, u32[]{:S(2)}) %collective-permute-start.3) | collective-permute-done | bytes 262176 | tf_op jit(solution)/shard_map/ppermute | solution.py:536
  18.2 3.6 %collective-permute-done.refs_0_.refs_8_ = bf16[4,144,512]{2,1,0:T(8,128)(2,1)S(1)} collective-permute-done((bf16[4,144,512]{2,1,0:T(8,128)(2,1)}, bf16[4,144,512]{2,1,0:T(8,128)(2,1)S(1)}, u32[]{:S(2)}, u32[]{:S(2)}) %collective-permute-start) | collective-permute-done | bytes 589856 | tf_op jit(solution)/shard_map/ppermute | solution.py:532
  21.9 4.8 %conv_rest.3 = (bf16[720,512]{1,0:T(8,128)(2,1)S(1)}, f32[720,512]{1,0:T(8,128)S(1)}) custom-call(bf16[4,144,512]{2,1,0:T(8,128)(2,1)S(1)} %collective-permute-done.refs_0_.refs_8_, f32[4,5,144,128]{3,2,1,0:T(8,128)S(1)} %conv_own.2.refs_1_, f32[2,512]{1,0:T(2,128)S(1)} %copy-done.7, f32[2,512]{1,0:T(2,128)S(1)} %copy-done.8, ...), custom_call_target="tpu_custom_call" | custom-call | flops 1 | tf_op jit(solution)/shard_map/conv_rest/pallas_call | solution.py:450
  27.4 1.5 %add.2.refs_0_ = f32[720,512]{1,0:T(8,128)S(1)} custom-call(bf16[720,512]{1,0:T(8,128)(2,1)S(1)} %get-tuple-element.26.x, f32[720,512]{1,0:T(8,128)S(1)} %get-tuple-element.27.before, bf16[528,256]{1,0:T(8,128)(2,1)S(1)} %collective-permute-done.2.refs_0_, bf16[256,512]{1,0:T(8,128)(2,1)S(1)} %collective-permute-done.3.refs_1_, ...), custom_call_target="tpu_custom_call" | custom-call | flops 1 | tf_op jit(solution)/shard_map/add/pallas_call | solution.py:463
  29.1 1.9 %more.3 = (bf16[5,144,512]{2,1,0:T(8,128)(2,1)S(1)}, bf16[2,136,512]{2,1,0:T(8,128)(2,1)S(1)}, bf16[3,136,512]{2,1,0:T(8,128)(2,1)S(1)}) custom-call(bf16[720,512]{1,0:T(8,128)(2,1)S(1)} %get-tuple-element.26.x, f32[720,512]{1,0:T(8,128)S(1)} %add.2.refs_0_, bf16[528,256]{1,0:T(8,128)(2,1)S(1)} %collective-permute-done.6.refs_1_, ...), custom_call_target="tpu_custom_call" | custom-call | flops 1 | tf_op jit(solution)/shard_map/more/pallas_call | solution.py:482
  31.3 2.6 %collective-permute-start.12 = (bf16[2,136,512]{2,1,0:T(8,128)(2,1)S(1)}, bf16[2,136,512]{2,1,0:T(8,128)(2,1)S(1)}, u32[]{:S(2)}, u32[]{:S(2)}) collective-permute-start(bf16[2,136,512]{2,1,0:T(8,128)(2,1)S(1)} %get-tuple-element.39), channel_id=1, source_target_pairs={{2,4},{6,8},{10,12},{14,16},{18,20},{22,24},{26,28},{4,2},{8,6},{1... | collective-permute-start | bytes 835592 | tf_op jit(solution)/shard_map/ppermute | solution.py:532
  34.0 3.3 %conv_own.3 = (f32[4,2,128,128]{3,2,1,0:T(8,128)S(1)}, f32[4,2,128,128]{3,2,1,0:T(8,128)S(1)}) custom-call(bf16[5,144,512]{2,1,0:T(8,128)(2,1)S(1)} %get-tuple-element.33.own.refs_2_.refs_5_, bf16[3,136,512]{2,1,0:T(8,128)(2,1)S(1)} %collective-permute-done.10.near, f32[2,7,7,512]{3,2,1,0:T(8,128)S(1)} %copy.12.taps.refs_4_, f32[2,512]{1,0:T(2,128)S(1)} %copy-done.9), custom_call_target="tpu_custom_call" | custom-call | flops 1 | tf_op jit(solution)/shard_map/conv_own/pallas_call | solution.py:424
  37.3 1.2 %conv_rest.4 = (bf16[256,512]{1,0:T(8,128)(2,1)S(1)}, f32[256,512]{1,0:T(8,128)S(1)}) custom-call(f32[4,2,128,128]{3,2,1,0:T(8,128)S(1)} %get-tuple-element.35.refs_0_, f32[2,512]{1,0:T(2,128)S(1)} %copy-done.7, f32[2,512]{1,0:T(2,128)S(1)} %copy-done.8, bf16[2,512,1024]{2,1,0:T(8,128)(2,1)S(1)} %copy-done, f32[2,1024]{1,0:T(2,128)S(1)} %copy-done.4, ...), custom_call_target="tpu_custom_call" | custom-call | flops 1 | tf_op jit(solution)/shard_map/conv_rest/pallas_call | solution.py:450
  38.5 1.6 %collective-permute-done.11.refs_0_.refs_3_ = bf16[1040,512]{1,0:T(8,128)(2,1)S(1)} collective-permute-done((bf16[1040,512]{1,0:T(8,128)(2,1)S(1)}, bf16[1040,512]{1,0:T(8,128)(2,1)S(1)}, u32[]{:S(2)}, u32[]{:S(2)}) %collective-permute-start.11) | collective-permute-done | bytes 1064992 | tf_op jit(solution)/shard_map/ppermute | solution.py:536
  40.7 1.4 %collective-permute-done.12.refs_0_ = bf16[2,136,512]{2,1,0:T(8,128)(2,1)S(1)} collective-permute-done((bf16[2,136,512]{2,1,0:T(8,128)(2,1)S(1)}, bf16[2,136,512]{2,1,0:T(8,128)(2,1)S(1)}, u32[]{:S(2)}, u32[]{:S(2)}) %collective-permute-start.12) | collective-permute-done | bytes 278560 | tf_op jit(solution)/shard_map/ppermute | solution.py:532
  42.1 0.8 %conv_rest.5.x = bf16[256,512]{1,0:T(8,128)(2,1)S(1)} custom-call(bf16[2,136,512]{2,1,0:T(8,128)(2,1)S(1)} %collective-permute-done.12.refs_0_, f32[4,2,128,128]{3,2,1,0:T(8,128)S(1)} %get-tuple-element.41.refs_1_, f32[2,512]{1,0:T(2,128)S(1)} %copy-done.7, f32[2,512]{1,0:T(2,128)S(1)} %copy-done.8, f32[2,7,7,512]{3,2,1,0:T(8,128)S(1)} %copy.12.taps.refs_4_), custom_call_target="tpu_custom_call" | custom-call | flops 99999997952 | tf_op jit(solution)/shard_map/conv_rest/pallas_call | solution.py:450
  44.3 0.8 %collective-permute-start.14 = (bf16[2,128,512]{2,1,0:T(8,128)(2,1)S(1)}, bf16[2,128,512]{2,1,0:T(8,128)(2,1)S(1)}, u32[]{:S(2)}, u32[]{:S(2)}) collective-permute-start(bf16[2,128,512]{2,1,0:T(8,128)(2,1)S(1)} %more.4.refs_0_), channel_id=1, source_target_pairs={{0,1},{1,0},{2,3},{3,2},{4,5},{5,4},{6,7},{7,6},{8,9},{9,8},{10,11... | collective-permute-start | bytes 786440 | tf_op jit(solution)/shard_map/ppermute | solution.py:536
  45.1 1.6 %more.5.refs_1_ = bf16[2,128,512]{2,1,0:T(8,128)(2,1)S(1)} custom-call(bf16[256,512]{1,0:T(8,128)(2,1)S(1)} %conv_rest.5.x, bf16[2,512,1024]{2,1,0:T(8,128)(2,1)S(1)} %copy-done, f32[2,1024]{1,0:T(2,128)S(1)} %copy-done.4, bf16[2,1024,512]{2,1,0:T(8,128)(2,1)S(1)} %copy-done.2, bf16[1040,512]{1,0:T(8,128)(2,1)S(1)} %collective-permute-done.11.refs_0_.refs_3_, ...), custom_call_target="tpu_custom_call" | custom-call | flops 1 | tf_op jit(solution)/shard_map/more/pallas_call | solution.py:482
  46.7 1.4 %collective-permute-start.15 = (bf16[2,128,512]{2,1,0:T(8,128)(2,1)S(1)}, bf16[2,128,512]{2,1,0:T(8,128)(2,1)S(1)}, u32[]{:S(2)}, u32[]{:S(2)}) collective-permute-start(bf16[2,128,512]{2,1,0:T(8,128)(2,1)S(1)} %more.5.refs_1_), channel_id=1, source_target_pairs={{0,1},{1,0},{2,3},{3,2},{4,5},{5,4},{6,7},{7,6},{8,9},{9,8},{10,11... | collective-permute-start | bytes 786440 | tf_op jit(solution)/shard_map/ppermute | solution.py:536
  48.0 5.5 %collective-permute-done.14.refs_2_ = bf16[2,128,512]{2,1,0:T(8,128)(2,1)S(1)} collective-permute-done((bf16[2,128,512]{2,1,0:T(8,128)(2,1)S(1)}, bf16[2,128,512]{2,1,0:T(8,128)(2,1)S(1)}, u32[]{:S(2)}, u32[]{:S(2)}) %collective-permute-start.14) | collective-permute-done | bytes 262176 | tf_op jit(solution)/shard_map/ppermute | solution.py:536
  53.5 0.9 %assemble.2.refs_0_ = bf16[4,256,512]{2,1,0:T(8,128)(2,1)} custom-call(bf16[2,128,512]{2,1,0:T(8,128)(2,1)S(1)} %more.4.refs_0_, bf16[2,128,512]{2,1,0:T(8,128)(2,1)S(1)} %more.5.refs_1_, bf16[2,128,512]{2,1,0:T(8,128)(2,1)S(1)} %collective-permute-done.14.refs_2_), custom_call_target="tpu_custom_call" | custom-call | flops 1 | tf_op jit(solution)/shard_map/assemble/pallas_call | solution.py:513
  54.5 3.5 %collective-permute-done.15.refs_1_ = bf16[2,128,512]{2,1,0:T(8,128)(2,1)S(1)} collective-permute-done((bf16[2,128,512]{2,1,0:T(8,128)(2,1)S(1)}, bf16[2,128,512]{2,1,0:T(8,128)(2,1)S(1)}, u32[]{:S(2)}, u32[]{:S(2)}) %collective-permute-start.15) | collective-permute-done | bytes 262176 | tf_op jit(solution)/shard_map/ppermute | solution.py:536
  (45 shorter events, 5.7 us)
Async XLA Ops:
  0.0 6.9 %copy-start = (bf16[2,512,1024]{2,1,0:T(8,128)(2,1)S(1)}, bf16[2,512,1024]{2,1,0:T(8,128)(2,1)}, u32[]{:S(2)}) copy-start(bf16[2,512,1024]{2,1,0:T(8,128)(2,1)} %refs_0_.3) | copy-start | bytes 6291460
  0.0 6.9 %copy-start.4 = (f32[2,1024]{1,0:T(2,128)S(1)}, f32[2,1024]{1,0:T(2,128)}, u32[]{:S(2)}) copy-start(f32[2,1024]{1,0:T(2,128)} %refs_1_.5) | copy-start | bytes 24580
  2.5 10.1 %collective-permute-start.1 = (bf16[3,144,512]{2,1,0:T(8,128)(2,1)}, bf16[3,144,512]{2,1,0:T(8,128)(2,1)S(1)}, u32[]{:S(2)}, u32[]{:S(2)}) collective-permute-start(bf16[3,144,512]{2,1,0:T(8,128)(2,1)} %get-tuple-element.25), channel_id=1, source_target_pairs={{0,2},{2,0},{4,6},{6,4},{8,10},{10,8},{12,14},{14,12},{16,18},{18,... | collective-permute-start | bytes 1327112 | tf_op jit(solution)/shard_map/ppermute | solution.py:527
  2.6 9.6 %collective-permute-start.2 = (bf16[528,256]{1,0:T(8,128)(2,1)}, bf16[528,256]{1,0:T(8,128)(2,1)S(1)}, u32[]{:S(2)}, u32[]{:S(2)}) collective-permute-start(bf16[528,256]{1,0:T(8,128)(2,1)} %get-tuple-element.28), channel_id=1, source_target_pairs={{0,1},{1,0},{2,3},{3,2},{4,5},{5,4},{6,7},{7,6},{8,9},{9,8},{10,11... | collective-permute-start | bytes 811016 | tf_op jit(solution)/shard_map/ppermute | solution.py:536
  4.1 17.7 %collective-permute-start = (bf16[4,144,512]{2,1,0:T(8,128)(2,1)}, bf16[4,144,512]{2,1,0:T(8,128)(2,1)S(1)}, u32[]{:S(2)}, u32[]{:S(2)}) collective-permute-start(bf16[4,144,512]{2,1,0:T(8,128)(2,1)} %get-tuple-element.24), channel_id=1, source_target_pairs={{2,4},{6,8},{10,12},{14,16},{18,20},{22,24},{26,28},{4,2},{8,6},{1... | collective-permute-start | bytes 1769480 | tf_op jit(solution)/shard_map/ppermute | solution.py:532
  6.3 11.4 %collective-permute-start.3 = (bf16[256,512]{1,0:T(8,128)(2,1)}, bf16[256,512]{1,0:T(8,128)(2,1)S(1)}, u32[]{:S(2)}, u32[]{:S(2)}) collective-permute-start(bf16[256,512]{1,0:T(8,128)(2,1)} %get-tuple-element.29), channel_id=1, source_target_pairs={{0,1},{1,0},{2,3},{3,2},{4,5},{5,4},{6,7},{7,6},{8,9},{9,8},{10,11... | collective-permute-start | bytes 786440 | tf_op jit(solution)/shard_map/ppermute | solution.py:536
  8.5 1.8 %copy-start.10 = (f32[2,7,7,512]{3,0,2,1:T(2,128)S(1)}, f32[2,7,7,512]{3,0,2,1:T(2,128)}, u32[]{:S(2)}) copy-start(f32[2,7,7,512]{3,0,2,1:T(2,128)} %param.11) | copy-start | bytes 602116
  8.5 4.1 %copy-start.3 = (bf16[4,256,512]{2,1,0:T(8,128)(2,1)S(1)}, bf16[4,256,512]{2,1,0:T(8,128)(2,1)}, u32[]{:S(2)}) copy-start(bf16[4,256,512]{2,1,0:T(8,128)(2,1)} %refs_5_.4) | copy-start | bytes 3145732
  8.5 4.1 %copy-start.9 = (f32[2,512]{1,0:T(2,128)S(1)}, f32[2,512]{1,0:T(2,128)}, u32[]{:S(2)}) copy-start(f32[2,512]{1,0:T(2,128)} %bias.3) | copy-start | bytes 12292
  8.7 31.4 %collective-permute-start.11 = (bf16[1040,512]{1,0:T(8,128)(2,1)S(1)}, bf16[1040,512]{1,0:T(8,128)(2,1)S(1)}, u32[]{:S(2)}, u32[]{:S(2)}) collective-permute-start(bf16[1040,512]{1,0:T(8,128)(2,1)S(1)} %pack.1), channel_id=1, source_target_pairs={{0,1},{1,0},{2,3},{3,2},{4,5},{5,4},{6,7},{7,6},{8,9},{9,8},{10,11... | collective-permute-start | bytes 3194888 | tf_op jit(solution)/shard_map/ppermute | solution.py:536
  10.3 11.5 %copy-start.2 = (bf16[2,1024,512]{2,1,0:T(8,128)(2,1)S(1)}, bf16[2,1024,512]{2,1,0:T(8,128)(2,1)}, u32[]{:S(2)}) copy-start(bf16[2,1024,512]{2,1,0:T(8,128)(2,1)} %refs_2_.9) | copy-start | bytes 6291460
  10.3 11.5 %copy-start.7 = (f32[2,512]{1,0:T(2,128)S(1)}, f32[2,512]{1,0:T(2,128)}, u32[]{:S(2)}) copy-start(f32[2,512]{1,0:T(2,128)} %refs_2_.8) | copy-start | bytes 12292
  10.4 11.5 %copy-start.8 = (f32[2,512]{1,0:T(2,128)S(1)}, f32[2,512]{1,0:T(2,128)}, u32[]{:S(2)}) copy-start(f32[2,512]{1,0:T(2,128)} %refs_3_.6) | copy-start | bytes 12292
  12.2 14.5 %collective-permute-start.4 = (bf16[528,256]{1,0:T(8,128)(2,1)S(1)}, bf16[528,256]{1,0:T(8,128)(2,1)S(1)}, u32[]{:S(2)}, u32[]{:S(2)}) collective-permute-start(bf16[528,256]{1,0:T(8,128)(2,1)S(1)} %collective-permute-done.2.refs_0_), channel_id=1, source_target_pairs={{0,8},{2,10},{4,12},{6,14},{8,0},{10,2},{12,4},{14,6},{16,24},{18,... | collective-permute-start | bytes 811016 | tf_op jit(solution)/shard_map/ppermute | solution.py:540
  17.8 9.5 %collective-permute-start.5 = (bf16[256,512]{1,0:T(8,128)(2,1)S(1)}, bf16[256,512]{1,0:T(8,128)(2,1)S(1)}, u32[]{:S(2)}, u32[]{:S(2)}) collective-permute-start(bf16[256,512]{1,0:T(8,128)(2,1)S(1)} %collective-permute-done.3.refs_1_), channel_id=1, source_target_pairs={{0,8},{2,10},{4,12},{6,14},{8,0},{10,2},{12,4},{14,6},{16,24},{18,... | collective-permute-start | bytes 786440 | tf_op jit(solution)/shard_map/ppermute | solution.py:540
  18.2 10.7 %collective-permute-start.6 = (bf16[528,256]{1,0:T(8,128)(2,1)S(1)}, bf16[528,256]{1,0:T(8,128)(2,1)S(1)}, u32[]{:S(2)}, u32[]{:S(2)}) collective-permute-start(bf16[528,256]{1,0:T(8,128)(2,1)S(1)} %collective-permute-done.2.refs_0_), channel_id=1, source_target_pairs={{0,2},{2,0},{4,6},{6,4},{8,10},{10,8},{12,14},{14,12},{16,18},{18,... | collective-permute-start | bytes 811016 | tf_op jit(solution)/shard_map/ppermute | solution.py:527
  26.7 2.2 %collective-permute-start.8 = (bf16[528,256]{1,0:T(8,128)(2,1)S(1)}, bf16[528,256]{1,0:T(8,128)(2,1)S(1)}, u32[]{:S(2)}, u32[]{:S(2)}) collective-permute-start(bf16[528,256]{1,0:T(8,128)(2,1)S(1)} %collective-permute-done.4.refs_2_), channel_id=1, source_target_pairs={{0,2},{2,0},{4,6},{6,4},{8,10},{10,8},{12,14},{14,12},{16,18},{18,... | collective-permute-start | bytes 811016 | tf_op jit(solution)/shard_map/ppermute | solution.py:527
  26.8 2.1 %collective-permute-start.7 = (bf16[256,512]{1,0:T(8,128)(2,1)S(1)}, bf16[256,512]{1,0:T(8,128)(2,1)S(1)}, u32[]{:S(2)}, u32[]{:S(2)}) collective-permute-start(bf16[256,512]{1,0:T(8,128)(2,1)S(1)} %collective-permute-done.3.refs_1_), channel_id=1, source_target_pairs={{0,2},{2,0},{4,6},{6,4},{8,10},{10,8},{12,14},{14,12},{16,18},{18,... | collective-permute-start | bytes 786440 | tf_op jit(solution)/shard_map/ppermute | solution.py:527
  27.3 1.8 %collective-permute-start.9 = (bf16[256,512]{1,0:T(8,128)(2,1)S(1)}, bf16[256,512]{1,0:T(8,128)(2,1)S(1)}, u32[]{:S(2)}, u32[]{:S(2)}) collective-permute-start(bf16[256,512]{1,0:T(8,128)(2,1)S(1)} %collective-permute-done.5.refs_3_), channel_id=1, source_target_pairs={{0,2},{2,0},{4,6},{6,4},{8,10},{10,8},{12,14},{14,12},{16,18},{18,... | collective-permute-start | bytes 786440 | tf_op jit(solution)/shard_map/ppermute | solution.py:527
  30.9 3.0 %collective-permute-start.10 = (bf16[3,136,512]{2,1,0:T(8,128)(2,1)S(1)}, bf16[3,136,512]{2,1,0:T(8,128)(2,1)S(1)}, u32[]{:S(2)}, u32[]{:S(2)}) collective-permute-start(bf16[3,136,512]{2,1,0:T(8,128)(2,1)S(1)} %get-tuple-element.34), channel_id=1, source_target_pairs={{0,2},{2,0},{4,6},{6,4},{8,10},{10,8},{12,14},{14,12},{16,18},{18,... | collective-permute-start | bytes 1253384 | tf_op jit(solution)/shard_map/ppermute | solution.py:527
  31.3 10.8 %collective-permute-start.12 = (bf16[2,136,512]{2,1,0:T(8,128)(2,1)S(1)}, bf16[2,136,512]{2,1,0:T(8,128)(2,1)S(1)}, u32[]{:S(2)}, u32[]{:S(2)}) collective-permute-start(bf16[2,136,512]{2,1,0:T(8,128)(2,1)S(1)} %get-tuple-element.39), channel_id=1, source_target_pairs={{2,4},{6,8},{10,12},{14,16},{18,20},{22,24},{26,28},{4,2},{8,6},{1... | collective-permute-start | bytes 835592 | tf_op jit(solution)/shard_map/ppermute | solution.py:532
  40.1 3.4 %collective-permute-start.13 = (bf16[1040,512]{1,0:T(8,128)(2,1)S(1)}, bf16[1040,512]{1,0:T(8,128)(2,1)S(1)}, u32[]{:S(2)}, u32[]{:S(2)}) collective-permute-start(bf16[1040,512]{1,0:T(8,128)(2,1)S(1)} %collective-permute-done.11.refs_0_.refs_3_), channel_id=1, source_target_pairs={{0,2},{2,0},{4,6},{6,4},{8,10},{10,8},{12,14},{14,12},{16,18},{18,... | collective-permute-start | bytes 3194888 | tf_op jit(solution)/shard_map/ppermute | solution.py:527
  44.3 9.3 %collective-permute-start.14 = (bf16[2,128,512]{2,1,0:T(8,128)(2,1)S(1)}, bf16[2,128,512]{2,1,0:T(8,128)(2,1)S(1)}, u32[]{:S(2)}, u32[]{:S(2)}) collective-permute-start(bf16[2,128,512]{2,1,0:T(8,128)(2,1)S(1)} %more.4.refs_0_), channel_id=1, source_target_pairs={{0,1},{1,0},{2,3},{3,2},{4,5},{5,4},{6,7},{7,6},{8,9},{9,8},{10,11... | collective-permute-start | bytes 786440 | tf_op jit(solution)/shard_map/ppermute | solution.py:536
  46.7 11.3 %collective-permute-start.15 = (bf16[2,128,512]{2,1,0:T(8,128)(2,1)S(1)}, bf16[2,128,512]{2,1,0:T(8,128)(2,1)S(1)}, u32[]{:S(2)}, u32[]{:S(2)}) collective-permute-start(bf16[2,128,512]{2,1,0:T(8,128)(2,1)S(1)} %more.5.refs_1_), channel_id=1, source_target_pairs={{0,1},{1,0},{2,3},{3,2},{4,5},{5,4},{6,7},{7,6},{8,9},{9,8},{10,11... | collective-permute-start | bytes 786440 | tf_op jit(solution)/shard_map/ppermute | solution.py:536
  (3 other events, 5.0 us)

commit v6 on v5

--- a/solution.py
+++ b/solution.py
@@ -227,31 +227,38 @@
         normalise(b, conv, gain, shift, refs[0])
 
 
-def pieces_of(kind, channels, parts):
+def pieces_of(kind, layout, b, parts):
+    channels = layout.channels
     if kind == "plain":
         return [(parts[n], parts[n + 1][...], parts[n + 2]) for n in range(0, len(parts), 3)]
-    pieces = []
-    if kind == "joined":
-        for part in parts:
-            last = part.shape[0] - MARGIN
-            terms = part[last:, :].astype(jnp.float32)
-            pieces.append((part.at[:channels], terms[0:1] + terms[1:2], part.at[channels:last]))
-        return pieces
-    for part, down in zip(parts[::2], parts[1::2]):
+
+    def bias(part):
         terms = part[channels:, :].astype(jnp.float32)
-        pieces.append((part.at[:channels], terms[0:1] + terms[1:2], down))
+        return terms[2 * b : 2 * b + 1] + terms[2 * b + 1 : 2 * b + 2]
+
+    if kind == "pairs":
+        return [(p.at[:channels], bias(p), q) for p, q in zip(parts[::2], parts[1::2])]
+    pieces, parity = [], layout.place(b)[3]
+    for part, mine, other in zip(parts[::3], parts[1::3], parts[2::3]):
+        mine, other = bias(mine), bias(other)
+        halves = jnp.where(parity == 0, mine, other), jnp.where(parity == 0, other, mine)
+        half = mine.shape[1]
+        for n in range(2):
+            columns = slice(n * half, (n + 1) * half)
+            down = part.at[channels + n * half : channels + (n + 1) * half]
+            pieces.append((part.at[:channels, columns], halves[n], down))
     return pieces
 
 
-def add_kernel(kind, channels, x, before, *refs):
-    for piece in pieces_of(kind, channels, refs[:-1]):
+def add_kernel(b, layout, kind, x, before, *refs):
+    for piece in pieces_of(kind, layout, b, refs[:-1]):
         project(x, *piece, refs[-1], before)
         before = refs[-1]
 
 
 def more_kernel(b, layout, chosen, kind, number, begun, x, *refs):
     place = layout.place(b)
-    channels, final = layout.channels, b == layout.blocks - 1
+    final = b == layout.blocks - 1
     refs = list(refs)
     take = lambda count: [refs.pop(0) for _ in range(count)]
     pieces, first = [], None
@@ -266,7 +273,7 @@
     out = refs.pop(0)
     sends = [] if final else take(2)
     total = refs.pop(0)
-    pieces += pieces_of(kind, channels, parts)
+    pieces += pieces_of(kind, layout, b, parts)
     for piece in pieces:
         project(x, *piece, total, first)
         first = total
@@ -297,18 +304,20 @@
 
 
 def take(b, place, weights, parts, up, down):
-    w_up, _, w_down = weights
+    w_up, w_down = weights
     hidden = w_up.shape[2] // parts
     at = place[2] * (w_up.shape[2] // 2) + (place[3] * hidden if parts == 4 else 0)
     at = pl.ds(pl.multiple_of(at, hidden), hidden)
     return at, [(w_up.at[b, :, at], up), (w_down.at[b, at, :], down)]
 
 
-def in_two_terms(value, terms):
+def in_two_terms(value, terms, first=0):
     high = value.astype(jnp.bfloat16).astype(jnp.float32)
     low = (value - high).astype(jnp.bfloat16).astype(jnp.float32)
     row = lax.broadcasted_iota(jnp.int32, terms.shape, 0)
-    terms[...] = jnp.where(row == 0, high, jnp.where(row == 1, low, 0.0)).astype(terms.dtype)
+    rest = terms[...].astype(jnp.float32) if first else 0.0
+    both = jnp.where(row == first, high, jnp.where(row == first + 1, low, rest))
+    terms[...] = both.astype(terms.dtype)
 
 
 def start(copies, sems):
@@ -334,11 +343,12 @@
         sources.pop()
     if weights:
         channels = layout.channels
-        hidden, taken = take(0, place, weights, 4, stages[2].at[:channels], stages[3])
+        hidden, taken = take(0, place, weights[::2], 4, stages[2].at[:channels], stages[3])
         first = start([*taken, (weights[1], bias)], sems.at[0])
         rest = start(list(zip(sources, stages)), sems.at[1])
         first[2].wait()
-        in_two_terms(bias[0:1, hidden], terms)
+        for b in range(layout.blocks):
+            in_two_terms(bias[b : b + 1, hidden], terms, 2 * b)
         first[0].wait()
         legs = [(stages[2].at[:channels], outs[2].at[:channels]), (terms, outs[2].at[channels:])]
         legs = start(legs, sems.at[2])
@@ -358,14 +368,10 @@
         copy.wait()
 
 
-def pack_kernel(b, layout, w_up, b_up, w_down, out, terms, sems):
-    channels, last = layout.channels, out.shape[0] - MARGIN
-    outs = out.at[:channels], out.at[channels:last]
-    hidden, copies = take(b, layout.place(b), (w_up, b_up, w_down), 2, *outs)
-    copies = start(copies, sems.at[0])
-    in_two_terms(b_up[b : b + 1, hidden], terms)
-    copies += start([(terms, out.at[last:])], sems.at[1])
-    for copy in copies:
+def pack_kernel(b, layout, w_up, w_down, out, sems):
+    channels = layout.channels
+    copies = take(b, layout.place(b), (w_up, w_down), 2, out.at[:channels], out.at[channels:])[1]
+    for copy in start(copies, sems):
         copy.wait()
 
 
@@ -397,21 +403,17 @@
 
 def pack(b, layout, weights):
     _, channels, hidden = weights[0].shape
-    hidden //= 2
-    shape = (channels + hidden + MARGIN, channels)
+    shape = (channels + hidden // 2, channels)
     return pl.pallas_call(
         functools.partial(pack_kernel, b, layout),
         out_shape=jax.ShapeDtypeStruct(shape, jnp.bfloat16),
-        in_specs=[HBM, VMEM, HBM],
+        in_specs=[HBM, HBM],
         out_specs=VMEM,
-        scratch_shapes=[
-            pltpu.VMEM((MARGIN, hidden), jnp.bfloat16),
-            pltpu.SemaphoreType.DMA((2, 2)),
-        ],
+        scratch_shapes=[pltpu.SemaphoreType.DMA((2,))],
         compiler_params=PARAMS,
         cost_estimate=cost(1),
         name="pack",
-    )(*weights)
+    )(*weights[::2])
 
 
 def conv_own(b, layout, own, near, taps, bias):
@@ -459,9 +461,9 @@
     )(*args)
 
 
-def add(x, before, kind, parts):
+def add(b, layout, x, before, kind, parts):
     return pl.pallas_call(
-        functools.partial(add_kernel, kind, x.shape[1]),
+        functools.partial(add_kernel, b, layout, kind),
         out_shape=jax.ShapeDtypeStruct(before.shape, jnp.float32),
         in_specs=[VMEM] * (2 + len(parts)),
         out_specs=VMEM,
@@ -581,9 +583,10 @@
                 up_other, down_other = after(up_other, total), after(down_other, total)
                 mine = [up, down, up_other, down_other]
                 kind, parts = "pairs", [within(a) for a in mine]
-                total = add(x, total, kind, mine)
+                biases = mine[::2], parts[::2]
+                total = add(b, layout, x, total, kind, mine)
             elif pairs:
-                kind, parts = "joined", [joined, within(joined)]
+                kind, parts = "joined", [joined, *biases[0], within(joined), *biases[1]]
             state, outer, inner = more(
                 b, layout, chosen, x, (total,), kind, parts, state, *ending, far
             )
@@ -593,15 +596,17 @@
             continue
         first, last = tuple(range(before.shape[1])), tuple(range(before.shape[1], rows))
         x, total = conv_rest(b, layout, last, None, complete[0], dw_weight, *norm, weights)
-        before, rest = after(before, total), parts if not pairs else None
+        rest = None if pairs else parts
         if pairs and b == 0:
             kind, parts = "plain", gather(w_up[b], b_up[b], w_down[b])
             rest = parts
         elif pairs:
             joined = after(joined, total)
-            kind, rest = "joined", [within(joined)]
-            parts = [joined, *rest]
-            total = add(x, total, kind, [joined])
+            kind, rest = "joined", [within(joined), *biases[1]]
+            here = [joined, *biases[0]]
+            parts = here + rest
+            total = add(b, layout, x, total, kind, here)
+        before = after(before, total)
         x_first, = conv_rest(b, layout, first, far, before, dw_weight, *norm)
         total = after(total, x_first)
         inner, = more(b, layout, last, x, (total,), kind, rest, state, *ending)

time: 59.8 us -> 59.4 us (level)
    ppermute x2, waiting for transfers between devices: 5.07 us -> 4.41 us  [across(): lax.ppermute(array, 'row', pairs + [(target, source) for source, target i...]
  transfers between devices with their start and end apart: 16 -> 16, of which waited for: 8 -> 9; matrix products, arithmetic and copies ran while one was open for 0% -> 0% of each run, Pallas kernels for 35% -> 35%
where the time goes in v6:
time: 59.4 us; the launch traced here: 58.8 us
  Pallas kernels  24.5 us (41%)
  waiting for transfers between devices  18.6 us (31%)
  starting transfers between devices  13.6 us (23%)
  local copies, waits for them, and re-layouts  1.68 us (3%)
    ppermute x5, waiting for transfers between devices, swap_hid(): return lax.ppermute(array, 'hid', [(0, 1), (1, 0)])  14 us
    pallas_call x2, Pallas kernels, conv_own(): pl.pallas_call(functools.partial(own_kernel, b, layout, complete), out_sh...  7.16 us
    pallas_call x3, Pallas kernels, conv_rest(): pl.pallas_call(functools.partial(rest_kernel, b, layout, chosen, bool(wei...  6.78 us
    ppermute x5, starting transfers between devices, swap_hid(): return lax.ppermute(array, 'hid', [(0, 1), (1, 0)])  5.88 us
    ppermute x2, starting transfers between devices, across(): lax.ppermute(array, 'row', pairs + [(target, source) for source, target i...  4.82 us
    ppermute x2, waiting for transfers between devices, across(): lax.ppermute(array, 'row', pairs + [(target, source) for source, target i...  4.41 us
    pallas_call x3, Pallas kernels, more(): pl.pallas_call(functools.partial(more_kernel, b, layout, chosen, kind, le...  4.11 us
    pallas_call x1, Pallas kernels, prepare(): pl.pallas_call(functools.partial(prepare_kernel, layout), out_shape=[jax....  2.5 us
  transfers between devices with their start and end apart: 16, of which 9 were waited for; matrix products, arithmetic and copies ran while one was open for 0% of the time, Pallas kernels for 35%

profile of v6, /device:TPU:12, one launch (start us, length us, event | category | flops | bytes accessed | tf_op | source)
XLA Modules:
  0.0 58.8 jit_solution(11647319482254356152)
XLA Ops:
  0.0 2.5 %prepare.1 = (bf16[4,144,512]{2,1,0:T(8,128)(2,1)}, bf16[3,144,512]{2,1,0:T(8,128)(2,1)}, bf16[528,256]{1,0:T(8,128)(2,1)}, bf16[256,512]{1,0:T(8,128)(2,1)}) custom-call(bf16[4,256,512]{2,1,0:T(8,128)(2,1)} %refs_5_.5, bf16[2,512,1024]{2,1,0:T(8,128)(2,1)} %refs_0_.3, f32[2,1024]{1,0:T(2,128)} %refs_1_.5, bf16[2,1024,512]{2,1,0:T(8,128)(2,1)} %refs_2_.9), custom_call_target="tpu_custom_call" | custom-call | flops 1 | tf_op jit(solution)/shard_map/prepare/pallas_call | solution.py:392
  2.6 1.6 %collective-permute-start.2 = (bf16[528,256]{1,0:T(8,128)(2,1)}, bf16[528,256]{1,0:T(8,128)(2,1)S(1)}, u32[]{:S(2)}, u32[]{:S(2)}) collective-permute-start(bf16[528,256]{1,0:T(8,128)(2,1)} %get-tuple-element.28), channel_id=1, source_target_pairs={{0,1},{1,0},{2,3},{3,2},{4,5},{5,4},{6,7},{7,6},{8,9},{9,8},{10,11... | collective-permute-start | bytes 811016 | tf_op jit(solution)/shard_map/ppermute | solution.py:538
  4.1 2.2 %collective-permute-start = (bf16[4,144,512]{2,1,0:T(8,128)(2,1)}, bf16[4,144,512]{2,1,0:T(8,128)(2,1)S(1)}, u32[]{:S(2)}, u32[]{:S(2)}) collective-permute-start(bf16[4,144,512]{2,1,0:T(8,128)(2,1)} %get-tuple-element.24), channel_id=1, source_target_pairs={{2,4},{6,8},{10,12},{14,16},{18,20},{22,24},{26,28},{4,2},{8,6},{1... | collective-permute-start | bytes 1769480 | tf_op jit(solution)/shard_map/ppermute | solution.py:534
  6.9 1.6 %copy-done.1 = bf16[2,1024,512]{2,1,0:T(8,128)(2,1)S(1)} copy-done((bf16[2,1024,512]{2,1,0:T(8,128)(2,1)S(1)}, bf16[2,1024,512]{2,1,0:T(8,128)(2,1)}, u32[]{:S(2)}) %copy-start.1) | copy-done | bytes 2097176
  8.7 1.6 %collective-permute-start.11 = (bf16[1024,512]{1,0:T(8,128)(2,1)S(1)}, bf16[1024,512]{1,0:T(8,128)(2,1)S(1)}, u32[]{:S(2)}, u32[]{:S(2)}) collective-permute-start(bf16[1024,512]{1,0:T(8,128)(2,1)S(1)} %pack.1), channel_id=1, source_target_pairs={{0,1},{1,0},{2,3},{3,2},{4,5},{5,4},{6,7},{7,6},{8,9},{9,8},{10,11... | collective-permute-start | bytes 3145736 | tf_op jit(solution)/shard_map/ppermute | solution.py:538
  10.3 1.8 %collective-permute-done.2.refs_0_.refs_1_.refs_4_ = bf16[528,256]{1,0:T(8,128)(2,1)S(1)} collective-permute-done((bf16[528,256]{1,0:T(8,128)(2,1)}, bf16[528,256]{1,0:T(8,128)(2,1)S(1)}, u32[]{:S(2)}, u32[]{:S(2)}) %collective-permute-start.2) | collective-permute-done | bytes 270368 | tf_op jit(solution)/shard_map/ppermute | solution.py:538
  12.6 3.8 %conv_own.2.refs_1_ = f32[4,5,144,128]{3,2,1,0:T(8,128)S(1)} custom-call(bf16[4,256,512]{2,1,0:T(8,128)(2,1)S(1)} %copy-done.3, bf16[3,144,512]{2,1,0:T(8,128)(2,1)S(1)} %collective-permute-done.1.near, f32[2,7,7,512]{3,2,1,0:T(8,128)S(1)} %copy.12.taps.refs_4_, f32[2,512]{1,0:T(2,128)S(1)} %copy-done.9), custom_call_target="tpu_custom_call" | custom-call | flops 99999997952 | tf_op jit(solution)/shard_map/conv_own/pallas_call | solution.py:426
  16.4 1.3 %collective-permute-done.3.refs_1_ = bf16[256,512]{1,0:T(8,128)(2,1)S(1)} collective-permute-done((bf16[256,512]{1,0:T(8,128)(2,1)}, bf16[256,512]{1,0:T(8,128)(2,1)S(1)}, u32[]{:S(2)}, u32[]{:S(2)}) %collective-permute-start.3) | collective-permute-done | bytes 262176 | tf_op jit(solution)/shard_map/ppermute | solution.py:538
  18.2 3.6 %collective-permute-done.refs_0_.refs_8_ = bf16[4,144,512]{2,1,0:T(8,128)(2,1)S(1)} collective-permute-done((bf16[4,144,512]{2,1,0:T(8,128)(2,1)}, bf16[4,144,512]{2,1,0:T(8,128)(2,1)S(1)}, u32[]{:S(2)}, u32[]{:S(2)}) %collective-permute-start) | collective-permute-done | bytes 589856 | tf_op jit(solution)/shard_map/ppermute | solution.py:534
  21.9 4.8 %conv_rest.3 = (bf16[720,512]{1,0:T(8,128)(2,1)S(1)}, f32[720,512]{1,0:T(8,128)S(1)}) custom-call(bf16[4,144,512]{2,1,0:T(8,128)(2,1)S(1)} %collective-permute-done.refs_0_.refs_8_, f32[4,5,144,128]{3,2,1,0:T(8,128)S(1)} %conv_own.2.refs_1_, f32[2,512]{1,0:T(2,128)S(1)} %copy-done.7, f32[2,512]{1,0:T(2,128)S(1)} %copy-done.8, ...), custom_call_target="tpu_custom_call" | custom-call | flops 1 | tf_op jit(solution)/shard_map/conv_rest/pallas_call | solution.py:452
  27.4 1.5 %add.2.refs_0_ = f32[720,512]{1,0:T(8,128)S(1)} custom-call(bf16[720,512]{1,0:T(8,128)(2,1)S(1)} %get-tuple-element.26.x, f32[720,512]{1,0:T(8,128)S(1)} %get-tuple-element.27.before, bf16[528,256]{1,0:T(8,128)(2,1)S(1)} %collective-permute-done.2.refs_0_.refs_1_.refs_4_, bf16[256,512]{1,0:T(8,128)(2,1)S(1)} %collective-permute-done.3.refs_1_, ...), custom_call_target="tpu_custom_call" | custom-call | flops 1 | tf_op jit(solution)/shard_map/add/pallas_call | solution.py:465
  29.1 1.9 %more.3 = (bf16[5,144,512]{2,1,0:T(8,128)(2,1)S(1)}, bf16[2,136,512]{2,1,0:T(8,128)(2,1)S(1)}, bf16[3,136,512]{2,1,0:T(8,128)(2,1)S(1)}) custom-call(bf16[720,512]{1,0:T(8,128)(2,1)S(1)} %get-tuple-element.26.x, f32[720,512]{1,0:T(8,128)S(1)} %add.2.refs_0_, bf16[528,256]{1,0:T(8,128)(2,1)S(1)} %collective-permute-done.6.refs_1_.refs_2_.refs_7_, ...), custom_call_target="tpu_custom_call" | custom-call | flops 1 | tf_op jit(solution)/shard_map/more/pallas_call | solution.py:484
  31.3 2.6 %collective-permute-start.12 = (bf16[2,136,512]{2,1,0:T(8,128)(2,1)S(1)}, bf16[2,136,512]{2,1,0:T(8,128)(2,1)S(1)}, u32[]{:S(2)}, u32[]{:S(2)}) collective-permute-start(bf16[2,136,512]{2,1,0:T(8,128)(2,1)S(1)} %get-tuple-element.39), channel_id=1, source_target_pairs={{2,4},{6,8},{10,12},{14,16},{18,20},{22,24},{26,28},{4,2},{8,6},{1... | collective-permute-start | bytes 835592 | tf_op jit(solution)/shard_map/ppermute | solution.py:534
  34.0 3.3 %conv_own.3 = (f32[4,2,128,128]{3,2,1,0:T(8,128)S(1)}, f32[4,2,128,128]{3,2,1,0:T(8,128)S(1)}) custom-call(bf16[5,144,512]{2,1,0:T(8,128)(2,1)S(1)} %get-tuple-element.33.own.refs_4_.refs_9_, bf16[3,136,512]{2,1,0:T(8,128)(2,1)S(1)} %collective-permute-done.10.near, f32[2,7,7,512]{3,2,1,0:T(8,128)S(1)} %copy.12.taps.refs_4_, f32[2,512]{1,0:T(2,128)S(1)} %copy-done.9), custom_call_target="tpu_custom_call" | custom-call | flops 1 | tf_op jit(solution)/shard_map/conv_own/pallas_call | solution.py:426
  37.3 1.2 %conv_rest.4 = (bf16[256,512]{1,0:T(8,128)(2,1)S(1)}, f32[256,512]{1,0:T(8,128)S(1)}) custom-call(f32[4,2,128,128]{3,2,1,0:T(8,128)S(1)} %get-tuple-element.35.refs_0_, f32[2,512]{1,0:T(2,128)S(1)} %copy-done.7, f32[2,512]{1,0:T(2,128)S(1)} %copy-done.8, bf16[2,512,1024]{2,1,0:T(8,128)(2,1)S(1)} %copy-done, f32[2,1024]{1,0:T(2,128)S(1)} %copy-done.4, ...), custom_call_target="tpu_custom_call" | custom-call | flops 1 | tf_op jit(solution)/shard_map/conv_rest/pallas_call | solution.py:452
  38.6 1.2 %collective-permute-done.11.refs_0_.refs_3_ = bf16[1024,512]{1,0:T(8,128)(2,1)S(1)} collective-permute-done((bf16[1024,512]{1,0:T(8,128)(2,1)S(1)}, bf16[1024,512]{1,0:T(8,128)(2,1)S(1)}, u32[]{:S(2)}, u32[]{:S(2)}) %collective-permute-start.11) | collective-permute-done | bytes 1048608 | tf_op jit(solution)/shard_map/ppermute | solution.py:538
  39.8 0.9 %collective-permute-start.13 = (bf16[1024,512]{1,0:T(8,128)(2,1)S(1)}, bf16[1024,512]{1,0:T(8,128)(2,1)S(1)}, u32[]{:S(2)}, u32[]{:S(2)}) collective-permute-start(bf16[1024,512]{1,0:T(8,128)(2,1)S(1)} %collective-permute-done.11.refs_0_.refs_3_), channel_id=1, source_target_pairs={{0,2},{2,0},{4,6},{6,4},{8,10},{10,8},{12,14},{14,12},{16,18},{18,... | collective-permute-start | bytes 3145736 | tf_op jit(solution)/shard_map/ppermute | solution.py:529
  41.4 0.8 %collective-permute-done.12.refs_0_ = bf16[2,136,512]{2,1,0:T(8,128)(2,1)S(1)} collective-permute-done((bf16[2,136,512]{2,1,0:T(8,128)(2,1)S(1)}, bf16[2,136,512]{2,1,0:T(8,128)(2,1)S(1)}, u32[]{:S(2)}, u32[]{:S(2)}) %collective-permute-start.12) | collective-permute-done | bytes 278560 | tf_op jit(solution)/shard_map/ppermute | solution.py:534
  43.7 1.0 %collective-permute-start.14 = (bf16[2,128,512]{2,1,0:T(8,128)(2,1)S(1)}, bf16[2,128,512]{2,1,0:T(8,128)(2,1)S(1)}, u32[]{:S(2)}, u32[]{:S(2)}) collective-permute-start(bf16[2,128,512]{2,1,0:T(8,128)(2,1)S(1)} %more.4.refs_0_), channel_id=1, source_target_pairs={{0,1},{1,0},{2,3},{3,2},{4,5},{5,4},{6,7},{7,6},{8,9},{9,8},{10,11... | collective-permute-start | bytes 786440 | tf_op jit(solution)/shard_map/ppermute | solution.py:538
  44.7 1.6 %more.5.refs_1_ = bf16[2,128,512]{2,1,0:T(8,128)(2,1)S(1)} custom-call(bf16[256,512]{1,0:T(8,128)(2,1)S(1)} %conv_rest.5.x, bf16[2,512,1024]{2,1,0:T(8,128)(2,1)S(1)} %copy-done, f32[2,1024]{1,0:T(2,128)S(1)} %copy-done.4, bf16[2,1024,512]{2,1,0:T(8,128)(2,1)S(1)} %copy-done.2, bf16[1024,512]{1,0:T(8,128)(2,1)S(1)} %collective-permute-done.11.refs_0_.refs_3_, ...), custom_call_target="tpu_custom_call" | custom-call | flops 1 | tf_op jit(solution)/shard_map/more/pallas_call | solution.py:484
  46.3 1.2 %collective-permute-start.15 = (bf16[2,128,512]{2,1,0:T(8,128)(2,1)S(1)}, bf16[2,128,512]{2,1,0:T(8,128)(2,1)S(1)}, u32[]{:S(2)}, u32[]{:S(2)}) collective-permute-start(bf16[2,128,512]{2,1,0:T(8,128)(2,1)S(1)} %more.5.refs_1_), channel_id=1, source_target_pairs={{0,1},{1,0},{2,3},{3,2},{4,5},{5,4},{6,7},{7,6},{8,9},{9,8},{10,11... | collective-permute-start | bytes 786440 | tf_op jit(solution)/shard_map/ppermute | solution.py:538
  47.5 5.4 %collective-permute-done.14.refs_2_ = bf16[2,128,512]{2,1,0:T(8,128)(2,1)S(1)} collective-permute-done((bf16[2,128,512]{2,1,0:T(8,128)(2,1)S(1)}, bf16[2,128,512]{2,1,0:T(8,128)(2,1)S(1)}, u32[]{:S(2)}, u32[]{:S(2)}) %collective-permute-start.14) | collective-permute-done | bytes 262176 | tf_op jit(solution)/shard_map/ppermute | solution.py:538
  52.9 0.9 %assemble.2.refs_0_ = bf16[4,256,512]{2,1,0:T(8,128)(2,1)} custom-call(bf16[2,128,512]{2,1,0:T(8,128)(2,1)S(1)} %more.4.refs_0_, bf16[2,128,512]{2,1,0:T(8,128)(2,1)S(1)} %more.5.refs_1_, bf16[2,128,512]{2,1,0:T(8,128)(2,1)S(1)} %collective-permute-done.14.refs_2_), custom_call_target="tpu_custom_call" | custom-call | flops 1 | tf_op jit(solution)/shard_map/assemble/pallas_call | solution.py:515
  53.8 4.2 %collective-permute-done.15.refs_1_ = bf16[2,128,512]{2,1,0:T(8,128)(2,1)S(1)} collective-permute-done((bf16[2,128,512]{2,1,0:T(8,128)(2,1)S(1)}, bf16[2,128,512]{2,1,0:T(8,128)(2,1)S(1)}, u32[]{:S(2)}, u32[]{:S(2)}) %collective-permute-start.15) | collective-permute-done | bytes 262176 | tf_op jit(solution)/shard_map/ppermute | solution.py:538
  (45 shorter events, 5.9 us)
Async XLA Ops:
  0.0 6.9 %copy-start = (bf16[2,512,1024]{2,1,0:T(8,128)(2,1)S(1)}, bf16[2,512,1024]{2,1,0:T(8,128)(2,1)}, u32[]{:S(2)}) copy-start(bf16[2,512,1024]{2,1,0:T(8,128)(2,1)} %refs_0_.3) | copy-start | bytes 6291460
  2.5 10.1 %collective-permute-start.1 = (bf16[3,144,512]{2,1,0:T(8,128)(2,1)}, bf16[3,144,512]{2,1,0:T(8,128)(2,1)S(1)}, u32[]{:S(2)}, u32[]{:S(2)}) collective-permute-start(bf16[3,144,512]{2,1,0:T(8,128)(2,1)} %get-tuple-element.25), channel_id=1, source_target_pairs={{0,2},{2,0},{4,6},{6,4},{8,10},{10,8},{12,14},{14,12},{16,18},{18,... | collective-permute-start | bytes 1327112 | tf_op jit(solution)/shard_map/ppermute | solution.py:529
  2.6 9.6 %collective-permute-start.2 = (bf16[528,256]{1,0:T(8,128)(2,1)}, bf16[528,256]{1,0:T(8,128)(2,1)S(1)}, u32[]{:S(2)}, u32[]{:S(2)}) collective-permute-start(bf16[528,256]{1,0:T(8,128)(2,1)} %get-tuple-element.28), channel_id=1, source_target_pairs={{0,1},{1,0},{2,3},{3,2},{4,5},{5,4},{6,7},{7,6},{8,9},{9,8},{10,11... | collective-permute-start | bytes 811016 | tf_op jit(solution)/shard_map/ppermute | solution.py:538
  4.1 17.7 %collective-permute-start = (bf16[4,144,512]{2,1,0:T(8,128)(2,1)}, bf16[4,144,512]{2,1,0:T(8,128)(2,1)S(1)}, u32[]{:S(2)}, u32[]{:S(2)}) collective-permute-start(bf16[4,144,512]{2,1,0:T(8,128)(2,1)} %get-tuple-element.24), channel_id=1, source_target_pairs={{2,4},{6,8},{10,12},{14,16},{18,20},{22,24},{26,28},{4,2},{8,6},{1... | collective-permute-start | bytes 1769480 | tf_op jit(solution)/shard_map/ppermute | solution.py:534
  6.3 11.4 %collective-permute-start.3 = (bf16[256,512]{1,0:T(8,128)(2,1)}, bf16[256,512]{1,0:T(8,128)(2,1)S(1)}, u32[]{:S(2)}, u32[]{:S(2)}) collective-permute-start(bf16[256,512]{1,0:T(8,128)(2,1)} %get-tuple-element.29), channel_id=1, source_target_pairs={{0,1},{1,0},{2,3},{3,2},{4,5},{5,4},{6,7},{7,6},{8,9},{9,8},{10,11... | collective-permute-start | bytes 786440 | tf_op jit(solution)/shard_map/ppermute | solution.py:538
  8.5 4.1 %copy-start.3 = (bf16[4,256,512]{2,1,0:T(8,128)(2,1)S(1)}, bf16[4,256,512]{2,1,0:T(8,128)(2,1)}, u32[]{:S(2)}) copy-start(bf16[4,256,512]{2,1,0:T(8,128)(2,1)} %refs_5_.5) | copy-start | bytes 3145732
  8.5 4.1 %copy-start.9 = (f32[2,512]{1,0:T(2,128)S(1)}, f32[2,512]{1,0:T(2,128)}, u32[]{:S(2)}) copy-start(f32[2,512]{1,0:T(2,128)} %bias.3) | copy-start | bytes 12292
  8.7 31.1 %collective-permute-start.11 = (bf16[1024,512]{1,0:T(8,128)(2,1)S(1)}, bf16[1024,512]{1,0:T(8,128)(2,1)S(1)}, u32[]{:S(2)}, u32[]{:S(2)}) collective-permute-start(bf16[1024,512]{1,0:T(8,128)(2,1)S(1)} %pack.1), channel_id=1, source_target_pairs={{0,1},{1,0},{2,3},{3,2},{4,5},{5,4},{6,7},{7,6},{8,9},{9,8},{10,11... | collective-permute-start | bytes 3145736 | tf_op jit(solution)/shard_map/ppermute | solution.py:538
  10.3 11.6 %copy-start.2 = (bf16[2,1024,512]{2,1,0:T(8,128)(2,1)S(1)}, bf16[2,1024,512]{2,1,0:T(8,128)(2,1)}, u32[]{:S(2)}) copy-start(bf16[2,1024,512]{2,1,0:T(8,128)(2,1)} %refs_2_.9) | copy-start | bytes 6291460
  10.3 11.6 %copy-start.4 = (f32[2,1024]{1,0:T(2,128)S(1)}, f32[2,1024]{1,0:T(2,128)}, u32[]{:S(2)}) copy-start(f32[2,1024]{1,0:T(2,128)} %refs_1_.5) | copy-start | bytes 24580
  10.3 11.6 %copy-start.7 = (f32[2,512]{1,0:T(2,128)S(1)}, f32[2,512]{1,0:T(2,128)}, u32[]{:S(2)}) copy-start(f32[2,512]{1,0:T(2,128)} %refs_2_.8) | copy-start | bytes 12292
  10.3 11.6 %copy-start.8 = (f32[2,512]{1,0:T(2,128)S(1)}, f32[2,512]{1,0:T(2,128)}, u32[]{:S(2)}) copy-start(f32[2,512]{1,0:T(2,128)} %refs_3_.5) | copy-start | bytes 12292
  12.1 14.6 %collective-permute-start.4 = (bf16[528,256]{1,0:T(8,128)(2,1)S(1)}, bf16[528,256]{1,0:T(8,128)(2,1)S(1)}, u32[]{:S(2)}, u32[]{:S(2)}) collective-permute-start(bf16[528,256]{1,0:T(8,128)(2,1)S(1)} %collective-permute-done.2.refs_0_.refs_1_.refs_4_), channel_id=1, source_target_pairs={{0,8},{2,10},{4,12},{6,14},{8,0},{10,2},{12,4},{14,6},{16,24},{18,... | collective-permute-start | bytes 811016 | tf_op jit(solution)/shard_map/ppermute | solution.py:542
  17.8 9.5 %collective-permute-start.5 = (bf16[256,512]{1,0:T(8,128)(2,1)S(1)}, bf16[256,512]{1,0:T(8,128)(2,1)S(1)}, u32[]{:S(2)}, u32[]{:S(2)}) collective-permute-start(bf16[256,512]{1,0:T(8,128)(2,1)S(1)} %collective-permute-done.3.refs_1_), channel_id=1, source_target_pairs={{0,8},{2,10},{4,12},{6,14},{8,0},{10,2},{12,4},{14,6},{16,24},{18,... | collective-permute-start | bytes 786440 | tf_op jit(solution)/shard_map/ppermute | solution.py:542
  18.2 10.7 %collective-permute-start.6 = (bf16[528,256]{1,0:T(8,128)(2,1)S(1)}, bf16[528,256]{1,0:T(8,128)(2,1)S(1)}, u32[]{:S(2)}, u32[]{:S(2)}) collective-permute-start(bf16[528,256]{1,0:T(8,128)(2,1)S(1)} %collective-permute-done.2.refs_0_.refs_1_.refs_4_), channel_id=1, source_target_pairs={{0,2},{2,0},{4,6},{6,4},{8,10},{10,8},{12,14},{14,12},{16,18},{18,... | collective-permute-start | bytes 811016 | tf_op jit(solution)/shard_map/ppermute | solution.py:529
  26.7 2.2 %collective-permute-start.8 = (bf16[528,256]{1,0:T(8,128)(2,1)S(1)}, bf16[528,256]{1,0:T(8,128)(2,1)S(1)}, u32[]{:S(2)}, u32[]{:S(2)}) collective-permute-start(bf16[528,256]{1,0:T(8,128)(2,1)S(1)} %collective-permute-done.4.refs_2_.refs_5_), channel_id=1, source_target_pairs={{0,2},{2,0},{4,6},{6,4},{8,10},{10,8},{12,14},{14,12},{16,18},{18,... | collective-permute-start | bytes 811016 | tf_op jit(solution)/shard_map/ppermute | solution.py:529
  26.8 2.1 %collective-permute-start.7 = (bf16[256,512]{1,0:T(8,128)(2,1)S(1)}, bf16[256,512]{1,0:T(8,128)(2,1)S(1)}, u32[]{:S(2)}, u32[]{:S(2)}) collective-permute-start(bf16[256,512]{1,0:T(8,128)(2,1)S(1)} %collective-permute-done.3.refs_1_), channel_id=1, source_target_pairs={{0,2},{2,0},{4,6},{6,4},{8,10},{10,8},{12,14},{14,12},{16,18},{18,... | collective-permute-start | bytes 786440 | tf_op jit(solution)/shard_map/ppermute | solution.py:529
  27.3 1.8 %collective-permute-start.9 = (bf16[256,512]{1,0:T(8,128)(2,1)S(1)}, bf16[256,512]{1,0:T(8,128)(2,1)S(1)}, u32[]{:S(2)}, u32[]{:S(2)}) collective-permute-start(bf16[256,512]{1,0:T(8,128)(2,1)S(1)} %collective-permute-done.5.refs_3_), channel_id=1, source_target_pairs={{0,2},{2,0},{4,6},{6,4},{8,10},{10,8},{12,14},{14,12},{16,18},{18,... | collective-permute-start | bytes 786440 | tf_op jit(solution)/shard_map/ppermute | solution.py:529
  27.4 1.7 %copy-start.6 = (f32[2,512]{1,0:T(2,128)S(1)}, f32[2,512]{1,0:T(2,128)}, u32[]{:S(2)}) copy-start(f32[2,512]{1,0:T(2,128)} %refs_11_.1) | copy-start | bytes 12292
  30.9 3.0 %collective-permute-start.10 = (bf16[3,136,512]{2,1,0:T(8,128)(2,1)S(1)}, bf16[3,136,512]{2,1,0:T(8,128)(2,1)S(1)}, u32[]{:S(2)}, u32[]{:S(2)}) collective-permute-start(bf16[3,136,512]{2,1,0:T(8,128)(2,1)S(1)} %get-tuple-element.34), channel_id=1, source_target_pairs={{0,2},{2,0},{4,6},{6,4},{8,10},{10,8},{12,14},{14,12},{16,18},{18,... | collective-permute-start | bytes 1253384 | tf_op jit(solution)/shard_map/ppermute | solution.py:529
  31.3 10.8 %collective-permute-start.12 = (bf16[2,136,512]{2,1,0:T(8,128)(2,1)S(1)}, bf16[2,136,512]{2,1,0:T(8,128)(2,1)S(1)}, u32[]{:S(2)}, u32[]{:S(2)}) collective-permute-start(bf16[2,136,512]{2,1,0:T(8,128)(2,1)S(1)} %get-tuple-element.39), channel_id=1, source_target_pairs={{2,4},{6,8},{10,12},{14,16},{18,20},{22,24},{26,28},{4,2},{8,6},{1... | collective-permute-start | bytes 835592 | tf_op jit(solution)/shard_map/ppermute | solution.py:534
  39.8 3.2 %collective-permute-start.13 = (bf16[1024,512]{1,0:T(8,128)(2,1)S(1)}, bf16[1024,512]{1,0:T(8,128)(2,1)S(1)}, u32[]{:S(2)}, u32[]{:S(2)}) collective-permute-start(bf16[1024,512]{1,0:T(8,128)(2,1)S(1)} %collective-permute-done.11.refs_0_.refs_3_), channel_id=1, source_target_pairs={{0,2},{2,0},{4,6},{6,4},{8,10},{10,8},{12,14},{14,12},{16,18},{18,... | collective-permute-start | bytes 3145736 | tf_op jit(solution)/shard_map/ppermute | solution.py:529
  43.7 9.2 %collective-permute-start.14 = (bf16[2,128,512]{2,1,0:T(8,128)(2,1)S(1)}, bf16[2,128,512]{2,1,0:T(8,128)(2,1)S(1)}, u32[]{:S(2)}, u32[]{:S(2)}) collective-permute-start(bf16[2,128,512]{2,1,0:T(8,128)(2,1)S(1)} %more.4.refs_0_), channel_id=1, source_target_pairs={{0,1},{1,0},{2,3},{3,2},{4,5},{5,4},{6,7},{7,6},{8,9},{9,8},{10,11... | collective-permute-start | bytes 786440 | tf_op jit(solution)/shard_map/ppermute | solution.py:538
  46.3 11.7 %collective-permute-start.15 = (bf16[2,128,512]{2,1,0:T(8,128)(2,1)S(1)}, bf16[2,128,512]{2,1,0:T(8,128)(2,1)S(1)}, u32[]{:S(2)}, u32[]{:S(2)}) collective-permute-start(bf16[2,128,512]{2,1,0:T(8,128)(2,1)S(1)} %more.5.refs_1_), channel_id=1, source_target_pairs={{0,1},{1,0},{2,3},{3,2},{4,5},{5,4},{6,7},{7,6},{8,9},{9,8},{10,11... | collective-permute-start | bytes 786440 | tf_op jit(solution)/shard_map/ppermute | solution.py:538
  (3 other events, 5.0 us)

commit v7 on v6

--- a/solution.py
+++ b/solution.py
@@ -32,7 +32,7 @@
 
 
 def tile_of(width):
-    return next(s for s in (48, 32, 16) if width % s == 0)
+    return next(s for s in (72, 64, 48, 32, 16) if width % s == 0)
 
 
 class Layout:

time: 59.4 us -> 59.4 us (level)
  no operation moved by 1% of the time
where the time goes in v7:
time: 59.4 us; the launch traced here: 58.8 us
  Pallas kernels  24.5 us (41%)
  waiting for transfers between devices  18.7 us (31%)
  starting transfers between devices  13.6 us (23%)
  local copies, waits for them, and re-layouts  1.68 us (3%)
    ppermute x5, waiting for transfers between devices, swap_hid(): return lax.ppermute(array, 'hid', [(0, 1), (1, 0)])  14 us
    pallas_call x2, Pallas kernels, conv_own(): pl.pallas_call(functools.partial(own_kernel, b, layout, complete), out_sh...  7.14 us
    pallas_call x3, Pallas kernels, conv_rest(): pl.pallas_call(functools.partial(rest_kernel, b, layout, chosen, bool(wei...  6.76 us
    ppermute x5, starting transfers between devices, swap_hid(): return lax.ppermute(array, 'hid', [(0, 1), (1, 0)])  5.88 us
    ppermute x2, starting transfers between devices, across(): lax.ppermute(array, 'row', pairs + [(target, source) for source, target i...  4.82 us
    ppermute x2, waiting for transfers between devices, across(): lax.ppermute(array, 'row', pairs + [(target, source) for source, target i...  4.39 us
    pallas_call x3, Pallas kernels, more(): pl.pallas_call(functools.partial(more_kernel, b, layout, chosen, kind, le...  4.11 us
    pallas_call x1, Pallas kernels, prepare(): pl.pallas_call(functools.partial(prepare_kernel, layout), out_shape=[jax....  2.5 us
  transfers between devices with their start and end apart: 16, of which 9 were waited for; matrix products, arithmetic and copies ran while one was open for 0% of the time, Pallas kernels for 35%

profile of v7, /device:TPU:12, one launch (start us, length us, event | category | flops | bytes accessed | tf_op | source)
XLA Modules:
  0.0 58.8 jit_solution(958657780198655269)
XLA Ops:
  0.0 2.5 %prepare.1 = (bf16[4,144,512]{2,1,0:T(8,128)(2,1)}, bf16[3,144,512]{2,1,0:T(8,128)(2,1)}, bf16[528,256]{1,0:T(8,128)(2,1)}, bf16[256,512]{1,0:T(8,128)(2,1)}) custom-call(bf16[4,256,512]{2,1,0:T(8,128)(2,1)} %refs_5_.5, bf16[2,512,1024]{2,1,0:T(8,128)(2,1)} %refs_0_.3, f32[2,1024]{1,0:T(2,128)} %refs_1_.5, bf16[2,1024,512]{2,1,0:T(8,128)(2,1)} %refs_2_.9), custom_call_target="tpu_custom_call" | custom-call | flops 1 | tf_op jit(solution)/shard_map/prepare/pallas_call | solution.py:392
  2.6 1.6 %collective-permute-start.2 = (bf16[528,256]{1,0:T(8,128)(2,1)}, bf16[528,256]{1,0:T(8,128)(2,1)S(1)}, u32[]{:S(2)}, u32[]{:S(2)}) collective-permute-start(bf16[528,256]{1,0:T(8,128)(2,1)} %get-tuple-element.28), channel_id=1, source_target_pairs={{0,1},{1,0},{2,3},{3,2},{4,5},{5,4},{6,7},{7,6},{8,9},{9,8},{10,11... | collective-permute-start | bytes 811016 | tf_op jit(solution)/shard_map/ppermute | solution.py:538
  4.1 2.2 %collective-permute-start = (bf16[4,144,512]{2,1,0:T(8,128)(2,1)}, bf16[4,144,512]{2,1,0:T(8,128)(2,1)S(1)}, u32[]{:S(2)}, u32[]{:S(2)}) collective-permute-start(bf16[4,144,512]{2,1,0:T(8,128)(2,1)} %get-tuple-element.24), channel_id=1, source_target_pairs={{2,4},{6,8},{10,12},{14,16},{18,20},{22,24},{26,28},{4,2},{8,6},{1... | collective-permute-start | bytes 1769480 | tf_op jit(solution)/shard_map/ppermute | solution.py:534
  6.9 1.6 %copy-done.1 = bf16[2,1024,512]{2,1,0:T(8,128)(2,1)S(1)} copy-done((bf16[2,1024,512]{2,1,0:T(8,128)(2,1)S(1)}, bf16[2,1024,512]{2,1,0:T(8,128)(2,1)}, u32[]{:S(2)}) %copy-start.1) | copy-done | bytes 2097176
  8.7 1.6 %collective-permute-start.11 = (bf16[1024,512]{1,0:T(8,128)(2,1)S(1)}, bf16[1024,512]{1,0:T(8,128)(2,1)S(1)}, u32[]{:S(2)}, u32[]{:S(2)}) collective-permute-start(bf16[1024,512]{1,0:T(8,128)(2,1)S(1)} %pack.1), channel_id=1, source_target_pairs={{0,1},{1,0},{2,3},{3,2},{4,5},{5,4},{6,7},{7,6},{8,9},{9,8},{10,11... | collective-permute-start | bytes 3145736 | tf_op jit(solution)/shard_map/ppermute | solution.py:538
  10.3 1.8 %collective-permute-done.2.refs_0_.refs_1_.refs_4_ = bf16[528,256]{1,0:T(8,128)(2,1)S(1)} collective-permute-done((bf16[528,256]{1,0:T(8,128)(2,1)}, bf16[528,256]{1,0:T(8,128)(2,1)S(1)}, u32[]{:S(2)}, u32[]{:S(2)}) %collective-permute-start.2) | collective-permute-done | bytes 270368 | tf_op jit(solution)/shard_map/ppermute | solution.py:538
  12.6 3.8 %conv_own.2.refs_1_ = f32[4,5,144,128]{3,2,1,0:T(8,128)S(1)} custom-call(bf16[4,256,512]{2,1,0:T(8,128)(2,1)S(1)} %copy-done.3, bf16[3,144,512]{2,1,0:T(8,128)(2,1)S(1)} %collective-permute-done.1.near, f32[2,7,7,512]{3,2,1,0:T(8,128)S(1)} %copy.12.taps.refs_4_, f32[2,512]{1,0:T(2,128)S(1)} %copy-done.9), custom_call_target="tpu_custom_call" | custom-call | flops 99999997952 | tf_op jit(solution)/shard_map/conv_own/pallas_call | solution.py:426
  16.4 1.4 %collective-permute-done.3.refs_1_ = bf16[256,512]{1,0:T(8,128)(2,1)S(1)} collective-permute-done((bf16[256,512]{1,0:T(8,128)(2,1)}, bf16[256,512]{1,0:T(8,128)(2,1)S(1)}, u32[]{:S(2)}, u32[]{:S(2)}) %collective-permute-start.3) | collective-permute-done | bytes 262176 | tf_op jit(solution)/shard_map/ppermute | solution.py:538
  18.2 3.6 %collective-permute-done.refs_0_.refs_8_ = bf16[4,144,512]{2,1,0:T(8,128)(2,1)S(1)} collective-permute-done((bf16[4,144,512]{2,1,0:T(8,128)(2,1)}, bf16[4,144,512]{2,1,0:T(8,128)(2,1)S(1)}, u32[]{:S(2)}, u32[]{:S(2)}) %collective-permute-start) | collective-permute-done | bytes 589856 | tf_op jit(solution)/shard_map/ppermute | solution.py:534
  21.9 4.8 %conv_rest.3 = (bf16[720,512]{1,0:T(8,128)(2,1)S(1)}, f32[720,512]{1,0:T(8,128)S(1)}) custom-call(bf16[4,144,512]{2,1,0:T(8,128)(2,1)S(1)} %collective-permute-done.refs_0_.refs_8_, f32[4,5,144,128]{3,2,1,0:T(8,128)S(1)} %conv_own.2.refs_1_, f32[2,512]{1,0:T(2,128)S(1)} %copy-done.7, f32[2,512]{1,0:T(2,128)S(1)} %copy-done.8, ...), custom_call_target="tpu_custom_call" | custom-call | flops 1 | tf_op jit(solution)/shard_map/conv_rest/pallas_call | solution.py:452
  27.4 1.5 %add.2.refs_0_ = f32[720,512]{1,0:T(8,128)S(1)} custom-call(bf16[720,512]{1,0:T(8,128)(2,1)S(1)} %get-tuple-element.26.x, f32[720,512]{1,0:T(8,128)S(1)} %get-tuple-element.27.before, bf16[528,256]{1,0:T(8,128)(2,1)S(1)} %collective-permute-done.2.refs_0_.refs_1_.refs_4_, bf16[256,512]{1,0:T(8,128)(2,1)S(1)} %collective-permute-done.3.refs_1_, ...), custom_call_target="tpu_custom_call" | custom-call | flops 1 | tf_op jit(solution)/shard_map/add/pallas_call | solution.py:465
  29.1 1.9 %more.3 = (bf16[5,144,512]{2,1,0:T(8,128)(2,1)S(1)}, bf16[2,136,512]{2,1,0:T(8,128)(2,1)S(1)}, bf16[3,136,512]{2,1,0:T(8,128)(2,1)S(1)}) custom-call(bf16[720,512]{1,0:T(8,128)(2,1)S(1)} %get-tuple-element.26.x, f32[720,512]{1,0:T(8,128)S(1)} %add.2.refs_0_, bf16[528,256]{1,0:T(8,128)(2,1)S(1)} %collective-permute-done.6.refs_1_.refs_2_.refs_7_, ...), custom_call_target="tpu_custom_call" | custom-call | flops 1 | tf_op jit(solution)/shard_map/more/pallas_call | solution.py:484
  31.3 2.6 %collective-permute-start.12 = (bf16[2,136,512]{2,1,0:T(8,128)(2,1)S(1)}, bf16[2,136,512]{2,1,0:T(8,128)(2,1)S(1)}, u32[]{:S(2)}, u32[]{:S(2)}) collective-permute-start(bf16[2,136,512]{2,1,0:T(8,128)(2,1)S(1)} %get-tuple-element.39), channel_id=1, source_target_pairs={{2,4},{6,8},{10,12},{14,16},{18,20},{22,24},{26,28},{4,2},{8,6},{1... | collective-permute-start | bytes 835592 | tf_op jit(solution)/shard_map/ppermute | solution.py:534
  34.0 3.3 %conv_own.3 = (f32[4,2,128,128]{3,2,1,0:T(8,128)S(1)}, f32[4,2,128,128]{3,2,1,0:T(8,128)S(1)}) custom-call(bf16[5,144,512]{2,1,0:T(8,128)(2,1)S(1)} %get-tuple-element.33.own.refs_4_.refs_9_, bf16[3,136,512]{2,1,0:T(8,128)(2,1)S(1)} %collective-permute-done.10.near, f32[2,7,7,512]{3,2,1,0:T(8,128)S(1)} %copy.12.taps.refs_4_, f32[2,512]{1,0:T(2,128)S(1)} %copy-done.9), custom_call_target="tpu_custom_call" | custom-call | flops 1 | tf_op jit(solution)/shard_map/conv_own/pallas_call | solution.py:426
  37.3 1.2 %conv_rest.4 = (bf16[256,512]{1,0:T(8,128)(2,1)S(1)}, f32[256,512]{1,0:T(8,128)S(1)}) custom-call(f32[4,2,128,128]{3,2,1,0:T(8,128)S(1)} %get-tuple-element.35.refs_0_, f32[2,512]{1,0:T(2,128)S(1)} %copy-done.7, f32[2,512]{1,0:T(2,128)S(1)} %copy-done.8, bf16[2,512,1024]{2,1,0:T(8,128)(2,1)S(1)} %copy-done, f32[2,1024]{1,0:T(2,128)S(1)} %copy-done.4, ...), custom_call_target="tpu_custom_call" | custom-call | flops 1 | tf_op jit(solution)/shard_map/conv_rest/pallas_call | solution.py:452
  38.5 1.2 %collective-permute-done.11.refs_0_.refs_3_ = bf16[1024,512]{1,0:T(8,128)(2,1)S(1)} collective-permute-done((bf16[1024,512]{1,0:T(8,128)(2,1)S(1)}, bf16[1024,512]{1,0:T(8,128)(2,1)S(1)}, u32[]{:S(2)}, u32[]{:S(2)}) %collective-permute-start.11) | collective-permute-done | bytes 1048608 | tf_op jit(solution)/shard_map/ppermute | solution.py:538
  39.8 0.9 %collective-permute-start.13 = (bf16[1024,512]{1,0:T(8,128)(2,1)S(1)}, bf16[1024,512]{1,0:T(8,128)(2,1)S(1)}, u32[]{:S(2)}, u32[]{:S(2)}) collective-permute-start(bf16[1024,512]{1,0:T(8,128)(2,1)S(1)} %collective-permute-done.11.refs_0_.refs_3_), channel_id=1, source_target_pairs={{0,2},{2,0},{4,6},{6,4},{8,10},{10,8},{12,14},{14,12},{16,18},{18,... | collective-permute-start | bytes 3145736 | tf_op jit(solution)/shard_map/ppermute | solution.py:529
  42.1 0.8 %conv_rest.5.x = bf16[256,512]{1,0:T(8,128)(2,1)S(1)} custom-call(bf16[2,136,512]{2,1,0:T(8,128)(2,1)S(1)} %collective-permute-done.12.refs_0_, f32[4,2,128,128]{3,2,1,0:T(8,128)S(1)} %get-tuple-element.41.refs_1_, f32[2,512]{1,0:T(2,128)S(1)} %copy-done.7, f32[2,512]{1,0:T(2,128)S(1)} %copy-done.8, f32[2,7,7,512]{3,2,1,0:T(8,128)S(1)} %copy.12.taps.refs_4_), custom_call_target="tpu_custom_call" | custom-call | flops 99999997952 | tf_op jit(solution)/shard_map/conv_rest/pallas_call | solution.py:452
  43.7 1.0 %collective-permute-start.14 = (bf16[2,128,512]{2,1,0:T(8,128)(2,1)S(1)}, bf16[2,128,512]{2,1,0:T(8,128)(2,1)S(1)}, u32[]{:S(2)}, u32[]{:S(2)}) collective-permute-start(bf16[2,128,512]{2,1,0:T(8,128)(2,1)S(1)} %more.4.refs_0_), channel_id=1, source_target_pairs={{0,1},{1,0},{2,3},{3,2},{4,5},{5,4},{6,7},{7,6},{8,9},{9,8},{10,11... | collective-permute-start | bytes 786440 | tf_op jit(solution)/shard_map/ppermute | solution.py:538
  44.7 1.6 %more.5.refs_1_ = bf16[2,128,512]{2,1,0:T(8,128)(2,1)S(1)} custom-call(bf16[256,512]{1,0:T(8,128)(2,1)S(1)} %conv_rest.5.x, bf16[2,512,1024]{2,1,0:T(8,128)(2,1)S(1)} %copy-done, f32[2,1024]{1,0:T(2,128)S(1)} %copy-done.4, bf16[2,1024,512]{2,1,0:T(8,128)(2,1)S(1)} %copy-done.2, bf16[1024,512]{1,0:T(8,128)(2,1)S(1)} %collective-permute-done.11.refs_0_.refs_3_, ...), custom_call_target="tpu_custom_call" | custom-call | flops 1 | tf_op jit(solution)/shard_map/more/pallas_call | solution.py:484
  46.3 1.2 %collective-permute-start.15 = (bf16[2,128,512]{2,1,0:T(8,128)(2,1)S(1)}, bf16[2,128,512]{2,1,0:T(8,128)(2,1)S(1)}, u32[]{:S(2)}, u32[]{:S(2)}) collective-permute-start(bf16[2,128,512]{2,1,0:T(8,128)(2,1)S(1)} %more.5.refs_1_), channel_id=1, source_target_pairs={{0,1},{1,0},{2,3},{3,2},{4,5},{5,4},{6,7},{7,6},{8,9},{9,8},{10,11... | collective-permute-start | bytes 786440 | tf_op jit(solution)/shard_map/ppermute | solution.py:538
  47.5 5.5 %collective-permute-done.14.refs_2_ = bf16[2,128,512]{2,1,0:T(8,128)(2,1)S(1)} collective-permute-done((bf16[2,128,512]{2,1,0:T(8,128)(2,1)S(1)}, bf16[2,128,512]{2,1,0:T(8,128)(2,1)S(1)}, u32[]{:S(2)}, u32[]{:S(2)}) %collective-permute-start.14) | collective-permute-done | bytes 262176 | tf_op jit(solution)/shard_map/ppermute | solution.py:538
  52.9 0.9 %assemble.2.refs_0_ = bf16[4,256,512]{2,1,0:T(8,128)(2,1)} custom-call(bf16[2,128,512]{2,1,0:T(8,128)(2,1)S(1)} %more.4.refs_0_, bf16[2,128,512]{2,1,0:T(8,128)(2,1)S(1)} %more.5.refs_1_, bf16[2,128,512]{2,1,0:T(8,128)(2,1)S(1)} %collective-permute-done.14.refs_2_), custom_call_target="tpu_custom_call" | custom-call | flops 1 | tf_op jit(solution)/shard_map/assemble/pallas_call | solution.py:515
  53.8 4.2 %collective-permute-done.15.refs_1_ = bf16[2,128,512]{2,1,0:T(8,128)(2,1)S(1)} collective-permute-done((bf16[2,128,512]{2,1,0:T(8,128)(2,1)S(1)}, bf16[2,128,512]{2,1,0:T(8,128)(2,1)S(1)}, u32[]{:S(2)}, u32[]{:S(2)}) %collective-permute-start.15) | collective-permute-done | bytes 262176 | tf_op jit(solution)/shard_map/ppermute | solution.py:538
  (45 shorter events, 5.9 us)
Async XLA Ops:
  0.0 6.9 %copy-start = (bf16[2,512,1024]{2,1,0:T(8,128)(2,1)S(1)}, bf16[2,512,1024]{2,1,0:T(8,128)(2,1)}, u32[]{:S(2)}) copy-start(bf16[2,512,1024]{2,1,0:T(8,128)(2,1)} %refs_0_.3) | copy-start | bytes 6291460
  2.5 10.1 %collective-permute-start.1 = (bf16[3,144,512]{2,1,0:T(8,128)(2,1)}, bf16[3,144,512]{2,1,0:T(8,128)(2,1)S(1)}, u32[]{:S(2)}, u32[]{:S(2)}) collective-permute-start(bf16[3,144,512]{2,1,0:T(8,128)(2,1)} %get-tuple-element.25), channel_id=1, source_target_pairs={{0,2},{2,0},{4,6},{6,4},{8,10},{10,8},{12,14},{14,12},{16,18},{18,... | collective-permute-start | bytes 1327112 | tf_op jit(solution)/shard_map/ppermute | solution.py:529
  2.6 9.6 %collective-permute-start.2 = (bf16[528,256]{1,0:T(8,128)(2,1)}, bf16[528,256]{1,0:T(8,128)(2,1)S(1)}, u32[]{:S(2)}, u32[]{:S(2)}) collective-permute-start(bf16[528,256]{1,0:T(8,128)(2,1)} %get-tuple-element.28), channel_id=1, source_target_pairs={{0,1},{1,0},{2,3},{3,2},{4,5},{5,4},{6,7},{7,6},{8,9},{9,8},{10,11... | collective-permute-start | bytes 811016 | tf_op jit(solution)/shard_map/ppermute | solution.py:538
  4.1 17.7 %collective-permute-start = (bf16[4,144,512]{2,1,0:T(8,128)(2,1)}, bf16[4,144,512]{2,1,0:T(8,128)(2,1)S(1)}, u32[]{:S(2)}, u32[]{:S(2)}) collective-permute-start(bf16[4,144,512]{2,1,0:T(8,128)(2,1)} %get-tuple-element.24), channel_id=1, source_target_pairs={{2,4},{6,8},{10,12},{14,16},{18,20},{22,24},{26,28},{4,2},{8,6},{1... | collective-permute-start | bytes 1769480 | tf_op jit(solution)/shard_map/ppermute | solution.py:534
  6.3 11.4 %collective-permute-start.3 = (bf16[256,512]{1,0:T(8,128)(2,1)}, bf16[256,512]{1,0:T(8,128)(2,1)S(1)}, u32[]{:S(2)}, u32[]{:S(2)}) collective-permute-start(bf16[256,512]{1,0:T(8,128)(2,1)} %get-tuple-element.29), channel_id=1, source_target_pairs={{0,1},{1,0},{2,3},{3,2},{4,5},{5,4},{6,7},{7,6},{8,9},{9,8},{10,11... | collective-permute-start | bytes 786440 | tf_op jit(solution)/shard_map/ppermute | solution.py:538
  8.5 4.1 %copy-start.3 = (bf16[4,256,512]{2,1,0:T(8,128)(2,1)S(1)}, bf16[4,256,512]{2,1,0:T(8,128)(2,1)}, u32[]{:S(2)}) copy-start(bf16[4,256,512]{2,1,0:T(8,128)(2,1)} %refs_5_.5) | copy-start | bytes 3145732
  8.5 4.1 %copy-start.9 = (f32[2,512]{1,0:T(2,128)S(1)}, f32[2,512]{1,0:T(2,128)}, u32[]{:S(2)}) copy-start(f32[2,512]{1,0:T(2,128)} %bias.3) | copy-start | bytes 12292
  8.7 31.1 %collective-permute-start.11 = (bf16[1024,512]{1,0:T(8,128)(2,1)S(1)}, bf16[1024,512]{1,0:T(8,128)(2,1)S(1)}, u32[]{:S(2)}, u32[]{:S(2)}) collective-permute-start(bf16[1024,512]{1,0:T(8,128)(2,1)S(1)} %pack.1), channel_id=1, source_target_pairs={{0,1},{1,0},{2,3},{3,2},{4,5},{5,4},{6,7},{7,6},{8,9},{9,8},{10,11... | collective-permute-start | bytes 3145736 | tf_op jit(solution)/shard_map/ppermute | solution.py:538
  10.3 11.6 %copy-start.2 = (bf16[2,1024,512]{2,1,0:T(8,128)(2,1)S(1)}, bf16[2,1024,512]{2,1,0:T(8,128)(2,1)}, u32[]{:S(2)}) copy-start(bf16[2,1024,512]{2,1,0:T(8,128)(2,1)} %refs_2_.9) | copy-start | bytes 6291460
  10.3 11.6 %copy-start.4 = (f32[2,1024]{1,0:T(2,128)S(1)}, f32[2,1024]{1,0:T(2,128)}, u32[]{:S(2)}) copy-start(f32[2,1024]{1,0:T(2,128)} %refs_1_.5) | copy-start | bytes 24580
  10.3 11.6 %copy-start.7 = (f32[2,512]{1,0:T(2,128)S(1)}, f32[2,512]{1,0:T(2,128)}, u32[]{:S(2)}) copy-start(f32[2,512]{1,0:T(2,128)} %refs_2_.8) | copy-start | bytes 12292
  10.3 11.6 %copy-start.8 = (f32[2,512]{1,0:T(2,128)S(1)}, f32[2,512]{1,0:T(2,128)}, u32[]{:S(2)}) copy-start(f32[2,512]{1,0:T(2,128)} %refs_3_.5) | copy-start | bytes 12292
  12.1 14.5 %collective-permute-start.4 = (bf16[528,256]{1,0:T(8,128)(2,1)S(1)}, bf16[528,256]{1,0:T(8,128)(2,1)S(1)}, u32[]{:S(2)}, u32[]{:S(2)}) collective-permute-start(bf16[528,256]{1,0:T(8,128)(2,1)S(1)} %collective-permute-done.2.refs_0_.refs_1_.refs_4_), channel_id=1, source_target_pairs={{0,8},{2,10},{4,12},{6,14},{8,0},{10,2},{12,4},{14,6},{16,24},{18,... | collective-permute-start | bytes 811016 | tf_op jit(solution)/shard_map/ppermute | solution.py:542
  17.8 9.5 %collective-permute-start.5 = (bf16[256,512]{1,0:T(8,128)(2,1)S(1)}, bf16[256,512]{1,0:T(8,128)(2,1)S(1)}, u32[]{:S(2)}, u32[]{:S(2)}) collective-permute-start(bf16[256,512]{1,0:T(8,128)(2,1)S(1)} %collective-permute-done.3.refs_1_), channel_id=1, source_target_pairs={{0,8},{2,10},{4,12},{6,14},{8,0},{10,2},{12,4},{14,6},{16,24},{18,... | collective-permute-start | bytes 786440 | tf_op jit(solution)/shard_map/ppermute | solution.py:542
  18.2 10.7 %collective-permute-start.6 = (bf16[528,256]{1,0:T(8,128)(2,1)S(1)}, bf16[528,256]{1,0:T(8,128)(2,1)S(1)}, u32[]{:S(2)}, u32[]{:S(2)}) collective-permute-start(bf16[528,256]{1,0:T(8,128)(2,1)S(1)} %collective-permute-done.2.refs_0_.refs_1_.refs_4_), channel_id=1, source_target_pairs={{0,2},{2,0},{4,6},{6,4},{8,10},{10,8},{12,14},{14,12},{16,18},{18,... | collective-permute-start | bytes 811016 | tf_op jit(solution)/shard_map/ppermute | solution.py:529
  26.7 2.2 %collective-permute-start.8 = (bf16[528,256]{1,0:T(8,128)(2,1)S(1)}, bf16[528,256]{1,0:T(8,128)(2,1)S(1)}, u32[]{:S(2)}, u32[]{:S(2)}) collective-permute-start(bf16[528,256]{1,0:T(8,128)(2,1)S(1)} %collective-permute-done.4.refs_2_.refs_5_), channel_id=1, source_target_pairs={{0,2},{2,0},{4,6},{6,4},{8,10},{10,8},{12,14},{14,12},{16,18},{18,... | collective-permute-start | bytes 811016 | tf_op jit(solution)/shard_map/ppermute | solution.py:529
  26.8 2.1 %collective-permute-start.7 = (bf16[256,512]{1,0:T(8,128)(2,1)S(1)}, bf16[256,512]{1,0:T(8,128)(2,1)S(1)}, u32[]{:S(2)}, u32[]{:S(2)}) collective-permute-start(bf16[256,512]{1,0:T(8,128)(2,1)S(1)} %collective-permute-done.3.refs_1_), channel_id=1, source_target_pairs={{0,2},{2,0},{4,6},{6,4},{8,10},{10,8},{12,14},{14,12},{16,18},{18,... | collective-permute-start | bytes 786440 | tf_op jit(solution)/shard_map/ppermute | solution.py:529
  27.3 1.8 %collective-permute-start.9 = (bf16[256,512]{1,0:T(8,128)(2,1)S(1)}, bf16[256,512]{1,0:T(8,128)(2,1)S(1)}, u32[]{:S(2)}, u32[]{:S(2)}) collective-permute-start(bf16[256,512]{1,0:T(8,128)(2,1)S(1)} %collective-permute-done.5.refs_3_), channel_id=1, source_target_pairs={{0,2},{2,0},{4,6},{6,4},{8,10},{10,8},{12,14},{14,12},{16,18},{18,... | collective-permute-start | bytes 786440 | tf_op jit(solution)/shard_map/ppermute | solution.py:529
  27.4 1.7 %copy-start.6 = (f32[2,512]{1,0:T(2,128)S(1)}, f32[2,512]{1,0:T(2,128)}, u32[]{:S(2)}) copy-start(f32[2,512]{1,0:T(2,128)} %refs_11_.1) | copy-start | bytes 12292
  30.9 3.0 %collective-permute-start.10 = (bf16[3,136,512]{2,1,0:T(8,128)(2,1)S(1)}, bf16[3,136,512]{2,1,0:T(8,128)(2,1)S(1)}, u32[]{:S(2)}, u32[]{:S(2)}) collective-permute-start(bf16[3,136,512]{2,1,0:T(8,128)(2,1)S(1)} %get-tuple-element.34), channel_id=1, source_target_pairs={{0,2},{2,0},{4,6},{6,4},{8,10},{10,8},{12,14},{14,12},{16,18},{18,... | collective-permute-start | bytes 1253384 | tf_op jit(solution)/shard_map/ppermute | solution.py:529
  31.3 10.8 %collective-permute-start.12 = (bf16[2,136,512]{2,1,0:T(8,128)(2,1)S(1)}, bf16[2,136,512]{2,1,0:T(8,128)(2,1)S(1)}, u32[]{:S(2)}, u32[]{:S(2)}) collective-permute-start(bf16[2,136,512]{2,1,0:T(8,128)(2,1)S(1)} %get-tuple-element.39), channel_id=1, source_target_pairs={{2,4},{6,8},{10,12},{14,16},{18,20},{22,24},{26,28},{4,2},{8,6},{1... | collective-permute-start | bytes 835592 | tf_op jit(solution)/shard_map/ppermute | solution.py:534
  39.8 3.2 %collective-permute-start.13 = (bf16[1024,512]{1,0:T(8,128)(2,1)S(1)}, bf16[1024,512]{1,0:T(8,128)(2,1)S(1)}, u32[]{:S(2)}, u32[]{:S(2)}) collective-permute-start(bf16[1024,512]{1,0:T(8,128)(2,1)S(1)} %collective-permute-done.11.refs_0_.refs_3_), channel_id=1, source_target_pairs={{0,2},{2,0},{4,6},{6,4},{8,10},{10,8},{12,14},{14,12},{16,18},{18,... | collective-permute-start | bytes 3145736 | tf_op jit(solution)/shard_map/ppermute | solution.py:529
  43.7 9.2 %collective-permute-start.14 = (bf16[2,128,512]{2,1,0:T(8,128)(2,1)S(1)}, bf16[2,128,512]{2,1,0:T(8,128)(2,1)S(1)}, u32[]{:S(2)}, u32[]{:S(2)}) collective-permute-start(bf16[2,128,512]{2,1,0:T(8,128)(2,1)S(1)} %more.4.refs_0_), channel_id=1, source_target_pairs={{0,1},{1,0},{2,3},{3,2},{4,5},{5,4},{6,7},{7,6},{8,9},{9,8},{10,11... | collective-permute-start | bytes 786440 | tf_op jit(solution)/shard_map/ppermute | solution.py:538
  46.3 11.7 %collective-permute-start.15 = (bf16[2,128,512]{2,1,0:T(8,128)(2,1)S(1)}, bf16[2,128,512]{2,1,0:T(8,128)(2,1)S(1)}, u32[]{:S(2)}, u32[]{:S(2)}) collective-permute-start(bf16[2,128,512]{2,1,0:T(8,128)(2,1)S(1)} %more.5.refs_1_), channel_id=1, source_target_pairs={{0,1},{1,0},{2,3},{3,2},{4,5},{5,4},{6,7},{7,6},{8,9},{9,8},{10,11... | collective-permute-start | bytes 786440 | tf_op jit(solution)/shard_map/ppermute | solution.py:538
  (3 other events, 5.0 us)

commit v8 on v7

--- a/solution.py
+++ b/solution.py
@@ -54,11 +54,10 @@
         return self.reach * (self.blocks - 1 - b), MARGIN
 
     def edge(self, b):
-        return self.reach * (self.blocks - b), 8 if b else MARGIN
+        return self.reach * (self.blocks - b), 8
 
     def extra(self, b):
-        same = self.size(*self.window(0)) == self.size(*self.edge(0))
-        return int(b == 0 and self.blocks > 1 and self.rows > self.reach and same)
+        return int(b == 0 and self.blocks > 1 and self.rows > self.reach)
 
     def own_rows(self, b):
         return range(-self.extra(b - 1), self.rows)
@@ -258,7 +257,7 @@
 
 def more_kernel(b, layout, chosen, kind, number, begun, x, *refs):
     place = layout.place(b)
-    final = b == layout.blocks - 1
+    final, channels = b == layout.blocks - 1, layout.channels
     refs = list(refs)
     take = lambda count: [refs.pop(0) for _ in range(count)]
     pieces, first = [], None
@@ -280,12 +279,16 @@
     count, width, _ = out.shape
     rows, reach = layout.rows, layout.reach
     for n, d in enumerate(chosen):
+        y = 0.5 * first[n * width : (n + 1) * width, :] + b_down[b : b + 1]
         if d < 0:
+            total[n * width : (n + 1) * width, :] = jnp.zeros((width, channels), jnp.float32)
+            at = pl.multiple_of(n * width + place[1] - MARGIN, 8)
             s = far_state[far_row(layout, b, place, -1 - d), :, :].astype(jnp.float32)
+            total[pl.ds(at, far_state.shape[1]), :] = s
+            s = total[n * width : (n + 1) * width, :]
         else:
             at = pl.ds(pl.multiple_of(place[0], MARGIN), width)
             s = state[own_row(layout, b, place, d), at, :].astype(jnp.float32)
-        y = 0.5 * first[n * width : (n + 1) * width, :] + b_down[b : b + 1]
         s = s + scale[b : b + 1] * y
         if final:
             out[jnp.where(place[2] == 1, count - 1 - n, n)] = s.astype(out.dtype)
@@ -329,42 +332,40 @@
 
 def prepare_kernel(layout, features, *refs):
     place = layout.place(0)
-    weights, refs = refs[: 3 if len(refs) > 5 else 0], refs[3 if len(refs) > 5 else 0 :]
-    *refs, sems = refs
+    weights, refs = refs[: 3 if len(refs) > 6 else 0], refs[3 if len(refs) > 6 else 0 :]
+    *refs, stage, moved, row, sems = refs
     if weights:
         *refs, bias, terms = refs
-    outs, stages = list(refs[: len(refs) // 2]), list(refs[len(refs) // 2 :])
-    at = pl.ds(pl.multiple_of(place[6], MARGIN), outs[0].shape[1])
-    sources = []
-    for side, out in zip((place[2], 1 - place[2]), outs):
-        count = out.shape[0]
-        sources.append(features.at[pl.ds(side * (layout.rows - count), count), at])
-    if outs[0].shape[0] == layout.rows:
-        sources.pop()
+        outs, stages = refs[:4], refs[4:]
+    else:
+        outs = refs
+    begin = layout.start(layout.reach * layout.blocks, MARGIN)
+    source = features.at[:, pl.ds(pl.multiple_of(begin, MARGIN), stage.shape[1])]
+    legs = []
     if weights:
         channels = layout.channels
-        hidden, taken = take(0, place, weights[::2], 4, stages[2].at[:channels], stages[3])
+        hidden, taken = take(0, place, weights[::2], 4, stages[0].at[:channels], stages[1])
         first = start([*taken, (weights[1], bias)], sems.at[0])
-        rest = start(list(zip(sources, stages)), sems.at[1])
+    rest = start([(source, stage)], sems.at[1])
+    if weights:
         first[2].wait()
         for b in range(layout.blocks):
             in_two_terms(bias[b : b + 1, hidden], terms, 2 * b)
         first[0].wait()
-        legs = [(stages[2].at[:channels], outs[2].at[:channels]), (terms, outs[2].at[channels:])]
+        legs = [(stages[0].at[:channels], outs[2].at[:channels]), (terms, outs[2].at[channels:])]
         legs = start(legs, sems.at[2])
         first[1].wait()
-        legs += start([(stages[3], outs[3])], sems.at[3])
-    else:
-        rest = start(list(zip(sources, stages)), sems.at[1])
-        legs = []
+        legs += start([(stages[1], outs[3])], sems.at[3])
     rest[0].wait()
-    if outs[0].shape[0] == layout.rows:
-        inner = stages[0].at[pl.ds((1 - place[2]) * (layout.rows - layout.reach), layout.reach)]
-    else:
-        rest[1].wait()
-        inner = stages[1]
-    legs += start([(stages[0], outs[0]), (inner, outs[1])], sems.at[4])
-    for copy in legs:
+    at = pl.ds(pl.multiple_of(place[6] - begin, 8), moved.shape[1])
+    for r in range(layout.rows):
+        row[r] = stage[r].astype(jnp.float32)
+        moved[r] = row[r, at, :].astype(moved.dtype)
+    rows = []
+    for side, out in zip((place[2], 1 - place[2]), outs):
+        count = out.shape[0]
+        rows.append((moved.at[pl.ds(side * (layout.rows - count), count)], out))
+    for copy in legs + start(rows, sems.at[4]):
         copy.wait()
 
 
@@ -383,18 +384,29 @@
     _, size = layout.size(*layout.edge(0))
     channels = layout.channels
     shapes = [(count, size, channels) for count in (len(layout.far_rows(0)), layout.reach)]
-    scratch = [pltpu.SemaphoreType.DMA((6, 3))]
+    _, wide = layout.size(layout.reach * layout.blocks, MARGIN)
+    scratch = [
+        pltpu.VMEM((layout.rows, wide, channels), jnp.bfloat16),
+        pltpu.VMEM((layout.rows, size, channels), jnp.bfloat16),
+        pltpu.VMEM((layout.rows, wide, channels), jnp.float32),
+        pltpu.SemaphoreType.DMA((5, 3)),
+    ]
     if weights:
         hidden = weights[0].shape[2] // 4
-        shapes += [(channels + MARGIN, hidden), (hidden, channels)]
-        scratch.insert(0, pltpu.VMEM((MARGIN, hidden), jnp.bfloat16))
-        scratch.insert(0, pltpu.VMEM(weights[1].shape, jnp.float32))
+        more_shapes = [(channels + MARGIN, hidden), (hidden, channels)]
+        shapes += more_shapes
+        scratch = [
+            *(pltpu.VMEM(shape, jnp.bfloat16) for shape in more_shapes),
+            pltpu.VMEM(weights[1].shape, jnp.float32),
+            pltpu.VMEM((MARGIN, hidden), jnp.bfloat16),
+            *scratch,
+        ]
     return pl.pallas_call(
         functools.partial(prepare_kernel, layout),
         out_shape=[jax.ShapeDtypeStruct(shape, jnp.bfloat16) for shape in shapes],
         in_specs=[HBM] + [HBM] * len(weights),
         out_specs=[HBM] * len(shapes),
-        scratch_shapes=[pltpu.VMEM(shape, jnp.bfloat16) for shape in shapes] + scratch,
+        scratch_shapes=scratch,
         compiler_params=COPIES,
         cost_estimate=cost(1),
         name="prepare",

time: 59.4 us -> 59.5 us (level)
    ppermute x2, waiting for transfers between devices: 4.39 us -> 3.36 us  [across(): lax.ppermute(array, 'row', pairs + [(target, source) for source, target i...]
where the time goes in v8:
time: 59.5 us; the launch traced here: 58.8 us
  Pallas kernels  24.7 us (42%)
  waiting for transfers between devices  18.5 us (31%)
  starting transfers between devices  13.4 us (23%)
  local copies, waits for them, and re-layouts  1.68 us (3%)
    ppermute x5, waiting for transfers between devices, swap_hid(): return lax.ppermute(array, 'hid', [(0, 1), (1, 0)])  14.6 us
    pallas_call x2, Pallas kernels, conv_own(): pl.pallas_call(functools.partial(own_kernel, b, layout, complete), out_sh...  7.15 us
    pallas_call x3, Pallas kernels, conv_rest(): pl.pallas_call(functools.partial(rest_kernel, b, layout, chosen, bool(wei...  6.78 us
    ppermute x5, starting transfers between devices, swap_hid(): return lax.ppermute(array, 'hid', [(0, 1), (1, 0)])  5.88 us
    ppermute x2, starting transfers between devices, across(): lax.ppermute(array, 'row', pairs + [(target, source) for source, target i...  4.81 us
    pallas_call x3, Pallas kernels, more(): pl.pallas_call(functools.partial(more_kernel, b, layout, chosen, kind, le...  4.25 us
    ppermute x2, waiting for transfers between devices, across(): lax.ppermute(array, 'row', pairs + [(target, source) for source, target i...  3.36 us
    pallas_call x1, Pallas kernels, prepare(): pl.pallas_call(functools.partial(prepare_kernel, layout), out_shape=[jax....  2.62 us
  transfers between devices with their start and end apart: 16, of which 9 were waited for; matrix products, arithmetic and copies ran while one was open for 0% of the time, Pallas kernels for 35%

profile of v8, /device:TPU:12, one launch (start us, length us, event | category | flops | bytes accessed | tf_op | source)
XLA Modules:
  0.0 58.8 jit_solution(13356632061121567196)
XLA Ops:
  0.0 2.6 %prepare.1 = (bf16[4,136,512]{2,1,0:T(8,128)(2,1)}, bf16[3,136,512]{2,1,0:T(8,128)(2,1)}, bf16[528,256]{1,0:T(8,128)(2,1)}, bf16[256,512]{1,0:T(8,128)(2,1)}) custom-call(bf16[4,256,512]{2,1,0:T(8,128)(2,1)} %refs_5_.5, bf16[2,512,1024]{2,1,0:T(8,128)(2,1)} %refs_0_.3, f32[2,1024]{1,0:T(2,128)} %refs_1_.5, bf16[2,1024,512]{2,1,0:T(8,128)(2,1)} %refs_2_.9), custom_call_target="tpu_custom_call" | custom-call | flops 1 | tf_op jit(solution)/shard_map/prepare/pallas_call | solution.py:404
  2.7 1.6 %collective-permute-start.2 = (bf16[528,256]{1,0:T(8,128)(2,1)}, bf16[528,256]{1,0:T(8,128)(2,1)S(1)}, u32[]{:S(2)}, u32[]{:S(2)}) collective-permute-start(bf16[528,256]{1,0:T(8,128)(2,1)} %get-tuple-element.28), channel_id=1, source_target_pairs={{0,1},{1,0},{2,3},{3,2},{4,5},{5,4},{6,7},{7,6},{8,9},{9,8},{10,11... | collective-permute-start | bytes 811016 | tf_op jit(solution)/shard_map/ppermute | solution.py:550
  4.3 2.2 %collective-permute-start = (bf16[4,136,512]{2,1,0:T(8,128)(2,1)}, bf16[4,136,512]{2,1,0:T(8,128)(2,1)S(1)}, u32[]{:S(2)}, u32[]{:S(2)}) collective-permute-start(bf16[4,136,512]{2,1,0:T(8,128)(2,1)} %get-tuple-element.24), channel_id=1, source_target_pairs={{2,4},{6,8},{10,12},{14,16},{18,20},{22,24},{26,28},{4,2},{8,6},{1... | collective-permute-start | bytes 1671176 | tf_op jit(solution)/shard_map/ppermute | solution.py:546
  7.1 1.6 %copy-done.1 = bf16[2,1024,512]{2,1,0:T(8,128)(2,1)S(1)} copy-done((bf16[2,1024,512]{2,1,0:T(8,128)(2,1)S(1)}, bf16[2,1024,512]{2,1,0:T(8,128)(2,1)}, u32[]{:S(2)}) %copy-start.1) | copy-done | bytes 2097176
  8.8 1.6 %collective-permute-start.11 = (bf16[1024,512]{1,0:T(8,128)(2,1)S(1)}, bf16[1024,512]{1,0:T(8,128)(2,1)S(1)}, u32[]{:S(2)}, u32[]{:S(2)}) collective-permute-start(bf16[1024,512]{1,0:T(8,128)(2,1)S(1)} %pack.1), channel_id=1, source_target_pairs={{0,1},{1,0},{2,3},{3,2},{4,5},{5,4},{6,7},{7,6},{8,9},{9,8},{10,11... | collective-permute-start | bytes 3145736 | tf_op jit(solution)/shard_map/ppermute | solution.py:550
  10.4 1.8 %collective-permute-done.2.refs_0_.refs_1_.refs_4_ = bf16[528,256]{1,0:T(8,128)(2,1)S(1)} collective-permute-done((bf16[528,256]{1,0:T(8,128)(2,1)}, bf16[528,256]{1,0:T(8,128)(2,1)S(1)}, u32[]{:S(2)}, u32[]{:S(2)}) %collective-permute-start.2) | collective-permute-done | bytes 270368 | tf_op jit(solution)/shard_map/ppermute | solution.py:550
  12.7 3.8 %conv_own.2.refs_1_ = f32[4,5,144,128]{3,2,1,0:T(8,128)S(1)} custom-call(bf16[4,256,512]{2,1,0:T(8,128)(2,1)S(1)} %copy-done.3, bf16[3,136,512]{2,1,0:T(8,128)(2,1)S(1)} %collective-permute-done.1.near, f32[2,7,7,512]{3,2,1,0:T(8,128)S(1)} %copy.12.taps.refs_4_, f32[2,512]{1,0:T(2,128)S(1)} %copy-done.9), custom_call_target="tpu_custom_call" | custom-call | flops 99999997952 | tf_op jit(solution)/shard_map/conv_own/pallas_call | solution.py:438
  16.5 1.3 %collective-permute-done.3.refs_1_ = bf16[256,512]{1,0:T(8,128)(2,1)S(1)} collective-permute-done((bf16[256,512]{1,0:T(8,128)(2,1)}, bf16[256,512]{1,0:T(8,128)(2,1)S(1)}, u32[]{:S(2)}, u32[]{:S(2)}) %collective-permute-start.3) | collective-permute-done | bytes 262176 | tf_op jit(solution)/shard_map/ppermute | solution.py:550
  18.3 2.9 %collective-permute-done.refs_0_.refs_8_ = bf16[4,136,512]{2,1,0:T(8,128)(2,1)S(1)} collective-permute-done((bf16[4,136,512]{2,1,0:T(8,128)(2,1)}, bf16[4,136,512]{2,1,0:T(8,128)(2,1)S(1)}, u32[]{:S(2)}, u32[]{:S(2)}) %collective-permute-start) | collective-permute-done | bytes 557088 | tf_op jit(solution)/shard_map/ppermute | solution.py:546
  21.3 4.8 %conv_rest.3 = (bf16[720,512]{1,0:T(8,128)(2,1)S(1)}, f32[720,512]{1,0:T(8,128)S(1)}) custom-call(bf16[4,136,512]{2,1,0:T(8,128)(2,1)S(1)} %collective-permute-done.refs_0_.refs_8_, f32[4,5,144,128]{3,2,1,0:T(8,128)S(1)} %conv_own.2.refs_1_, f32[2,512]{1,0:T(2,128)S(1)} %copy-done.7, f32[2,512]{1,0:T(2,128)S(1)} %copy-done.8, ...), custom_call_target="tpu_custom_call" | custom-call | flops 1 | tf_op jit(solution)/shard_map/conv_rest/pallas_call | solution.py:464
  26.8 1.5 %add.2.refs_0_ = f32[720,512]{1,0:T(8,128)S(1)} custom-call(bf16[720,512]{1,0:T(8,128)(2,1)S(1)} %get-tuple-element.26.x, f32[720,512]{1,0:T(8,128)S(1)} %get-tuple-element.27.before, bf16[528,256]{1,0:T(8,128)(2,1)S(1)} %collective-permute-done.2.refs_0_.refs_1_.refs_4_, bf16[256,512]{1,0:T(8,128)(2,1)S(1)} %collective-permute-done.3.refs_1_, ...), custom_call_target="tpu_custom_call" | custom-call | flops 1 | tf_op jit(solution)/shard_map/add/pallas_call | solution.py:477
  28.5 2.0 %more.3 = (bf16[5,144,512]{2,1,0:T(8,128)(2,1)S(1)}, bf16[2,136,512]{2,1,0:T(8,128)(2,1)S(1)}, bf16[3,136,512]{2,1,0:T(8,128)(2,1)S(1)}) custom-call(bf16[720,512]{1,0:T(8,128)(2,1)S(1)} %get-tuple-element.26.x, f32[720,512]{1,0:T(8,128)S(1)} %add.2.refs_0_, bf16[528,256]{1,0:T(8,128)(2,1)S(1)} %collective-permute-done.6.refs_1_.refs_2_.refs_7_, ...), custom_call_target="tpu_custom_call" | custom-call | flops 1 | tf_op jit(solution)/shard_map/more/pallas_call | solution.py:496
  30.9 2.6 %collective-permute-start.12 = (bf16[2,136,512]{2,1,0:T(8,128)(2,1)S(1)}, bf16[2,136,512]{2,1,0:T(8,128)(2,1)S(1)}, u32[]{:S(2)}, u32[]{:S(2)}) collective-permute-start(bf16[2,136,512]{2,1,0:T(8,128)(2,1)S(1)} %get-tuple-element.39), channel_id=1, source_target_pairs={{2,4},{6,8},{10,12},{14,16},{18,20},{22,24},{26,28},{4,2},{8,6},{1... | collective-permute-start | bytes 835592 | tf_op jit(solution)/shard_map/ppermute | solution.py:546
  33.5 3.3 %conv_own.3 = (f32[4,2,128,128]{3,2,1,0:T(8,128)S(1)}, f32[4,2,128,128]{3,2,1,0:T(8,128)S(1)}) custom-call(bf16[5,144,512]{2,1,0:T(8,128)(2,1)S(1)} %get-tuple-element.33.own.refs_4_.refs_9_, bf16[3,136,512]{2,1,0:T(8,128)(2,1)S(1)} %collective-permute-done.10.near, f32[2,7,7,512]{3,2,1,0:T(8,128)S(1)} %copy.12.taps.refs_4_, f32[2,512]{1,0:T(2,128)S(1)} %copy-done.9), custom_call_target="tpu_custom_call" | custom-call | flops 1 | tf_op jit(solution)/shard_map/conv_own/pallas_call | solution.py:438
  36.9 1.2 %conv_rest.4 = (bf16[256,512]{1,0:T(8,128)(2,1)S(1)}, f32[256,512]{1,0:T(8,128)S(1)}) custom-call(f32[4,2,128,128]{3,2,1,0:T(8,128)S(1)} %get-tuple-element.35.refs_0_, f32[2,512]{1,0:T(2,128)S(1)} %copy-done.7, f32[2,512]{1,0:T(2,128)S(1)} %copy-done.8, bf16[2,512,1024]{2,1,0:T(8,128)(2,1)S(1)} %copy-done, f32[2,1024]{1,0:T(2,128)S(1)} %copy-done.4, ...), custom_call_target="tpu_custom_call" | custom-call | flops 1 | tf_op jit(solution)/shard_map/conv_rest/pallas_call | solution.py:464
  38.1 1.8 %collective-permute-done.11.refs_0_.refs_3_ = bf16[1024,512]{1,0:T(8,128)(2,1)S(1)} collective-permute-done((bf16[1024,512]{1,0:T(8,128)(2,1)S(1)}, bf16[1024,512]{1,0:T(8,128)(2,1)S(1)}, u32[]{:S(2)}, u32[]{:S(2)}) %collective-permute-start.11) | collective-permute-done | bytes 1048608 | tf_op jit(solution)/shard_map/ppermute | solution.py:550
  39.9 0.7 %collective-permute-start.13 = (bf16[1024,512]{1,0:T(8,128)(2,1)S(1)}, bf16[1024,512]{1,0:T(8,128)(2,1)S(1)}, u32[]{:S(2)}, u32[]{:S(2)}) collective-permute-start(bf16[1024,512]{1,0:T(8,128)(2,1)S(1)} %collective-permute-done.11.refs_0_.refs_3_), channel_id=1, source_target_pairs={{0,2},{2,0},{4,6},{6,4},{8,10},{10,8},{12,14},{14,12},{16,18},{18,... | collective-permute-start | bytes 3145736 | tf_op jit(solution)/shard_map/ppermute | solution.py:541
  41.7 0.8 %conv_rest.5.x = bf16[256,512]{1,0:T(8,128)(2,1)S(1)} custom-call(bf16[2,136,512]{2,1,0:T(8,128)(2,1)S(1)} %collective-permute-done.12.refs_0_, f32[4,2,128,128]{3,2,1,0:T(8,128)S(1)} %get-tuple-element.41.refs_1_, f32[2,512]{1,0:T(2,128)S(1)} %copy-done.7, f32[2,512]{1,0:T(2,128)S(1)} %copy-done.8, f32[2,7,7,512]{3,2,1,0:T(8,128)S(1)} %copy.12.taps.refs_4_), custom_call_target="tpu_custom_call" | custom-call | flops 99999997952 | tf_op jit(solution)/shard_map/conv_rest/pallas_call | solution.py:464
  43.6 1.2 %collective-permute-start.14 = (bf16[2,128,512]{2,1,0:T(8,128)(2,1)S(1)}, bf16[2,128,512]{2,1,0:T(8,128)(2,1)S(1)}, u32[]{:S(2)}, u32[]{:S(2)}) collective-permute-start(bf16[2,128,512]{2,1,0:T(8,128)(2,1)S(1)} %more.4.refs_0_), channel_id=1, source_target_pairs={{0,1},{1,0},{2,3},{3,2},{4,5},{5,4},{6,7},{7,6},{8,9},{9,8},{10,11... | collective-permute-start | bytes 786440 | tf_op jit(solution)/shard_map/ppermute | solution.py:550
  44.8 1.6 %more.5.refs_1_ = bf16[2,128,512]{2,1,0:T(8,128)(2,1)S(1)} custom-call(bf16[256,512]{1,0:T(8,128)(2,1)S(1)} %conv_rest.5.x, bf16[2,512,1024]{2,1,0:T(8,128)(2,1)S(1)} %copy-done, f32[2,1024]{1,0:T(2,128)S(1)} %copy-done.4, bf16[2,1024,512]{2,1,0:T(8,128)(2,1)S(1)} %copy-done.2, bf16[1024,512]{1,0:T(8,128)(2,1)S(1)} %collective-permute-done.11.refs_0_.refs_3_, ...), custom_call_target="tpu_custom_call" | custom-call | flops 1 | tf_op jit(solution)/shard_map/more/pallas_call | solution.py:496
  46.4 1.0 %collective-permute-start.15 = (bf16[2,128,512]{2,1,0:T(8,128)(2,1)S(1)}, bf16[2,128,512]{2,1,0:T(8,128)(2,1)S(1)}, u32[]{:S(2)}, u32[]{:S(2)}) collective-permute-start(bf16[2,128,512]{2,1,0:T(8,128)(2,1)S(1)} %more.5.refs_1_), channel_id=1, source_target_pairs={{0,1},{1,0},{2,3},{3,2},{4,5},{5,4},{6,7},{7,6},{8,9},{9,8},{10,11... | collective-permute-start | bytes 786440 | tf_op jit(solution)/shard_map/ppermute | solution.py:550
  47.4 5.5 %collective-permute-done.14.refs_2_ = bf16[2,128,512]{2,1,0:T(8,128)(2,1)S(1)} collective-permute-done((bf16[2,128,512]{2,1,0:T(8,128)(2,1)S(1)}, bf16[2,128,512]{2,1,0:T(8,128)(2,1)S(1)}, u32[]{:S(2)}, u32[]{:S(2)}) %collective-permute-start.14) | collective-permute-done | bytes 262176 | tf_op jit(solution)/shard_map/ppermute | solution.py:550
  52.8 0.9 %assemble.2.refs_0_ = bf16[4,256,512]{2,1,0:T(8,128)(2,1)} custom-call(bf16[2,128,512]{2,1,0:T(8,128)(2,1)S(1)} %more.4.refs_0_, bf16[2,128,512]{2,1,0:T(8,128)(2,1)S(1)} %more.5.refs_1_, bf16[2,128,512]{2,1,0:T(8,128)(2,1)S(1)} %collective-permute-done.14.refs_2_), custom_call_target="tpu_custom_call" | custom-call | flops 1 | tf_op jit(solution)/shard_map/assemble/pallas_call | solution.py:527
  53.7 4.2 %collective-permute-done.15.refs_1_ = bf16[2,128,512]{2,1,0:T(8,128)(2,1)S(1)} collective-permute-done((bf16[2,128,512]{2,1,0:T(8,128)(2,1)S(1)}, bf16[2,128,512]{2,1,0:T(8,128)(2,1)S(1)}, u32[]{:S(2)}, u32[]{:S(2)}) %collective-permute-start.15) | collective-permute-done | bytes 262176 | tf_op jit(solution)/shard_map/ppermute | solution.py:550
  (45 shorter events, 5.9 us)
Async XLA Ops:
  0.0 7.1 %copy-start = (bf16[2,512,1024]{2,1,0:T(8,128)(2,1)S(1)}, bf16[2,512,1024]{2,1,0:T(8,128)(2,1)}, u32[]{:S(2)}) copy-start(bf16[2,512,1024]{2,1,0:T(8,128)(2,1)} %refs_0_.3) | copy-start | bytes 6291460
  2.6 10.1 %collective-permute-start.1 = (bf16[3,136,512]{2,1,0:T(8,128)(2,1)}, bf16[3,136,512]{2,1,0:T(8,128)(2,1)S(1)}, u32[]{:S(2)}, u32[]{:S(2)}) collective-permute-start(bf16[3,136,512]{2,1,0:T(8,128)(2,1)} %get-tuple-element.25), channel_id=1, source_target_pairs={{0,2},{2,0},{4,6},{6,4},{8,10},{10,8},{12,14},{14,12},{16,18},{18,... | collective-permute-start | bytes 1253384 | tf_op jit(solution)/shard_map/ppermute | solution.py:541
  2.7 9.6 %collective-permute-start.2 = (bf16[528,256]{1,0:T(8,128)(2,1)}, bf16[528,256]{1,0:T(8,128)(2,1)S(1)}, u32[]{:S(2)}, u32[]{:S(2)}) collective-permute-start(bf16[528,256]{1,0:T(8,128)(2,1)} %get-tuple-element.28), channel_id=1, source_target_pairs={{0,1},{1,0},{2,3},{3,2},{4,5},{5,4},{6,7},{7,6},{8,9},{9,8},{10,11... | collective-permute-start | bytes 811016 | tf_op jit(solution)/shard_map/ppermute | solution.py:550
  4.3 17.0 %collective-permute-start = (bf16[4,136,512]{2,1,0:T(8,128)(2,1)}, bf16[4,136,512]{2,1,0:T(8,128)(2,1)S(1)}, u32[]{:S(2)}, u32[]{:S(2)}) collective-permute-start(bf16[4,136,512]{2,1,0:T(8,128)(2,1)} %get-tuple-element.24), channel_id=1, source_target_pairs={{2,4},{6,8},{10,12},{14,16},{18,20},{22,24},{26,28},{4,2},{8,6},{1... | collective-permute-start | bytes 1671176 | tf_op jit(solution)/shard_map/ppermute | solution.py:546
  6.5 11.4 %collective-permute-start.3 = (bf16[256,512]{1,0:T(8,128)(2,1)}, bf16[256,512]{1,0:T(8,128)(2,1)S(1)}, u32[]{:S(2)}, u32[]{:S(2)}) collective-permute-start(bf16[256,512]{1,0:T(8,128)(2,1)} %get-tuple-element.29), channel_id=1, source_target_pairs={{0,1},{1,0},{2,3},{3,2},{4,5},{5,4},{6,7},{7,6},{8,9},{9,8},{10,11... | collective-permute-start | bytes 786440 | tf_op jit(solution)/shard_map/ppermute | solution.py:550
  8.6 4.1 %copy-start.3 = (bf16[4,256,512]{2,1,0:T(8,128)(2,1)S(1)}, bf16[4,256,512]{2,1,0:T(8,128)(2,1)}, u32[]{:S(2)}) copy-start(bf16[4,256,512]{2,1,0:T(8,128)(2,1)} %refs_5_.5) | copy-start | bytes 3145732
  8.7 4.1 %copy-start.9 = (f32[2,512]{1,0:T(2,128)S(1)}, f32[2,512]{1,0:T(2,128)}, u32[]{:S(2)}) copy-start(f32[2,512]{1,0:T(2,128)} %bias.3) | copy-start | bytes 12292
  8.8 31.1 %collective-permute-start.11 = (bf16[1024,512]{1,0:T(8,128)(2,1)S(1)}, bf16[1024,512]{1,0:T(8,128)(2,1)S(1)}, u32[]{:S(2)}, u32[]{:S(2)}) collective-permute-start(bf16[1024,512]{1,0:T(8,128)(2,1)S(1)} %pack.1), channel_id=1, source_target_pairs={{0,1},{1,0},{2,3},{3,2},{4,5},{5,4},{6,7},{7,6},{8,9},{9,8},{10,11... | collective-permute-start | bytes 3145736 | tf_op jit(solution)/shard_map/ppermute | solution.py:550
  10.4 10.9 %copy-start.2 = (bf16[2,1024,512]{2,1,0:T(8,128)(2,1)S(1)}, bf16[2,1024,512]{2,1,0:T(8,128)(2,1)}, u32[]{:S(2)}) copy-start(bf16[2,1024,512]{2,1,0:T(8,128)(2,1)} %refs_2_.9) | copy-start | bytes 6291460
  10.4 10.9 %copy-start.4 = (f32[2,1024]{1,0:T(2,128)S(1)}, f32[2,1024]{1,0:T(2,128)}, u32[]{:S(2)}) copy-start(f32[2,1024]{1,0:T(2,128)} %refs_1_.5) | copy-start | bytes 24580
  10.4 10.9 %copy-start.7 = (f32[2,512]{1,0:T(2,128)S(1)}, f32[2,512]{1,0:T(2,128)}, u32[]{:S(2)}) copy-start(f32[2,512]{1,0:T(2,128)} %refs_2_.8) | copy-start | bytes 12292
  10.4 10.9 %copy-start.8 = (f32[2,512]{1,0:T(2,128)S(1)}, f32[2,512]{1,0:T(2,128)}, u32[]{:S(2)}) copy-start(f32[2,512]{1,0:T(2,128)} %refs_3_.5) | copy-start | bytes 12292
  12.3 13.9 %collective-permute-start.4 = (bf16[528,256]{1,0:T(8,128)(2,1)S(1)}, bf16[528,256]{1,0:T(8,128)(2,1)S(1)}, u32[]{:S(2)}, u32[]{:S(2)}) collective-permute-start(bf16[528,256]{1,0:T(8,128)(2,1)S(1)} %collective-permute-done.2.refs_0_.refs_1_.refs_4_), channel_id=1, source_target_pairs={{0,8},{2,10},{4,12},{6,14},{8,0},{10,2},{12,4},{14,6},{16,24},{18,... | collective-permute-start | bytes 811016 | tf_op jit(solution)/shard_map/ppermute | solution.py:554
  17.9 8.8 %collective-permute-start.5 = (bf16[256,512]{1,0:T(8,128)(2,1)S(1)}, bf16[256,512]{1,0:T(8,128)(2,1)S(1)}, u32[]{:S(2)}, u32[]{:S(2)}) collective-permute-start(bf16[256,512]{1,0:T(8,128)(2,1)S(1)} %collective-permute-done.3.refs_1_), channel_id=1, source_target_pairs={{0,8},{2,10},{4,12},{6,14},{8,0},{10,2},{12,4},{14,6},{16,24},{18,... | collective-permute-start | bytes 786440 | tf_op jit(solution)/shard_map/ppermute | solution.py:554
  18.3 10.0 %collective-permute-start.6 = (bf16[528,256]{1,0:T(8,128)(2,1)S(1)}, bf16[528,256]{1,0:T(8,128)(2,1)S(1)}, u32[]{:S(2)}, u32[]{:S(2)}) collective-permute-start(bf16[528,256]{1,0:T(8,128)(2,1)S(1)} %collective-permute-done.2.refs_0_.refs_1_.refs_4_), channel_id=1, source_target_pairs={{0,2},{2,0},{4,6},{6,4},{8,10},{10,8},{12,14},{14,12},{16,18},{18,... | collective-permute-start | bytes 811016 | tf_op jit(solution)/shard_map/ppermute | solution.py:541
  26.1 2.2 %collective-permute-start.8 = (bf16[528,256]{1,0:T(8,128)(2,1)S(1)}, bf16[528,256]{1,0:T(8,128)(2,1)S(1)}, u32[]{:S(2)}, u32[]{:S(2)}) collective-permute-start(bf16[528,256]{1,0:T(8,128)(2,1)S(1)} %collective-permute-done.4.refs_2_.refs_5_), channel_id=1, source_target_pairs={{0,2},{2,0},{4,6},{6,4},{8,10},{10,8},{12,14},{14,12},{16,18},{18,... | collective-permute-start | bytes 811016 | tf_op jit(solution)/shard_map/ppermute | solution.py:541
  26.2 2.1 %collective-permute-start.7 = (bf16[256,512]{1,0:T(8,128)(2,1)S(1)}, bf16[256,512]{1,0:T(8,128)(2,1)S(1)}, u32[]{:S(2)}, u32[]{:S(2)}) collective-permute-start(bf16[256,512]{1,0:T(8,128)(2,1)S(1)} %collective-permute-done.3.refs_1_), channel_id=1, source_target_pairs={{0,2},{2,0},{4,6},{6,4},{8,10},{10,8},{12,14},{14,12},{16,18},{18,... | collective-permute-start | bytes 786440 | tf_op jit(solution)/shard_map/ppermute | solution.py:541
  26.7 1.8 %collective-permute-start.9 = (bf16[256,512]{1,0:T(8,128)(2,1)S(1)}, bf16[256,512]{1,0:T(8,128)(2,1)S(1)}, u32[]{:S(2)}, u32[]{:S(2)}) collective-permute-start(bf16[256,512]{1,0:T(8,128)(2,1)S(1)} %collective-permute-done.5.refs_3_), channel_id=1, source_target_pairs={{0,2},{2,0},{4,6},{6,4},{8,10},{10,8},{12,14},{14,12},{16,18},{18,... | collective-permute-start | bytes 786440 | tf_op jit(solution)/shard_map/ppermute | solution.py:541
  26.8 1.7 %copy-start.6 = (f32[2,512]{1,0:T(2,128)S(1)}, f32[2,512]{1,0:T(2,128)}, u32[]{:S(2)}) copy-start(f32[2,512]{1,0:T(2,128)} %refs_11_.1) | copy-start | bytes 12292
  30.5 3.0 %collective-permute-start.10 = (bf16[3,136,512]{2,1,0:T(8,128)(2,1)S(1)}, bf16[3,136,512]{2,1,0:T(8,128)(2,1)S(1)}, u32[]{:S(2)}, u32[]{:S(2)}) collective-permute-start(bf16[3,136,512]{2,1,0:T(8,128)(2,1)S(1)} %get-tuple-element.34), channel_id=1, source_target_pairs={{0,2},{2,0},{4,6},{6,4},{8,10},{10,8},{12,14},{14,12},{16,18},{18,... | collective-permute-start | bytes 1253384 | tf_op jit(solution)/shard_map/ppermute | solution.py:541
  30.9 10.8 %collective-permute-start.12 = (bf16[2,136,512]{2,1,0:T(8,128)(2,1)S(1)}, bf16[2,136,512]{2,1,0:T(8,128)(2,1)S(1)}, u32[]{:S(2)}, u32[]{:S(2)}) collective-permute-start(bf16[2,136,512]{2,1,0:T(8,128)(2,1)S(1)} %get-tuple-element.39), channel_id=1, source_target_pairs={{2,4},{6,8},{10,12},{14,16},{18,20},{22,24},{26,28},{4,2},{8,6},{1... | collective-permute-start | bytes 835592 | tf_op jit(solution)/shard_map/ppermute | solution.py:546
  39.9 3.0 %collective-permute-start.13 = (bf16[1024,512]{1,0:T(8,128)(2,1)S(1)}, bf16[1024,512]{1,0:T(8,128)(2,1)S(1)}, u32[]{:S(2)}, u32[]{:S(2)}) collective-permute-start(bf16[1024,512]{1,0:T(8,128)(2,1)S(1)} %collective-permute-done.11.refs_0_.refs_3_), channel_id=1, source_target_pairs={{0,2},{2,0},{4,6},{6,4},{8,10},{10,8},{12,14},{14,12},{16,18},{18,... | collective-permute-start | bytes 3145736 | tf_op jit(solution)/shard_map/ppermute | solution.py:541
  43.6 9.2 %collective-permute-start.14 = (bf16[2,128,512]{2,1,0:T(8,128)(2,1)S(1)}, bf16[2,128,512]{2,1,0:T(8,128)(2,1)S(1)}, u32[]{:S(2)}, u32[]{:S(2)}) collective-permute-start(bf16[2,128,512]{2,1,0:T(8,128)(2,1)S(1)} %more.4.refs_0_), channel_id=1, source_target_pairs={{0,1},{1,0},{2,3},{3,2},{4,5},{5,4},{6,7},{7,6},{8,9},{9,8},{10,11... | collective-permute-start | bytes 786440 | tf_op jit(solution)/shard_map/ppermute | solution.py:550
  46.4 11.5 %collective-permute-start.15 = (bf16[2,128,512]{2,1,0:T(8,128)(2,1)S(1)}, bf16[2,128,512]{2,1,0:T(8,128)(2,1)S(1)}, u32[]{:S(2)}, u32[]{:S(2)}) collective-permute-start(bf16[2,128,512]{2,1,0:T(8,128)(2,1)S(1)} %more.5.refs_1_), channel_id=1, source_target_pairs={{0,1},{1,0},{2,3},{3,2},{4,5},{5,4},{6,7},{7,6},{8,9},{9,8},{10,11... | collective-permute-start | bytes 786440 | tf_op jit(solution)/shard_map/ppermute | solution.py:550
  (3 other events, 5.0 us)
